TPU v7x, 32 devices: a whole 2x2x4 slice. The times are simulated.
32 devices in a mesh: dp: 4 (over y, x), row: 4 (over z), col: 2 (over core).
Axes of the slice: x: 2, y: 2, z: 4, core: 2. Of those that a mesh axis runs over, the one named last changes fastest.
Arguments:
- tokens_in: bfloat16 [16384, 1024], P(('dp', 'col'), 'row'), may hold values from -6 to 6
- prefix_len: int32 [16], P(('dp', 'row')), may hold values from 102 to 512
- first_gain: float32 [1024], P('row'), may hold values from 0.5 to 1.5
- first_shift: float32 [1024], P('row'), may hold values from -1.75 to 1.75
- second_gain: float32 [1024], P('row'), may hold values from 0.5 to 1.5
- second_shift: float32 [1024], P('row'), may hold values from -1.75 to 1.75
- qkv_weight: float32 [1024, 3072], P(('row', 'dp'), 'col'), may hold values from -0.1875 to 0.1875
- qkv_bias: float32 [3072], P(('col', 'dp')), may hold values from -1.75 to 1.75
- up_weight: float32 [1024, 4096], P(('row', 'dp'), 'col'), may hold values from -0.1875 to 0.1875
- up_bias: float32 [4096], P(('col', 'dp')), may hold values from -1.75 to 1.75
- dense_weight: float32 [1024, 1024], P(('col', 'dp'), 'row'), may hold values from -3 to 3
- dense_bias: float32 [1024], P(('row', 'dp')), may hold values from -1.75 to 1.75
- down_weight: float32 [4096, 1024], P(('col', 'dp'), 'row'), may hold values from -0.09375 to 0.09375
- down_bias: float32 [1024], P(('row', 'dp')), may hold values from -1.75 to 1.75
- cotangent: bfloat16 [16384, 1024], P(('dp', 'col'), 'row'), may hold values from -6 to 6
Outputs:
- layer_out: bfloat16 [16384, 1024], P(('dp', 'col'), 'row')
- grad_tokens: bfloat16 [16384, 1024], P(('dp', 'col'), 'row')
- grad_qkv_weight: float32 [1024, 3072], P(('row', 'dp'), 'col')
- grad_qkv_bias: float32 [3072], P(('col', 'dp'))
- grad_up_weight: float32 [1024, 4096], P(('row', 'dp'), 'col')
- grad_up_bias: float32 [4096], P(('col', 'dp'))
- grad_dense_weight: float32 [1024, 1024], P(('col', 'dp'), 'row')
- grad_dense_bias: float32 [1024], P(('row', 'dp'))
- grad_down_weight: float32 [4096, 1024], P(('col', 'dp'), 'row')
- grad_down_bias: float32 [1024], P(('row', 'dp'))
- grad_first_gain: float32 [1024], P('row')
- grad_first_shift: float32 [1024], P('row')
- grad_second_gain: float32 [1024], P('row')
- grad_second_shift: float32 [1024], P('row')
All inputs are finite; a program needn't handle non-finite values.
Results may differ from a plain program's by a relative error of at most 0.012.
The roundings to bfloat16 on the way count: a program that leaves them out, or rounds other values in their place, can miss the bound.
Values may be sent and summed in bfloat16 or wider, within the bound.
A program may use at most 320 MiB of HBM per device.

v0:
```python
from functools import partial
import math

import jax
import jax.numpy as jnp
from jax import lax
from jax.sharding import PartitionSpec as P

D = 1024
HD = 64
ROT = 16
SEQ_LEN = 1024
SEQ_GROUP = 1


EPS = 1e-05
NEGATIVE = -1e30


def angles_table():
    half_rot = ROT // 2
    places = jnp.arange(SEQ_LEN, dtype=jnp.float32)
    rates = jnp.exp(jnp.arange(half_rot, dtype=jnp.float32) * (-2.0 * math.log(10000.0) / ROT))
    turned = places[:, None] * rates[None, :]
    return (jnp.cos(turned), jnp.sin(turned))


def rotate(paired, cos_table, sin_table):
    half_rot = cos_table.shape[1]
    cos_wide = cos_table[None, :, None, None, :]
    sin_wide = sin_table[None, :, None, None, :]
    first_half = paired[..., :half_rot]
    second_half = paired[..., half_rot : 2 * half_rot]
    return jnp.concatenate(
        [
            first_half * cos_wide - second_half * sin_wide,
            second_half * cos_wide + first_half * sin_wide,
            paired[..., 2 * half_rot :],
        ],
        axis=-1,
    )


def score_block(queries, key_rows, prefix_end):
    scores = jnp.einsum(
        "qhd,khd->hqk", queries, key_rows, preferred_element_type=jnp.float32
    ) * HD ** (-0.5)
    places = jnp.arange(SEQ_LEN)
    visible = (places[None, :] <= places[:, None]) | (places[None, :] < prefix_end)
    return jnp.where(visible[None], scores, NEGATIVE)


def attend_forward(inputs):
    queries, key_rows, value_rows, prefix_end = inputs
    scores = score_block(queries, key_rows, prefix_end)
    highest = jnp.max(scores, axis=-1, keepdims=True)
    exp_total = jnp.sum(jnp.exp(scores - highest), axis=-1, keepdims=True)
    log_sum = highest + jnp.log(exp_total)
    weights = jnp.exp(scores - log_sum).astype(jnp.bfloat16)
    outputs = jnp.einsum("hqk,khd->qhd", weights, value_rows, preferred_element_type=jnp.float32)
    return (outputs, log_sum[..., 0])


def attend_backward(inputs):
    queries, key_rows, value_rows, prefix_end, log_sum, upstream = inputs
    scores = score_block(queries, key_rows, prefix_end)
    chances = jnp.exp(scores - log_sum[..., None])
    grad_values = jnp.einsum(
        "hqk,qhd->khd", chances.astype(jnp.bfloat16), upstream, preferred_element_type=jnp.float32
    )
    grad_chances = jnp.einsum(
        "qhd,khd->hqk", upstream, value_rows, preferred_element_type=jnp.float32
    )
    inner_sum = jnp.sum(chances * grad_chances, axis=-1, keepdims=True)
    grad_scores = (chances * (grad_chances - inner_sum)).astype(jnp.bfloat16)
    grad_queries = jnp.einsum(
        "hqk,khd->qhd", grad_scores, key_rows, preferred_element_type=jnp.float32
    ) * HD ** (-0.5)
    grad_keys = jnp.einsum(
        "hqk,qhd->khd", grad_scores, queries, preferred_element_type=jnp.float32
    ) * HD ** (-0.5)
    return (grad_queries, grad_keys, grad_values)


def norm_parts(gathered, center, scale_inv, first_gain, first_shift, second_gain, second_shift):
    normed = (gathered.astype(jnp.float32) - center[:, None]) * scale_inv[:, None]
    first_in = (normed * first_gain + first_shift).astype(jnp.bfloat16)
    second_in = (normed * second_gain + second_shift).astype(jnp.bfloat16)
    return (normed, first_in, second_in)


def contract_rows(left_side, right_side):
    return lax.dot_general(
        left_side, right_side, (((0,), (0,)), ((), ())), preferred_element_type=jnp.float32
    )


def contract_cols(left_side, right_side):
    return lax.dot_general(
        left_side, right_side, (((1,), (1,)), ((), ())), preferred_element_type=jnp.float32
    )


def shards(
    tokens_in,
    prefix_len,
    first_gain,
    first_shift,
    second_gain,
    second_shift,
    qkv_weight,
    qkv_bias,
    up_weight,
    up_bias,
    dense_weight,
    dense_bias,
    down_weight,
    down_bias,
    cotangent,
):
    tok_col = tokens_in.shape[0]
    col_count = lax.axis_size("col")
    row_count = lax.axis_size("row")
    group_rows = tok_col * col_count
    seq_rows = group_rows // row_count
    qkv_w, up_w, dense_w, down_w, qkv_b, up_b, dense_b, down_b = (
        lax.all_gather(qkv_weight.astype(jnp.bfloat16), "dp", axis=0, tiled=True),
        lax.all_gather(up_weight.astype(jnp.bfloat16), "dp", axis=0, tiled=True),
        lax.all_gather(dense_weight.astype(jnp.bfloat16), "dp", axis=0, tiled=True),
        lax.all_gather(down_weight.astype(jnp.bfloat16), "dp", axis=0, tiled=True),
        lax.all_gather(qkv_bias.astype(jnp.bfloat16), "dp", axis=0, tiled=True),
        lax.all_gather(up_bias.astype(jnp.bfloat16), "dp", axis=0, tiled=True),
        lax.all_gather(dense_bias.astype(jnp.bfloat16), "dp", axis=0, tiled=True),
        lax.all_gather(down_bias.astype(jnp.bfloat16), "dp", axis=0, tiled=True),
    )
    width_qkv = qkv_w.shape[1]
    heads_here = width_qkv // (3 * HD)
    width_att = heads_here * HD
    out_weight = jnp.concatenate([dense_w, down_w], axis=0)
    gathered, cot_all = (
        lax.all_gather(tokens_in, "col", axis=0, tiled=True),
        lax.all_gather(cotangent, "col", axis=0, tiled=True),
    )
    gathered_wide = gathered.astype(jnp.float32)
    line_sum, square_sum = lax.psum(
        (jnp.sum(gathered_wide, axis=1), jnp.sum(gathered_wide * gathered_wide, axis=1)), "row"
    )
    center = line_sum / D
    scale_inv = lax.rsqrt(square_sum / D - center * center + EPS)
    normed, first_in, second_in = norm_parts(
        gathered, center, scale_inv, first_gain, first_shift, second_gain, second_shift
    )
    own_first, own_second, own_cot = (
        lax.all_to_all(first_in, "row", split_axis=0, concat_axis=1, tiled=True),
        lax.all_to_all(second_in, "row", split_axis=0, concat_axis=1, tiled=True),
        lax.all_to_all(cot_all, "row", split_axis=0, concat_axis=1, tiled=True),
    )
    qkv_full, up_full, out_full = (
        lax.all_gather(qkv_w, "row", axis=0, tiled=True),
        lax.all_gather(up_w, "row", axis=0, tiled=True),
        lax.all_gather(out_weight, "row", axis=1, tiled=True),
    )
    summed = jnp.concatenate(
        [
            jnp.dot(own_first, qkv_full, preferred_element_type=jnp.float32),
            jnp.dot(own_second, up_full, preferred_element_type=jnp.float32),
        ],
        axis=1,
    )
    mixed = summed[:, :width_qkv] + qkv_b.astype(jnp.float32)
    hidden_pre = summed[:, width_qkv:] + up_b.astype(jnp.float32)
    mixed_heads = mixed.reshape(SEQ_GROUP, SEQ_LEN, heads_here, 3, HD)
    cos_table, sin_table = angles_table()
    turned = rotate(mixed_heads[:, :, :, :2, :], cos_table, sin_table).astype(jnp.bfloat16)
    queries = turned[:, :, :, 0, :]
    key_rows = turned[:, :, :, 1, :]
    value_rows = mixed_heads[:, :, :, 2, :].astype(jnp.bfloat16)
    outputs, log_sums = lax.map(attend_forward, (queries, key_rows, value_rows, prefix_len))
    attended = outputs.reshape(seq_rows, width_att).astype(jnp.bfloat16)
    hidden = jax.nn.gelu(hidden_pre, approximate=False).astype(jnp.bfloat16)
    joined = jnp.concatenate([attended, hidden], axis=1)
    joined_all = lax.all_gather(joined, "row", axis=0, tiled=True)
    branch_sum = lax.psum_scatter(
        jnp.dot(joined_all, out_weight, preferred_element_type=jnp.float32),
        "col",
        scatter_dimension=0,
        tiled=True,
    )
    layer_out = (
        tokens_in.astype(jnp.float32)
        + branch_sum
        + dense_b.astype(jnp.float32)
        + down_b.astype(jnp.float32)
    ).astype(jnp.bfloat16)
    grad_joined = contract_cols(own_cot, out_full)
    grad_out_weight = contract_rows(joined_all, cot_all)
    grad_out_bias = jnp.sum(cot_all, axis=0, dtype=jnp.float32)
    upstream = (
        grad_joined[:, :width_att].astype(jnp.bfloat16).reshape(SEQ_GROUP, SEQ_LEN, heads_here, HD)
    )
    ignored_value, gelu_back = jax.vjp(partial(jax.nn.gelu, approximate=False), hidden_pre)
    grad_hidden_pre = gelu_back(grad_joined[:, width_att:])[0].astype(jnp.bfloat16)
    grad_queries, grad_keys, grad_values = lax.map(
        attend_backward, (queries, key_rows, value_rows, prefix_len, log_sums, upstream)
    )
    ignored_pair, rotate_back = jax.vjp(
        lambda paired: rotate(paired, cos_table, sin_table), mixed_heads[:, :, :, :2, :]
    )
    grad_pair = rotate_back(jnp.stack([grad_queries, grad_keys], axis=3))[0]
    grad_mixed = jnp.concatenate([grad_pair, grad_values[:, :, :, None, :]], axis=3)
    grad_mixed = grad_mixed.reshape(seq_rows, width_qkv).astype(jnp.bfloat16)
    grad_inputs = jnp.concatenate([grad_mixed, grad_hidden_pre], axis=1)
    grad_all = lax.all_gather(grad_inputs, "row", axis=0, tiled=True)
    grad_qkv_full = grad_all[:, :width_qkv]
    grad_up_full = grad_all[:, width_qkv:]
    grad_qkv_w = contract_rows(first_in, grad_qkv_full)
    grad_up_w = contract_rows(second_in, grad_up_full)
    grad_qkv_b = jnp.sum(grad_qkv_full, axis=0, dtype=jnp.float32)
    grad_up_b = jnp.sum(grad_up_full, axis=0, dtype=jnp.float32)
    grad_first = contract_cols(grad_qkv_full, qkv_w)
    grad_second = contract_cols(grad_up_full, up_w)
    gain_terms = (
        jnp.sum(normed * grad_first, axis=0),
        jnp.sum(grad_first, axis=0),
        jnp.sum(normed * grad_second, axis=0),
        jnp.sum(grad_second, axis=0),
    )
    combined_part = grad_first * first_gain + grad_second * second_gain
    combined = lax.psum_scatter(combined_part, "col", scatter_dimension=0, tiled=True)
    gain_sums = lax.psum(
        (gain_terms[0], gain_terms[1], gain_terms[2], gain_terms[3]), ("dp", "col")
    )
    offset_rows = lax.axis_index("col") * tok_col
    own_normed = lax.dynamic_slice_in_dim(normed, offset_rows, tok_col, 0)
    own_scale = lax.dynamic_slice_in_dim(scale_inv, offset_rows, tok_col, 0)
    line_total, cross_total = lax.psum(
        (jnp.sum(combined, axis=1), jnp.sum(combined * own_normed, axis=1)), "row"
    )
    grad_tokens = (
        cotangent.astype(jnp.float32)
        + own_scale[:, None]
        * (combined - line_total[:, None] / D - own_normed * cross_total[:, None] / D)
    ).astype(jnp.bfloat16)
    reduced = (
        lax.psum_scatter(
            grad_qkv_w.astype(jnp.bfloat16), "dp", scatter_dimension=0, tiled=True
        ).astype(jnp.float32),
        lax.psum_scatter(
            grad_up_w.astype(jnp.bfloat16), "dp", scatter_dimension=0, tiled=True
        ).astype(jnp.float32),
        lax.psum_scatter(
            grad_out_weight[:width_att].astype(jnp.bfloat16), "dp", scatter_dimension=0, tiled=True
        ).astype(jnp.float32),
        lax.psum_scatter(
            grad_out_weight[width_att:].astype(jnp.bfloat16), "dp", scatter_dimension=0, tiled=True
        ).astype(jnp.float32),
        lax.psum_scatter(
            grad_qkv_b.astype(jnp.bfloat16), "dp", scatter_dimension=0, tiled=True
        ).astype(jnp.float32),
        lax.psum_scatter(
            grad_up_b.astype(jnp.bfloat16), "dp", scatter_dimension=0, tiled=True
        ).astype(jnp.float32),
        lax.psum_scatter(
            grad_out_bias.astype(jnp.bfloat16), "dp", scatter_dimension=0, tiled=True
        ).astype(jnp.float32),
    )
    return (
        layer_out,
        grad_tokens,
        reduced[0],
        reduced[4],
        reduced[1],
        reduced[5],
        reduced[2],
        reduced[6],
        reduced[3],
        reduced[6],
        gain_sums[0],
        gain_sums[1],
        gain_sums[2],
        gain_sums[3],
    )


def solution(mesh):
    in_specs = (
        P(("dp", "col"), "row"),
        P(("dp", "row")),
        P("row"),
        P("row"),
        P("row"),
        P("row"),
        P(("row", "dp"), "col"),
        P(("col", "dp")),
        P(("row", "dp"), "col"),
        P(("col", "dp")),
        P(("col", "dp"), "row"),
        P(("row", "dp")),
        P(("col", "dp"), "row"),
        P(("row", "dp")),
        P(("dp", "col"), "row"),
    )
    out_specs = (
        P(("dp", "col"), "row"),
        P(("dp", "col"), "row"),
        P(("row", "dp"), "col"),
        P(("col", "dp")),
        P(("row", "dp"), "col"),
        P(("col", "dp")),
        P(("col", "dp"), "row"),
        P(("row", "dp")),
        P(("col", "dp"), "row"),
        P(("row", "dp")),
        P("row"),
        P("row"),
        P("row"),
        P("row"),
    )
    return jax.shard_map(shards, mesh=mesh, in_specs=in_specs, out_specs=out_specs, check_vma=False)
```

profile of v0, /device:TPU:0, one launch (start us, length us, event | category | flops | bytes accessed | tf_op | source)
XLA Modules:
  0.0 1500.4 jit_solution(10189567568798957667)
XLA Ops:
  7.2 1.8 convert_element_type.156
  10.6 1.8 convert_element_type.151
  13.4 17.0 %all_gather.46 = bf16[256,1536]{1,0:T(8,128)(2,1)} all-gather(bf16[64,1536]{1,0:T(8,128)(2,1)S(1)} %convert_element_type.142), channel_id=1, replica_groups=mesh['dp'=4,'row'=4,'col'=2] {'dp'}, dimensions={0}, use_global_device_ids=true | all-gather | bytes 983040 | tf_op jit(solution)/shard_map/all_gather | solution.py:127
  31.4 9.9 all_gather.53
  41.4 2.7 all-gather.22.cloned.1.call-done
  46.5 9.7 all-gather.26.cloned.1.call-done
  56.2 4.9 all-to-all-start.2
  61.0 8.5 all-gather.12.cloned.1.call-done
  69.5 2.7 convert_reduce_fusion
  72.3 48.0 %all-reduce.10 = (f32[4096]{0:T(1024)S(1)}, f32[4096]{0:T(1024)S(1)}) all-reduce(f32[4096]{0:T(1024)S(1)} %get-tuple-element.72, f32[4096]{0:T(1024)S(1)} %get-tuple-element.71), channel_id=1, replica_groups=mesh['dp'=4,'row'=4,'col'=2] {'row'}, use_global_device_ids=true, to_apply=%region_3.0 | all-reduce | flops 8192 | bytes 65536 | tf_op jit(solution)/shard_map/psum | solution.py:145
  120.9 5.3 add_convert_fusion.3
  126.3 4.0 copy.71
  130.3 4.5 all-to-all-start
  135.5 8.4 all-gather
  144.0 8.0 all-gather.1
  152.6 4.0 copy.77
  156.6 2.4 copy.79
  159.0 50.1 %all-to-all-done = bf16[4,1024,256]{1,2,0:T(8,128)(2,1)} async-done(((bf16[4,1024,256]{1,2,0:T(8,128)(2,1)}), bf16[4,1024,256]{1,2,0:T(8,128)(2,1)}, u32[]{:S(2)}, u32[]{:S(2)}) %all-to-all-start) | async-done | bytes 2097184 | tf_op jit(solution)/shard_map/all_to_all | solution.py:154
  209.2 4.5 all-to-all-start.1
  213.7 8.8 convolution_add_fusion
  222.5 7.0 copy.72
  229.5 3.3 copy.93
  232.9 2.1 subtract_convert_fusion
  235.3 13.6 fusion
  248.9 14.2 exponential_reduce_fusion
  263.2 15.0 convolution_convert_fusion.2
  278.7 66.6 %all-gather.24.cloned.1.call-done = bf16[2560,1024]{1,0:T(8,128)(2,1)} async-done(((bf16[2560,256]{1,0:T(8,128)(2,1)}), bf16[2560,1024]{1,0:T(8,128)(2,1)}) %all-gather.24.cloned.1.call-update) | async-done | bytes 5242896 | tf_op jit(solution)/shard_map/all_gather | solution.py:161
  345.3 11.2 convolution_bitcast_fusion
  356.5 71.4 %all-gather.18.cloned.1.call-done = bf16[1024,2048]{1,0:T(8,128)(2,1)} async-done(((bf16[256,2048]{1,0:T(8,128)(2,1)}), bf16[1024,2048]{1,0:T(8,128)(2,1)}) %all-gather.18.cloned.1.call-update) | async-done | bytes 4194320 | tf_op jit(solution)/shard_map/all_gather | solution.py:160
  427.8 28.7 %add_convert_fusion = (bf16[1024,2048]{1,0:T(8,128)(2,1)}, f32[1024,2048]{1,0:T(8,128)}, f32[1024,2048]{1,0:T(8,128)}) fusion(f32[1024,2560]{1,0:T(8,128)} %convolution_bitcast_fusion, f32[2048]{0:T(1024)S(1)} %bitcast.83, bf16[1024,1024]{0,1:T(8,128)(2,1)} %bitcast.12, bf16[1024,2048]{1,0:T(8,128)(2,1)} %all-gather.18.cloned.1.call-done), kind=kOutput, calls=%fused_computation.19 | convolution fusion | flops 4448059392 | bytes 35659776 | tf_op jit(solution)/shard_map/dot_general | solution.py:166
  456.5 10.1 multiply_convert_fusion.1
  466.6 4.9 pad_maximum_fusion.1
  471.6 1.7 slice.98
  474.1 26.4 %multiply_reduce_fusion = (f32[8,1024]{1,0:T(8,128)S(1)}, f32[8,1024,1024]{1,2,0:T(8,128)}) fusion(f32[8,1024,1024]{1,2,0:T(8,128)} %get-tuple-element.106, f32[8,1024]{1,0:T(8,128)S(1)} %log_add_fusion, pred[1024,1024]{0,1:T(8,128)(4,1)S(1)} %fusion.18, bf16[1024,8,64]{0,2,1:T(8,128)(2,1)S(1)} %bitcast.79, bf16[1,1024,8,3,64]{1,4,2,3,0:T(8,128)(2,1)} %copy-done.1), kind=kOutput, calls=%fused_computation.1 | convolution fusion | flops 1115676672 | bytes 70320128 | tf_op jit(solution)/shard_map/while/body/eval_jaxpr/qhd,khd->hqk/dot_general | solution.py:71
  500.5 28.7 %multiply_convert_fusion = bf16[8,1024,1024]{1,2,0:T(8,128)(2,1)} fusion(f32[8,1024,1024]{1,2,0:T(8,128)} %get-tuple-element.108, f32[8,1024,1024]{1,2,0:T(8,128)} %get-tuple-element.106, f32[8,1024]{1,0:T(8,128)S(1)} %get-tuple-element.107, f32[8,1024]{1,0:T(8,128)S(1)} %log_add_fusion, pred[1024,1024]{0,1:T(8,128)(4,1)S(1)} %fusion.18), kind=kLoop, calls=%fused_computation | loop fusion | flops 50331648 | bytes 85000192 | tf_op jit(solution)/shard_map/while/body/eval_jaxpr/convert_element_type | solution.py:75
  529.2 11.4 multiply_bitcast_fusion
  540.6 9.1 multiply_bitcast_fusion.1
  550.6 16.5 %fusion.26 = bf16[1,1024,8,1,64]{1,4,2,3,0:T(8,128)(2,1)} fusion(bf16[1024,8,64]{0,2,1:T(8,128)(2,1)} %bitcast.80, f32[8,1024,1024]{1,2,0:T(8,128)} %get-tuple-element.106, f32[8,1024]{1,0:T(8,128)S(1)} %log_add_fusion, pred[1024,1024]{0,1:T(8,128)(4,1)S(1)} %fusion.18), kind=kOutput, calls=%fused_computation.69 | convolution fusion | flops 1107820544 | bytes 36732928 | tf_op jit(solution)/shard_map/while/body/eval_jaxpr/hqk,qhd->khd/dot_general | solution.py:68
  568.6 2.1 copy.85
  570.7 3.2 copy.86
  573.9 5.6 pad_maximum_fusion
  579.6 247.4 %all-gather.20.cloned.1.call-done = bf16[4096,2560]{1,0:T(8,128)(2,1)} async-done(((bf16[1024,2560]{1,0:T(8,128)(2,1)}), bf16[4096,2560]{1,0:T(8,128)(2,1)}) %all-gather.20.cloned.1.call-update) | async-done | bytes 20971536 | tf_op jit(solution)/shard_map/all_gather | solution.py:182
  827.0 11.2 convolution_convert_fusion
  840.2 14.3 fusion.39
  854.8 465.6 %all-gather.28.cloned.1.call-done = bf16[4096,3584]{1,0:T(8,128)(2,1)} async-done(((bf16[1024,3584]{1,0:T(8,128)(2,1)}), bf16[4096,3584]{1,0:T(8,128)(2,1)}) %all-gather.28.cloned.1.call-update) | async-done | bytes 29360144 | tf_op jit(solution)/shard_map/all_gather | solution.py:213
  1320.4 9.5 fusion.23
  1330.0 9.4 fusion.20
  1339.5 6.8 fusion.8
  1346.4 11.8 fusion.34
  1364.1 13.2 reduce-scatter.17.cloned.1.call-done
  1377.3 1.8 convert_element_type.175
  1379.1 6.3 slice_reduce_fusion.1
  1385.4 8.5 slice_reduce_fusion
  1394.0 9.9 all-reduce.11
  1404.0 12.5 all-reduce.8
  1417.7 2.9 add_convert_fusion.5
  1420.6 1.5 reduce-scatter.11.cloned.1.call-done
  1422.1 1.7 convert_element_type.168
  1423.8 29.6 %reduce-scatter.13.cloned.1.call-done = bf16[64,2048]{1,0:T(8,128)(2,1)} async-done(((bf16[256,2048]{1,0:T(8,128)(2,1)}), bf16[64,2048]{1,0:T(8,128)(2,1)}) %reduce-scatter.13.cloned.1.call-update) | async-done | bytes 262160 | tf_op jit(solution)/shard_map/reduce_scatter | solution.py:248
  1453.5 1.8 convert_element_type.171
  1455.3 12.4 reduce-scatter.9.cloned.1.call-done
  1467.7 2.8 fusion.36
  1470.5 19.1 %all-reduce.9 = (f32[2048]{0:T(1024)S(1)}, f32[2048]{0:T(1024)S(1)}) all-reduce(f32[2048]{0:T(1024)S(1)} %get-tuple-element.70, f32[2048]{0:T(1024)S(1)} %get-tuple-element.69), channel_id=1, replica_groups=mesh['dp'=4,'row'=4,'col'=2] {'row'}, use_global_device_ids=true, to_apply=%region_12.13 | all-reduce | flops 4096 | bytes 32768 | tf_op jit(solution)/shard_map/psum | solution.py:236
  1489.7 3.5 add_convert_fusion.4
  (145 shorter events, 18.9 us)
Async XLA Ops:
  7.2 36.9 %all-gather.22.cloned.1.call-start = ((), (), s32[]{:S(2)}) async-start(), calls=%async_computation.14 | async-start | bytes 1310720 | tf_op jit(solution)/shard_map/all_gather | solution.py:130
  9.0 111.9 %copy-start.23 = (f32[256]{0:T(256)S(1)}, f32[256]{0:T(256)}, u32[]{:S(2)}) copy-start(f32[256]{0:T(256)} %param.18) | copy-start | bytes 3076
  9.0 111.9 %copy-start.24 = (f32[256]{0:T(256)S(1)}, f32[256]{0:T(256)}, u32[]{:S(2)}) copy-start(f32[256]{0:T(256)} %param.20) | copy-start | bytes 3076
  9.0 111.9 %copy-start.25 = (f32[256]{0:T(256)S(1)}, f32[256]{0:T(256)}, u32[]{:S(2)}) copy-start(f32[256]{0:T(256)} %param.17) | copy-start | bytes 3076
  9.0 111.9 %copy-start.27 = (f32[256]{0:T(256)S(1)}, f32[256]{0:T(256)}, u32[]{:S(2)}) copy-start(f32[256]{0:T(256)} %param.19) | copy-start | bytes 3076
  9.0 47.2 %all-gather.26.cloned.1.call-start = ((), (), s32[]{:S(2)}) async-start(), calls=%async_computation.17 | async-start | bytes 3145728 | tf_op jit(solution)/shard_map/all_gather | solution.py:142
  9.8 59.7 %all-gather.12.cloned.1.call-start = ((), (), s32[]{:S(2)}) async-start(), calls=%async_computation.9 | async-start | bytes 3145728 | tf_op jit(solution)/shard_map/all_gather | solution.py:141
  10.5 142.1 %all-gather.16.cloned.1.call-start = ((), (), s32[]{:S(2)}) async-start(), calls=%async_computation.11 | async-start | bytes 1310720 | tf_op jit(solution)/shard_map/all_gather | solution.py:128
  12.4 201.4 %all-gather.14.cloned.1.call-start = ((), (), s32[]{:S(2)}) async-start(), calls=%async_computation.10 | async-start | bytes 3932160 | tf_op jit(solution)/shard_map/all_gather | solution.py:159
  30.5 314.8 %all-gather.24.cloned.1.call-start = ((), (), s32[]{:S(2)}) async-start(), calls=%async_computation.16 | async-start | bytes 6553600 | tf_op jit(solution)/shard_map/all_gather | solution.py:161
  45.3 1.1 copy-start.9
  56.2 74.1 %all-to-all-start.2 = ((bf16[4,1024,256]{2,1,0:T(8,128)(2,1)}), bf16[4,1024,256]{2,1,0:T(8,128)(2,1)S(1)}, u32[]{:S(2)}, u32[]{:S(2)}) async-start(bf16[4,1024,256]{2,1,0:T(8,128)(2,1)} %bitcast.75), calls=%async_computation.3 | async-start | bytes 4194304 | tf_op jit(solution)/shard_map/all_to_all | solution.py:156
  61.0 74.4 %copy-start.21 = (f32[384]{0:T(512)S(1)}, f32[384]{0:T(512)}, u32[]{:S(2)}) copy-start(f32[384]{0:T(512)} %param.22) | copy-start | bytes 4612
  61.0 74.4 %copy-start.22 = (f32[512]{0:T(512)S(1)}, f32[512]{0:T(512)}, u32[]{:S(2)}) copy-start(f32[512]{0:T(512)} %param.24) | copy-start | bytes 6148
  120.3 0.6 copy-start.16
  120.3 6.0 copy-start.18
  130.3 78.9 %all-to-all-start = ((bf16[4,1024,256]{1,2,0:T(8,128)(2,1)}), bf16[4,1024,256]{1,2,0:T(8,128)(2,1)}, u32[]{:S(2)}, u32[]{:S(2)}) async-start(bf16[4,1024,256]{1,2,0:T(8,128)(2,1)} %copy.71), calls=%async_computation | async-start | bytes 4194304 | tf_op jit(solution)/shard_map/all_to_all | solution.py:154
  134.8 293.1 %all-gather.18.cloned.1.call-start = ((), (), s32[]{:S(2)}) async-start(), calls=%async_computation.12 | async-start | bytes 5242880 | tf_op jit(solution)/shard_map/all_gather | solution.py:160
  152.2 80.7 %copy-start.12 = (f32[1024,8]{0,1:T(8,128)}, f32[1024,8]{0,1:T(8,128)S(1)}, u32[]{:S(2)}) copy-start(f32[1024,8]{0,1:T(8,128)S(1)} %get-tuple-element.102) | copy-start | bytes 98308
  152.2 80.7 %copy-start.14 = (f32[1024,8]{0,1:T(8,128)}, f32[1024,8]{0,1:T(8,128)S(1)}, u32[]{:S(2)}) copy-start(f32[1024,8]{0,1:T(8,128)S(1)} %get-tuple-element.103) | copy-start | bytes 98308
  209.2 147.3 %all-to-all-start.1 = ((bf16[4,1024,256]{1,2,0:T(8,128)(2,1)}), bf16[4,1024,256]{1,2,0:T(8,128)(2,1)}, u32[]{:S(2)}, u32[]{:S(2)}) async-start(bf16[4,1024,256]{1,2,0:T(8,128)(2,1)} %copy.77), calls=%async_computation.1 | async-start | bytes 4194304 | tf_op jit(solution)/shard_map/all_to_all | solution.py:155
  213.7 613.4 %all-gather.20.cloned.1.call-start = ((), (), s32[]{:S(2)}) async-start(), calls=%async_computation.13 | async-start | bytes 26214400 | tf_op jit(solution)/shard_map/all_gather | solution.py:182
  232.8 30.4 %copy-start.1 = (bf16[1,1024,8,3,64]{1,4,2,3,0:T(8,128)(2,1)}, bf16[1,1024,8,3,64]{1,4,2,3,0:T(8,128)(2,1)S(1)}, u32[]{:S(2)}) copy-start(bf16[1,1024,8,3,64]{1,4,2,3,0:T(8,128)(2,1)S(1)} %copy.93) | copy-start | bytes 9437188
  235.3 13.6 copy-start
  471.5 848.9 %all-gather.28.cloned.1.call-start = ((), (), s32[]{:S(2)}) async-start(), calls=%async_computation.18 | async-start | bytes 36700160 | tf_op jit(solution)/shard_map/all_gather | solution.py:213
  474.0 26.4 %copy-start.5 = (bf16[1024,512]{0,1:T(8,128)(2,1)}, bf16[1024,512]{0,1:T(8,128)(2,1)S(1)}, u32[]{:S(2)}) copy-start(bf16[1024,512]{0,1:T(8,128)(2,1)S(1)} %copy.81) | copy-start | bytes 3145732
  540.6 9.5 copy-start.13
  540.6 9.5 copy-start.15
  579.5 260.6 %copy-start.10 = (bf16[2560,256]{1,0:T(8,128)(2,1)S(1)}, bf16[2560,256]{1,0:T(8,128)(2,1)}, u32[]{:S(2)}) copy-start(bf16[2560,256]{1,0:T(8,128)(2,1)} %copy-done.9) | copy-start | bytes 3932164
  579.5 783.0 %reduce-scatter.15.cloned.1.call-start = ((), (), s32[]{:S(2)}) async-start(), calls=%async_computation.22 | async-start | bytes 327680 | tf_op jit(solution)/shard_map/reduce_scatter | solution.py:251
  839.0 538.3 %reduce-scatter.17.cloned.1.call-start = ((), (), s32[]{:S(2)}) async-start(), calls=%async_computation.23 | async-start | bytes 1310720 | tf_op jit(solution)/shard_map/reduce_scatter | solution.py:254
  840.1 577.6 %reduce-scatter.7.cloned.1.call-start = ((), (), s32[]{:S(2)}) async-start(), calls=%async_computation.15 | async-start | bytes 6291456 | tf_op jit(solution)/shard_map/reduce_scatter | solution.py:183
  854.5 475.4 %copy-start.4 = (bf16[4096,256]{1,0:T(8,128)(2,1)S(1)}, bf16[4096,256]{1,0:T(8,128)(2,1)}, u32[]{:S(2)}) copy-start(bf16[4096,256]{1,0:T(8,128)(2,1)} %get-tuple-element.97) | copy-start | bytes 6291460
  854.5 567.6 %reduce-scatter.11.cloned.1.call-start = ((), (), s32[]{:S(2)}) async-start(), calls=%async_computation.20 | async-start | bytes 983040 | tf_op jit(solution)/shard_map/reduce_scatter | solution.py:245
  1329.9 9.6 copy-start.8
  1329.9 123.6 %reduce-scatter.13.cloned.1.call-start = ((), (), s32[]{:S(2)}) async-start(), calls=%async_computation.21 | async-start | bytes 1310720 | tf_op jit(solution)/shard_map/reduce_scatter | solution.py:248
  1339.4 6.9 copy-start.17
  1339.4 6.9 copy-start.19
  1339.4 6.9 copy-start.26
  1339.4 6.9 copy-start.28
  1339.4 128.3 %reduce-scatter.9.cloned.1.call-start = ((), (), s32[]{:S(2)}) async-start(), calls=%async_computation.19 | async-start | bytes 6291456 | tf_op jit(solution)/shard_map/reduce_scatter | solution.py:229
  1339.5 6.8 copy-start.3
  1339.5 6.8 copy-start.11
  1346.4 11.9 copy-start.20
  1346.4 14.5 copy-start.29
  1346.4 14.5 copy-start.30
  1346.4 15.6 %copy-start.2 = (bf16[4096,256]{1,0:T(8,128)(2,1)S(1)}, bf16[4096,256]{1,0:T(8,128)(2,1)}, u32[]{:S(2)}) copy-start(bf16[4096,256]{1,0:T(8,128)(2,1)} %all-gather.26.cloned.1.call-done) | copy-start | bytes 6291460
  1385.4 32.3 %copy-start.7 = (bf16[2048,256]{1,0:T(8,128)(2,1)S(1)}, bf16[2048,256]{1,0:T(8,128)(2,1)}, u32[]{:S(2)}) copy-start(bf16[2048,256]{1,0:T(8,128)(2,1)} %param.15) | copy-start | bytes 3145732
  1393.9 95.7 %copy-start.6 = (bf16[2048,256]{1,0:T(8,128)(2,1)S(1)}, bf16[2048,256]{1,0:T(8,128)(2,1)}, u32[]{:S(2)}) copy-start(bf16[2048,256]{1,0:T(8,128)(2,1)} %param.29) | copy-start | bytes 3145732
  1404.0 89.7 %copy-start.31 = (f32[64]{0:T(128)}, f32[64]{0:T(128)S(1)}, u32[]{:S(2)}) copy-start(f32[64]{0:T(128)S(1)} %dynamic-slice_convert_fusion.2) | copy-start | bytes 772
Sparse Core Ops, SparseCore 0:
  10.4 33.5 all-gather.21
  45.6 10.5 all-gather.25
  57.7 11.7 all-gather.11
  71.8 27.7 all-gather.15
  101.0 101.5 all-gather.13
  204.0 141.2 all-gather.23
  346.8 80.9 all-gather.17
  471.6 355.3 all-gather.19
  828.6 491.6 all-gather.27
  1323.5 22.2 reduce-scatter.14
  1349.6 27.7 reduce-scatter.16
  1379.5 12.0 reduce-scatter.6
  1394.7 27.3 reduce-scatter.10
  1425.7 27.7 reduce-scatter.12
  1455.6 12.0 reduce-scatter.8
where the time goes:
time: 1510 us; the launch traced here: 1500 us
  waiting for transfers between devices  980 us (65%)
  matrix products  204 us (14%)
  blocking collectives  133 us (9%)
  other arithmetic  115 us (8%)
  local copies, waits for them, and re-layouts  35.6 us (2%)
  between operations  18.1 us (1%)
    all_gather x1, waiting for transfers between devices, shards(): grad_all = lax.all_gather(grad_inputs, 'row', axis=0, tiled=True)  466 us
    all_gather x1, waiting for transfers between devices, shards(): joined_all = lax.all_gather(joined, 'row', axis=0, tiled=True)  247 us
    all_gather x1, waiting for transfers between devices, shards(): lax.all_gather(up_w, 'row', axis=0, tiled=True)  71.4 us
    all_gather x1, waiting for transfers between devices, shards(): lax.all_gather(out_weight, 'row', axis=1, tiled=True)  66.6 us
    all_to_all x1, waiting for transfers between devices, shards(): lax.all_to_all(first_in, 'row', split_axis=0, concat_axis=1, tiled=True)  50.1 us
    psum x1, blocking collectives, shards(): lax.psum((jnp.sum(gathered_wide, axis=1), jnp.sum(gathered_wide * gathere...  48 us
  transfers between devices with their start and end apart: 18, of which 12 were waited for; matrix products, arithmetic and copies ran while one was open for 20% of the time, Pallas kernels for 0%

commit v1 on v0

v1 whole, which is shorter than its diff:
```python
import functools
import math

import jax
import jax.numpy as jnp
from jax import lax
from jax.experimental import pallas as pl
from jax.experimental.pallas import tpu as pltpu
from jax.sharding import PartitionSpec as P

D = 1024
HD = 64
ROT = 16
FF = 4096
SEQ_LEN = 1024
EPS = 1e-05
NEGATIVE = -1e30
ROWS = 4
DPS = 4
MESH = pl.DeviceIdType.MESH
BF = jnp.bfloat16
F32 = jnp.float32


def places():
    dp, row, col = lax.axis_index("dp"), lax.axis_index("row"), lax.axis_index("col")
    across = dp + 1 - 2 * lax.rem(dp, 2)
    along = lax.rem(dp + 2, 4)
    return dp, row, col, across, along


def line_order(row):
    far = row // 2
    side = row - 3 * far + 2 * far * (3 - row)
    side = lax.rem(jnp.abs(side), 2)
    at = lambda place: far * 3 + (1 - 2 * far) * place
    return side, at


def greet(targets):
    barrier = pltpu.get_barrier_semaphore()
    for target in targets:
        pl.semaphore_signal(barrier, inc=1, device_id=target, device_id_type=MESH)
    pl.semaphore_wait(barrier, len(targets))


def peers_of(dp, row, col, cols):
    group = []
    for step in range(1, ROWS * cols):
        flat = lax.rem(row * cols + col + step, ROWS * cols)
        group.append((dp, flat // cols, lax.rem(flat, cols)))
    for step in range(1, DPS):
        for other in range(ROWS):
            group.append((lax.rem(dp + step, DPS), lax.rem(row + other, ROWS), col))
    return group


def remote(src, dst, send, recv, target):
    return pltpu.make_async_remote_copy(
        src_ref=src, dst_ref=dst, send_sem=send, recv_sem=recv, device_id=target, device_id_type=MESH
    )


N_W = 4


def slot(name, ref, row, dp, half=None):
    if name < 2:
        return ref.at[row, dp] if half is None else ref.at[row, dp, half]
    columns = pl.ds(pl.multiple_of(row * 256, 256), 256)
    return ref.at[dp, :, :, columns] if half is None else ref.at[dp, half, :, columns]


def gather_kernel(cols, *refs):
    (tok_ref, cot_ref, small_ref, wq_ref, wu_ref, wd_ref, wp_ref) = refs[:7]
    (x_ref, c_ref, smalls_ref, gq_ref, gu_ref, gd_ref, gp_ref) = refs[7:14]
    (z_send, z_recv, s1_send, s1_recv, s2_send, s2_recv, t_send, t_recv, a_send, a_recv, m_send, m_recv, l_sem) = refs[14:]
    own = (wq_ref, wu_ref, wd_ref, wp_ref)
    full = (gq_ref, gu_ref, gd_ref, gp_ref)
    dp, row, col, across, along = places()
    side, at = line_order(row)
    order = [row, at(1 - side), at(2), at(3)]
    middle = side == 1
    tok_col = tok_ref.shape[0]
    part = SEQ_LEN // cols
    chunk = min(tok_col, SEQ_LEN)
    n_seq = tok_col // chunk
    n_part = chunk // part

    greet(peers_of(dp, row, col, cols))

    waits = []

    def token_copy(kind, j, i):
        src_ref, dst_ref = ((tok_ref, x_ref), (cot_ref, c_ref))[kind]
        start = col * tok_col + j * chunk
        to_row = start // SEQ_LEN
        piece = lax.rem(start, SEQ_LEN) // part + i
        src = src_ref.at[pl.ds(j * chunk + i * part, part), :]
        dst = dst_ref.at[pl.ds(pl.multiple_of(piece * part, part), part), pl.ds(pl.multiple_of(row * 256, 256), 256)]
        sends, recvs = t_send.at[kind, j * n_part + i], t_recv.at[kind, row]
        is_here = jnp.logical_and(to_row == row, piece == col)
        far = remote(src, dst, sends, recvs, (dp, to_row, piece))
        near = pltpu.make_async_copy(src, dst, recvs)
        return is_here, far, near

    def token_start(kind):
        for j in range(n_seq):
            for i in range(n_part):
                is_here, far, near = token_copy(kind, j, i)
                pl.when(jnp.logical_not(is_here))(far.start)
                pl.when(is_here)(near.start)

    def part_rows(piece):
        return pl.ds(pl.multiple_of(piece * part, part), part)

    def spread_copy(kind, step):
        dst_ref = (x_ref, c_ref)[kind]
        mine = dst_ref.at[part_rows(col), :]
        to_col = lax.rem(col + step, cols)
        return remote(mine, mine, a_send.at[kind, step - 1], a_recv.at[kind, step - 1], (dp, row, to_col))

    def token_spread(kind):
        dst_ref = (x_ref, c_ref)[kind]
        for other in range(ROWS):
            block = dst_ref.at[part_rows(col), pl.ds(other * 256, 256)]
            pltpu.make_async_copy(block, block, t_recv.at[kind, other]).wait()
        for step in range(1, cols):
            spread_copy(kind, step).start()

    def token_finish(kind):
        dst_ref = (x_ref, c_ref)[kind]
        for j in range(n_seq):
            for i in range(n_part):
                is_here, far, near = token_copy(kind, j, i)
                pl.when(jnp.logical_not(is_here))(far.wait_send)
        for step in range(1, cols):
            copy = spread_copy(kind, step)
            copy.wait_send()
            from_col = lax.rem(col + cols - step, cols)
            theirs = dst_ref.at[part_rows(from_col), :]
            pltpu.make_async_copy(theirs, theirs, a_recv.at[kind, step - 1]).wait()

    me = row * DPS + dp

    def small_copy(step):
        flat = lax.rem(me + step, ROWS * DPS)
        return remote(
            small_ref, smalls_ref.at[me], m_send.at[step - 1], m_recv.at[step - 1], (lax.rem(flat, DPS), flat // DPS, col)
        )

    def source(w, k, half=None):
        if k == 0:
            return own[w] if half is None else own[w].at[half]
        return slot(w, full[w], order[k], dp, half)

    def line_copies(w, k):
        src = source(w, k)
        dst = slot(w, full[w], order[k], dp)
        recv = z_recv.at[w, order[k]]
        if k == 0:
            return [
                (None, remote(src, dst, z_send.at[w, 0], recv, (dp, at(1 - side), col))),
                (middle, remote(src, dst, z_send.at[w, 1], recv, (dp, at(2), col))),
            ]
        onward = at(2) if k == 1 else at(0)
        return [(middle, remote(src, dst, z_send.at[w, k + 1], recv, (dp, onward, col)))]

    def first_copies(w, k):
        out = []
        for half, target in ((0, across), (1, along)):
            out.append(
                remote(source(w, k, half), slot(w, full[w], order[k], dp, half), s1_send.at[w, k, half],
                       s1_recv.at[w, k, half], (target, row, col))
            )
        return out

    def second_copies(w, k, which):
        out = []
        for half, target, other in ((0, along, across), (1, across, along)):
            if which == 0:
                src, owner = source(w, k, half), dp
            else:
                src, owner = slot(w, full[w], order[k], other, half), other
            out.append(
                remote(src, slot(w, full[w], order[k], owner, half), s2_send.at[w, k, which, half],
                       s2_recv.at[w, k, which, half], (target, row, col))
            )
        return out

    def arrived(w, k):
        if k > 0:
            block = slot(w, full[w], order[k], dp)
            pltpu.make_async_copy(block, block, z_recv.at[w, order[k]]).wait()
        for cond, copy in line_copies(w, k):
            if cond is None:
                copy.start()
            else:
                pl.when(cond)(copy.start)
        for copy in first_copies(w, k) + second_copies(w, k, 0):
            copy.start()

    def passed(w, k):
        for copy in first_copies(w, k):
            copy.wait_recv()
        for copy in second_copies(w, k, 1):
            copy.start()

    def finished(w, k):
        for which in range(2):
            for copy in second_copies(w, k, which):
                copy.wait_recv()

    def drained(w, k):
        for cond, copy in line_copies(w, k):
            if cond is None:
                copy.wait_send()
            else:
                pl.when(cond)(copy.wait_send)
        for copy in first_copies(w, k) + second_copies(w, k, 0) + second_copies(w, k, 1):
            copy.wait_send()

    def home(w):
        return pltpu.make_async_copy(own[w], slot(w, full[w], row, dp), l_sem.at[w])

    small_home = pltpu.make_async_copy(small_ref, smalls_ref.at[me], l_sem.at[N_W])
    small_home.start()
    for step in range(1, ROWS * DPS):
        small_copy(step).start()
    token_start(0)
    for w in range(N_W):
        arrived(w, 0)
        home(w).start()
    token_start(1)
    token_spread(0)
    for w in range(N_W):
        passed(w, 0)
        for k in range(1, 4):
            arrived(w, k)
        for k in range(1, 4):
            passed(w, k)
    token_spread(1)
    for w in range(N_W):
        for k in range(4):
            finished(w, k)
            drained(w, k)
        home(w).wait()
    small_home.wait()
    for step in range(1, ROWS * DPS):
        small_copy(step).wait()
    for kind in range(2):
        token_finish(kind)


def gather(tokens_in, cotangent, small, weights, cols):
    wq, wu, wd, wp = weights
    any_spec = pl.BlockSpec(memory_space=pl.ANY)
    shapes = [
        jax.ShapeDtypeStruct((SEQ_LEN, D), BF),
        jax.ShapeDtypeStruct((SEQ_LEN, D), BF),
        jax.ShapeDtypeStruct((ROWS * DPS,) + small.shape, F32),
        jax.ShapeDtypeStruct((ROWS, DPS) + wq.shape, BF),
        jax.ShapeDtypeStruct((ROWS, DPS) + wu.shape, BF),
        jax.ShapeDtypeStruct((DPS,) + wd.shape[:2] + (D,), BF),
        jax.ShapeDtypeStruct((DPS,) + wp.shape[:2] + (D,), BF),
    ]
    tok_col = tokens_in.shape[0]
    pieces = tok_col // (SEQ_LEN // cols)
    dma = pltpu.SemaphoreType.DMA
    return pl.pallas_call(
        functools.partial(gather_kernel, cols),
        out_shape=shapes,
        in_specs=[any_spec] * 7,
        out_specs=[any_spec] * 7,
        scratch_shapes=[
            dma((N_W, 5)), dma((N_W, 4)), dma((N_W, 4, 2)), dma((N_W, 4, 2)), dma((N_W, 4, 2, 2)), dma((N_W, 4, 2, 2)),
            dma((2, pieces)), dma((2, 4)), dma((2, cols - 1)), dma((2, cols - 1)),
            dma((ROWS * DPS - 1,)), dma((ROWS * DPS - 1,)), dma((N_W + 1,)),
        ],
        compiler_params=pltpu.CompilerParams(collective_id=0, has_side_effects=True),
    )(tokens_in, cotangent, small, wq, wu, wd, wp)


def lead(name, y, x, half):
    return (slice(None), y, x, half) if name < 2 else (y, x, half)


def add_into(dst, src):
    shape = dst.shape
    outer, height = shape[:-2], shape[-2]
    step = 32
    per = height // step
    total = math.prod(outer) * per

    def body(i, carry):
        index, rest = [], i // per
        for size in reversed(outer):
            index.append(lax.rem(rest, size))
            rest = rest // size
        where = tuple(reversed(index)) + (pl.ds(pl.multiple_of(lax.rem(i, per) * step, step), step),)
        dst[where] = (dst[where].astype(F32) + src[where].astype(F32)).astype(BF)
        return carry

    lax.fori_loop(0, total, body, 0)


def scatter_kernel(cols, heights, *refs):
    g_refs = refs[:4]
    out_refs = refs[4:8]
    mine = (refs[8:10], refs[10:12], refs[12:14], refs[14:16])
    got1 = (refs[16:18], refs[18:20], refs[20:22], refs[22:24])
    got2 = (refs[24:26], refs[26:28], refs[28:30], refs[30:32])
    got3 = (refs[32:34], refs[34:36], refs[36:38], refs[38:40])
    l_sem, s1_send, s1_recv, s2_send, s2_recv, s3_send, s3_recv = refs[40:]
    dp, row, col, across, along = places()
    x, y = lax.rem(dp, 2), dp // 2

    greet(peers_of(dp, row, col, cols))

    def first(w, half):
        if half == 0:
            src, target = g_refs[w].at[lead(w, 1 - y, slice(None), 0)], along
        else:
            src, target = g_refs[w].at[lead(w, slice(None), 1 - x, 1)], across
        return remote(src, got1[w][half], s1_send.at[w, half], s1_recv.at[w, half], (target, row, col))

    def fetch(w, half):
        src = g_refs[w].at[lead(w, y, slice(None), 0)] if half == 0 else g_refs[w].at[lead(w, slice(None), x, 1)]
        return pltpu.make_async_copy(src, mine[w][half], l_sem.at[w, half])

    def keep(w, half, other):
        which = (x if half == 0 else y)
        which = 1 - which if other else which
        return mine[w][half].at[:, which] if w < 2 else mine[w][half].at[which]

    def second(w, half):
        target = across if half == 0 else along
        return remote(keep(w, half, True), got2[w][half], s2_send.at[w, half], s2_recv.at[w, half], (target, row, col))

    def block(w, half, r):
        kept = keep(w, half, False)
        if w < 2:
            return kept.at[r]
        return kept.at[:, pl.ds(pl.multiple_of(r * 256, 256), 256)]

    def third(w, half, step):
        to_row = lax.rem(row + step, ROWS)
        return remote(
            block(w, half, to_row), got3[w][half].at[step - 1], s3_send.at[w, half, step - 1],
            s3_recv.at[w, half, step - 1], (dp, to_row, col)
        )

    def total(w, half):
        height = out_refs[w].shape[1]
        step = 32

        def body(i, carry):
            rows = pl.ds(pl.multiple_of(i * step, step), step)
            value = block(w, half, row)[rows, :].astype(F32)
            for s in range(3):
                value = value + got3[w][half][s, rows, :].astype(F32)
            out_refs[w][half, rows, :] = value
            return carry

        lax.fori_loop(0, height // step, body, 0)

    sequence = [(w, half) for w in (0, 1, 2, 3) for half in range(2)]
    for w, half in sequence:
        first(w, half).start()
        fetch(w, half).start()

    def stage_two(w, half):
        fetch(w, half).wait()
        first(w, half).wait_recv()
        add_into(mine[w][half], got1[w][half])
        second(w, half).start()

    def stage_three(w, half):
        second(w, half).wait()
        add_into(keep(w, half, False), got2[w][half])
        for step in range(1, ROWS):
            third(w, half, step).start()

    def stage_four(w, half):
        for step in range(1, ROWS):
            third(w, half, step).wait()
        total(w, half)

    lag2, lag3 = 2, 4
    n = len(sequence)
    for i in range(n + lag3):
        if i < n:
            stage_two(*sequence[i])
        if 0 <= i - lag2 < n:
            stage_three(*sequence[i - lag2])
        if 0 <= i - lag3 < n:
            stage_four(*sequence[i - lag3])
    for w, half in sequence:
        first(w, half).wait_send()


def scatter(grads, cols):
    any_spec = pl.BlockSpec(memory_space=pl.ANY)
    vmem = pl.BlockSpec(memory_space=pltpu.VMEM)
    dma = pltpu.SemaphoreType.DMA
    outs, mine, got1, got2, got3 = [], [], [], [], []
    for w, grad in enumerate(grads):
        h, n = grad.shape[-2:]
        if w < 2:
            outs.append(jax.ShapeDtypeStruct((2, h, n), F32))
            mine += [pltpu.VMEM((ROWS, 2, h, n), BF)] * 2
            got1 += [pltpu.VMEM((ROWS, 2, h, n), BF)] * 2
            got2 += [pltpu.VMEM((ROWS, h, n), BF)] * 2
            got3 += [pltpu.VMEM((3, h, n), BF)] * 2
        else:
            outs.append(jax.ShapeDtypeStruct((2, h, 256), F32))
            mine += [pltpu.VMEM((2, h, n), BF)] * 2
            got1 += [pltpu.VMEM((2, h, n), BF)] * 2
            got2 += [pltpu.VMEM((h, n), BF)] * 2
            got3 += [pltpu.VMEM((3, h, 256), BF)] * 2
    return pl.pallas_call(
        functools.partial(scatter_kernel, cols, None),
        out_shape=outs,
        in_specs=[any_spec] * 4,
        out_specs=[vmem] * 4,
        scratch_shapes=mine + got1 + got2 + got3 + [
            dma((N_W, 2)), dma((N_W, 2)), dma((N_W, 2)), dma((N_W, 2)), dma((N_W, 2)), dma((N_W, 2, 3)), dma((N_W, 2, 3)),
        ],
        compiler_params=pltpu.CompilerParams(collective_id=1, has_side_effects=True, vmem_limit_bytes=48 << 20),
    )(*grads)


def angles_table():
    half_rot = ROT // 2
    places_ = jnp.arange(SEQ_LEN, dtype=F32)
    rates = jnp.exp(jnp.arange(half_rot, dtype=F32) * (-2.0 * math.log(10000.0) / ROT))
    turned = places_[:, None] * rates[None, :]
    return (jnp.cos(turned), jnp.sin(turned))


def rotate(paired, cos_table, sin_table):
    half_rot = cos_table.shape[1]
    cos_wide = cos_table[:, None, None, :]
    sin_wide = sin_table[:, None, None, :]
    first_half = paired[..., :half_rot]
    second_half = paired[..., half_rot : 2 * half_rot]
    return jnp.concatenate(
        [
            first_half * cos_wide - second_half * sin_wide,
            second_half * cos_wide + first_half * sin_wide,
            paired[..., 2 * half_rot :],
        ],
        axis=-1,
    )


def score_block(queries, key_rows, prefix_end):
    scores = jnp.einsum("qhd,khd->hqk", queries, key_rows, preferred_element_type=F32) * HD ** (-0.5)
    at = jnp.arange(SEQ_LEN)
    visible = (at[None, :] <= at[:, None]) | (at[None, :] < prefix_end)
    return jnp.where(visible[None], scores, NEGATIVE)


def attend_forward(queries, key_rows, value_rows, prefix_end):
    scores = score_block(queries, key_rows, prefix_end)
    highest = jnp.max(scores, axis=-1, keepdims=True)
    exp_total = jnp.sum(jnp.exp(scores - highest), axis=-1, keepdims=True)
    log_sum = highest + jnp.log(exp_total)
    weights = jnp.exp(scores - log_sum).astype(BF)
    outputs = jnp.einsum("hqk,khd->qhd", weights, value_rows, preferred_element_type=F32)
    return (outputs, log_sum[..., 0])


def attend_backward(queries, key_rows, value_rows, prefix_end, log_sum, upstream):
    scores = score_block(queries, key_rows, prefix_end)
    chances = jnp.exp(scores - log_sum[..., None])
    grad_values = jnp.einsum("hqk,qhd->khd", chances.astype(BF), upstream, preferred_element_type=F32)
    grad_chances = jnp.einsum("qhd,khd->hqk", upstream, value_rows, preferred_element_type=F32)
    inner_sum = jnp.sum(chances * grad_chances, axis=-1, keepdims=True)
    grad_scores = (chances * (grad_chances - inner_sum)).astype(BF)
    grad_queries = jnp.einsum("hqk,khd->qhd", grad_scores, key_rows, preferred_element_type=F32) * HD ** (-0.5)
    grad_keys = jnp.einsum("hqk,qhd->khd", grad_scores, queries, preferred_element_type=F32) * HD ** (-0.5)
    return (grad_queries, grad_keys, grad_values)


def contract_rows(left_side, right_side):
    return lax.dot_general(left_side, right_side, (((0,), (0,)), ((), ())), preferred_element_type=F32)


def contract_cols(left_side, right_side):
    return lax.dot_general(left_side, right_side, (((1,), (1,)), ((), ())), preferred_element_type=F32)


def shards(cols, tokens_in, prefix_len, first_gain, first_shift, second_gain, second_shift, qkv_weight, qkv_bias,
           up_weight, up_bias, dense_weight, dense_bias, down_weight, down_bias, cotangent):
    tok_col = tokens_in.shape[0]
    n_q, n_u = qkv_weight.shape[1], up_weight.shape[1]
    h_d, h_p = dense_weight.shape[0], down_weight.shape[0]
    heads = n_q // (3 * HD)
    width_att = heads * HD

    weights = (
        qkv_weight.astype(BF).reshape(2, 32, n_q),
        up_weight.astype(BF).reshape(2, 32, n_u),
        dense_weight.astype(BF).reshape(2, h_d // 2, 256),
        down_weight.astype(BF).reshape(2, h_p // 2, 256),
    )
    pieces = (first_gain, first_shift, second_gain, second_shift, dense_bias, down_bias, qkv_bias, up_bias)
    small = jnp.concatenate(pieces)
    size = -(-small.shape[0] // 1024) * 1024
    small = jnp.pad(small, (0, size - small.shape[0])).reshape(size // 128, 128)
    own_x, own_cot, smalls, wq, wu, wd, wp = gather(tokens_in, cotangent, small, weights, cols)
    wq = wq.reshape(D, n_q)
    wu = wu.reshape(D, n_u)
    wd = wd.reshape(width_att, D)
    wp = wp.reshape(h_p * DPS, D)
    flat = smalls.reshape(ROWS, DPS, size)
    gains = [flat[:, 0, 256 * i : 256 * (i + 1)].reshape(D) for i in range(4)]
    out_bias = [flat[:, :, 1024 + 64 * i : 1088 + 64 * i].reshape(D).astype(BF).astype(F32) for i in range(2)]
    n_qb, n_ub = qkv_bias.shape[0], up_bias.shape[0]
    q_bias = flat[0, :, 1152 : 1152 + n_qb].reshape(n_q).astype(BF).astype(F32)
    u_bias = flat[0, :, 1152 + n_qb : 1152 + n_qb + n_ub].reshape(n_u).astype(BF).astype(F32)

    wide = own_x.astype(F32)
    center = jnp.mean(wide, axis=1, keepdims=True)
    spread = jnp.mean(wide * wide, axis=1, keepdims=True) - center * center
    scale_inv = lax.rsqrt(spread + EPS)
    normed = (wide - center) * scale_inv
    first_in = (normed * gains[0] + gains[1]).astype(BF)
    second_in = (normed * gains[2] + gains[3]).astype(BF)

    mixed = jnp.dot(first_in, wq, preferred_element_type=F32) + q_bias
    hidden_pre = jnp.dot(second_in, wu, preferred_element_type=F32) + u_bias
    mixed_heads = mixed.reshape(SEQ_LEN, heads, 3, HD)
    cos_table, sin_table = angles_table()
    turned = rotate(mixed_heads[:, :, :2, :], cos_table, sin_table).astype(BF)
    queries, key_rows = turned[:, :, 0, :], turned[:, :, 1, :]
    value_rows = mixed_heads[:, :, 2, :].astype(BF)
    outputs, log_sums = attend_forward(queries, key_rows, value_rows, prefix_len[0])
    attended = outputs.reshape(SEQ_LEN, width_att).astype(BF)
    hidden = jax.nn.gelu(hidden_pre, approximate=False).astype(BF)
    branch = jnp.dot(attended, wd, preferred_element_type=F32) + jnp.dot(hidden, wp, preferred_element_type=F32)

    upstream = contract_cols(own_cot, wd).astype(BF).reshape(SEQ_LEN, heads, HD)
    grad_hidden = contract_cols(own_cot, wp)
    ignored, gelu_back = jax.vjp(functools.partial(jax.nn.gelu, approximate=False), hidden_pre)
    grad_hidden_pre = gelu_back(grad_hidden)[0].astype(BF)
    grad_q, grad_k, grad_v = attend_backward(queries, key_rows, value_rows, prefix_len[0], log_sums, upstream)
    ignored, rotate_back = jax.vjp(lambda paired: rotate(paired, cos_table, sin_table), mixed_heads[:, :, :2, :])
    grad_pair = rotate_back(jnp.stack([grad_q, grad_k], axis=2))[0]
    grad_mixed = jnp.concatenate([grad_pair, grad_v[:, :, None, :]], axis=2).reshape(SEQ_LEN, n_q).astype(BF)

    grads = (
        contract_rows(first_in, grad_mixed).astype(BF).reshape(ROWS, 2, 2, 2, 32, n_q),
        contract_rows(second_in, grad_hidden_pre).astype(BF).reshape(ROWS, 2, 2, 2, 32, n_u),
        contract_rows(attended, own_cot).astype(BF).reshape(2, 2, 2, h_d // 2, D),
        contract_rows(hidden, own_cot).astype(BF).reshape(2, 2, 2, h_p // 2, D),
    )
    out_q, out_u, out_d, out_p = scatter(grads, cols)

    grad_first = contract_cols(grad_mixed, wq)
    grad_second = contract_cols(grad_hidden_pre, wu)
    combined = grad_first * gains[0] + grad_second * gains[2]
    part = SEQ_LEN // cols

    def to_owner(partial):
        moved = lax.all_to_all(partial, "row", split_axis=1, concat_axis=0, tiled=True)
        return lax.psum_scatter(moved, "col", scatter_dimension=0, tiled=True)

    branch_sum = to_owner(branch)
    combined = lax.psum(combined, "col")
    gain_rows = jnp.stack([
        jnp.sum(normed * grad_first, axis=0), jnp.sum(grad_first, axis=0),
        jnp.sum(normed * grad_second, axis=0), jnp.sum(grad_second, axis=0),
    ])
    line_total = jnp.mean(combined, axis=1, keepdims=True)
    cross_total = jnp.mean(combined * normed, axis=1, keepdims=True)
    grad_tokens = (own_cot.astype(F32) + scale_inv * (combined - line_total - normed * cross_total)).astype(BF)
    grad_tokens = lax.all_to_all(grad_tokens, "row", split_axis=1, concat_axis=0, tiled=True)
    grad_tokens = lax.dynamic_slice_in_dim(grad_tokens, lax.axis_index("col") * tok_col, tok_col, 0)
    row = lax.axis_index("row")
    here = [lax.dynamic_slice_in_dim(b, row * 256, 256, 0) for b in out_bias]
    layer_out = (tokens_in.astype(F32) + branch_sum + here[0] + here[1]).astype(BF)

    gain_sums = lax.psum_scatter(
        lax.psum(gain_rows, ("dp", "col")), "row", scatter_dimension=1, tiled=True
    )
    out_b = lax.psum_scatter(jnp.sum(own_cot.astype(F32), axis=0), ("row", "dp"), scatter_dimension=0, tiled=True)
    q_b = lax.psum_scatter(
        lax.psum(jnp.sum(grad_mixed.astype(F32), axis=0), "row"), "dp", scatter_dimension=0, tiled=True
    )
    u_b = lax.psum_scatter(
        lax.psum(jnp.sum(grad_hidden_pre.astype(F32), axis=0), "row"), "dp", scatter_dimension=0, tiled=True
    )
    return (
        layer_out, grad_tokens, out_q.reshape(64, n_q), q_b, out_u.reshape(64, n_u), u_b,
        out_d.reshape(h_d, 256), out_b, out_p.reshape(h_p, 256), out_b,
        gain_sums[0], gain_sums[1], gain_sums[2], gain_sums[3],
    )


def solution(mesh):
    in_specs = (
        P(("dp", "col"), "row"), P(("dp", "row")), P("row"), P("row"), P("row"), P("row"),
        P(("row", "dp"), "col"), P(("col", "dp")), P(("row", "dp"), "col"), P(("col", "dp")),
        P(("col", "dp"), "row"), P(("row", "dp")), P(("col", "dp"), "row"), P(("row", "dp")),
        P(("dp", "col"), "row"),
    )
    out_specs = (
        P(("dp", "col"), "row"), P(("dp", "col"), "row"), P(("row", "dp"), "col"), P(("col", "dp")),
        P(("row", "dp"), "col"), P(("col", "dp")), P(("col", "dp"), "row"), P(("row", "dp")),
        P(("col", "dp"), "row"), P(("row", "dp")), P("row"), P("row"), P("row"), P("row"),
    )
    body = functools.partial(shards, mesh.shape["col"])
    return jax.shard_map(body, mesh=mesh, in_specs=in_specs, out_specs=out_specs, check_vma=False)
```

time: 1510 us -> 735 us (0.49)
  waiting for transfers between devices: 980 us -> 29 us
  Pallas kernels: 0 us -> 298 us
  blocking collectives: 133 us -> 77.2 us
  other arithmetic: 115 us -> 83.7 us
  matrix products: 204 us -> 178 us
    all_gather x9 -> x0, waiting for transfers between devices: 872 us -> none  [the longest x1 466 us: shards(): grad_all = lax.all_gather(grad_inputs, 'row', axis=0, tiled=True)]
    pallas_call x0 -> x2, Pallas kernels: none -> 298 us  [the longest x1 150 us: scatter(): pl.pallas_call(functools.partial(scatter_kernel, cols, None), out_shape=o...]
    reduce_scatter x6 -> x1, waiting for transfers between devices: 56.8 us -> 0.01 us  [to_owner(): return lax.psum_scatter(moved, 'col', scatter_dimension=0, tiled=True)]
    psum x3 -> x2, blocking collectives: 79.6 us -> 25 us  [the longest x1 13.2 us: shards(): lax.psum(jnp.sum(grad_mixed.astype(F32), axis=0), 'row')]
    all_to_all x3 -> x2, waiting for transfers between devices: 50.2 us -> 0.01 us  [the longest x1 0.01 us: to_owner(): lax.all_to_all(partial, 'row', split_axis=1, concat_axis=0, tiled=True)]
    all_gather x4 -> x0, blocking collectives: 43.3 us -> none  [the longest x1 17 us: shards(): lax.all_gather(qkv_weight.astype(jnp.bfloat16), 'dp', axis=0, tiled=True)]
    unnamed x1 -> x2, blocking collectives: 9.92 us -> 52.2 us
    psum x0 -> x1, waiting for transfers between devices: none -> 28.9 us  [shards(): combined = lax.psum(combined, 'col')]
  transfers between devices with their start and end apart: 18 -> 5, of which waited for: 12 -> 1; matrix products, arithmetic and copies ran while one was open for 20% -> 21% of each run, Pallas kernels for 0% -> 20%
where the time goes in v1:
time: 735 us; the launch traced here: 730 us
  Pallas kernels  298 us (41%)
  matrix products  178 us (24%)
  other arithmetic  83.7 us (11%)
  blocking collectives  77.2 us (11%)
  local copies, waits for them, and re-layouts  35.9 us (5%)
  waiting for transfers between devices  29 us (4%)
  between operations  17.3 us (2%)
  starting transfers between devices  10.1 us (1%)
    pallas_call x1, Pallas kernels, scatter(): pl.pallas_call(functools.partial(scatter_kernel, cols, None), out_shape=o...  150 us
    pallas_call x1, Pallas kernels, gather(): pl.pallas_call(functools.partial(gather_kernel, cols), out_shape=shapes,...  148 us
    unnamed x2, blocking collectives  52.2 us
    dot_general x4, matrix products, contract_cols(): lax.dot_general(left_side, right_side, (((1,), (1,)), ((), ())), preferre...  38.5 us
    psum x1, waiting for transfers between devices, shards(): combined = lax.psum(combined, 'col')  28.9 us
    convert_element_type x1, other arithmetic, attend_backward(): grad_scores = (chances * (grad_chances - inner_sum)).astype(BF)  28.4 us
    dot_general x1, matrix products, attend_backward(): jnp.einsum('qhd,khd->hqk', upstream, value_rows, preferred_element_type=F32)  24 us
    dot_general x4, matrix products, contract_rows(): lax.dot_general(left_side, right_side, (((0,), (0,)), ((), ())), preferre...  22.6 us
  transfers between devices with their start and end apart: 5, of which 1 were waited for; matrix products, arithmetic and copies ran while one was open for 21% of the time, Pallas kernels for 20%

profile of v1, /device:TPU:0, one launch (start us, length us, event | category | flops | bytes accessed | tf_op | source)
XLA Modules:
  0.0 729.6 jit_solution(15375666904695701381)
XLA Ops:
  7.2 1.8 convert_element_type.149
  9.0 1.8 convert_element_type.151
  10.7 1.7 convert_element_type.148
  12.4 1.5 convert_element_type.150
  14.0 1.5 concatenate.10
  15.4 148.4 %shard_map.254 = (bf16[1024,1024]{1,0:T(8,128)(2,1)}, bf16[1024,1024]{1,0:T(8,128)(2,1)}, f32[16,16,128]{2,1,0:T(8,128)}, bf16[4,4,2,32,1536]{4,3,2,1,0:T(8,128)...) custom-call(bf16[2048,256]{1,0:T(8,128)(2,1)} %refs_0_.1, ...), custom_call_target="tpu_custom_call" | custom-call | tf_op jit(solution)/shard_map/pallas_call | solution.py:270
  163.8 0.9 reshape.252
  164.9 0.6 copy-done.24
  165.5 2.3 convert_reduce_fusion.2
  167.8 8.7 %convolution_add_fusion = f32[1024,1536]{1,0:T(8,128)} fusion(bf16[1024,1536]{1,0:T(8,128)(2,1)} %bitcast.161, f32[1536]{0:T(1024)S(1)} %reshape.267, bf16[1024,1024]{1,0:T(8,128)(2,1)} %get-tuple-element.25, f32[1024]{0:T(1024)S(1)} %bitcast.151, f32[1024]{0:T(1024)S(1)} %bitcast.148, f32[1024]{0:T(1024)S(1)} %get-tuple-element.74, ...), kind=kOutput, calls=%fused_computation.36 | convolution fusion | flops 3229089792 | bytes 11556864 | tf_op jit(solution)/shard_map/dot_general | solution.py:532
  176.5 7.0 copy.49
  183.8 3.3 copy.71
  188.3 1.3 subtract_convert_fusion
  189.9 13.6 %fusion = (f32[8,1024]{1,0:T(8,128)S(1)}, f32[8,1024,1024]{1,2,0:T(8,128)}) fusion(pred[1024,1024]{0,1:T(8,128)(4,1)S(1)} %fusion.26, bf16[1024,8,2,64]{0,3,1,2:T(8,128)(2,1)S(1)} %pad_maximum_fusion), kind=kOutput, calls=%fused_computation.5 | convolution fusion | flops 1098899456 | bytes 36732928 | tf_op jit(solution)/shard_map/qhd,khd->hqk/dot_general | solution.py:458
  203.5 14.2 %exponential_reduce_fusion = f32[8,1024]{1,0:T(8,128)S(1)} fusion(f32[8,1024,1024]{1,2,0:T(8,128)} %get-tuple-element.78, f32[8,1024]{1,0:T(8,128)S(1)} %get-tuple-element.77, pred[1024,1024]{0,1:T(8,128)(4,1)S(1)} %fusion.26), kind=kLoop, calls=%fused_computation.3 | loop fusion | flops 33546240 | bytes 34668544 | tf_op jit(solution)/shard_map/reduce_sum | solution.py:467
  217.8 15.1 %convolution_convert_fusion.5 = bf16[8,64,1024]{2,1,0:T(8,128)(2,1)S(1)} fusion(bf16[1024,8,3,64]{0,3,1,2:T(8,128)(2,1)} %copy-done.7, f32[8,1024,1024]{1,2,0:T(8,128)} %get-tuple-element.78, f32[8,1024]{1,0:T(8,128)S(1)} %log_add_fusion, pred[1024,1024]{0,1:T(8,128)(4,1)S(1)} %fusion.26), kind=kOutput, calls=%fused_computation.72 | convolution fusion | flops 1107820544 | bytes 36732928 | tf_op jit(solution)/shard_map/hqk,khd->qhd/dot_general | solution.py:470
  232.9 6.8 fusion.36
  239.8 25.7 %convert_reduce_fusion = (f32[2048]{0:T(1024)}, bf16[1024,2048]{1,0:T(8,128)(2,1)}, f32[1024,2048]{1,0:T(8,128)}) fusion(f32[1024,2048]{1,0:T(8,128)S(1)} %fusion.36, f32[2048]{0:T(1024)S(1)} %bitcast.137, bf16[1024,1024]{1,0:T(8,128)(2,1)S(1)} %copy-done.14, bf16[2048,1024]{1,0:T(8,128)(2,1)S(1)} %bitcast.160), kind=kOutput, calls=%fused_computation.9 | convolution fusion | flops 4452251648 | bytes 27279360 | tf_op jit(solution)/shard_map/dot_general | solution.py:491
  265.5 10.0 %multiply_convert_fusion.1 = bf16[1024,2048]{1,0:T(8,128)(2,1)} fusion(f32[1024,2048]{1,0:T(8,128)} %get-tuple-element.54, f32[1024,2048]{1,0:T(8,128)} %copy-done.8, f32[2048]{0:T(1024)S(1)} %bitcast.138), kind=kLoop, calls=%fused_computation.11 | loop fusion | flops 8388608 | bytes 20979712 | tf_op jit(solution)/shard_map/convert_element_type | solution.py:541
  275.5 7.7 %fusion.44 = f32[1024,1024]{0,1:T(8,128)S(1)} fusion(bf16[1024,2048]{1,0:T(8,128)(2,1)} %multiply_convert_fusion.1, bf16[2048,1024]{1,0:T(8,128)(2,1)} %bitcast.159), kind=kOutput, calls=%fused_computation.105 | convolution fusion | flops 4294967296 | bytes 12582912 | tf_op jit(solution)/shard_map/dot_general | solution.py:542
  283.2 3.3 convolution_add_fusion.1
  286.5 4.9 all-to-all-start
  291.4 2.5 convolution_convert_fusion.4
  294.0 24.0 %multiply_reduce_fusion = (f32[8,1024]{1,0:T(8,128)S(1)}, f32[8,1024,1024]{1,2,0:T(8,128)}) fusion(f32[8,1024,1024]{1,2,0:T(8,128)} %get-tuple-element.78, f32[8,1024]{1,0:T(8,128)S(1)} %log_add_fusion, pred[1024,1024]{0,1:T(8,128)(4,1)S(1)} %fusion.26, bf16[1024,8,64]{0,2,1:T(8,128)(2,1)S(1)} %bitcast.127, bf16[1024,8,3,64]{0,3,1,2:T(8,128)(2,1)} %copy-done.7), kind=kOutput, calls=%fused_computation.1 | convolution fusion | flops 1115676672 | bytes 70320128 | tf_op jit(solution)/shard_map/qhd,khd->hqk/dot_general | solution.py:478
  318.0 28.4 %multiply_convert_fusion = bf16[8,1024,1024]{1,2,0:T(8,128)(2,1)} fusion(f32[8,1024,1024]{1,2,0:T(8,128)} %get-tuple-element.80, f32[8,1024,1024]{1,2,0:T(8,128)} %get-tuple-element.78, f32[8,1024]{1,0:T(8,128)S(1)} %get-tuple-element.79, f32[8,1024]{1,0:T(8,128)S(1)} %log_add_fusion, pred[1024,1024]{0,1:T(8,128)(4,1)S(1)} %fusion.26), kind=kLoop, calls=%fused_computation | loop fusion | flops 50331648 | bytes 85000192 | tf_op jit(solution)/shard_map/convert_element_type | solution.py:480
  346.4 9.1 %multiply_bitcast_fusion.1 = f32[1024,8,1,64]{0,3,1,2:T(8,128)S(1)} fusion(bf16[8,1024,1024]{1,2,0:T(8,128)(2,1)} %multiply_convert_fusion, bf16[1024,8,2,64]{0,3,1,2:T(8,128)(2,1)} %copy-done.1), kind=kOutput, calls=%fused_computation.67 | convolution fusion | flops 1074266112 | bytes 19922944 | tf_op jit(solution)/shard_map/hqk,khd->qhd/dot_general | solution.py:481
  355.5 12.7 %multiply_bitcast_fusion = f32[1024,8,1,64]{0,3,1,2:T(8,128)} fusion(bf16[8,1024,1024]{1,2,0:T(8,128)(2,1)} %multiply_convert_fusion, bf16[1024,8,2,64]{0,3,1,2:T(8,128)(2,1)} %copy-done.1), kind=kOutput, calls=%fused_computation.66 | convolution fusion | flops 1074266112 | bytes 19922944 | tf_op jit(solution)/shard_map/hqk,qhd->khd/dot_general | solution.py:482
  368.2 3.5 fusion.27
  371.7 1.0 multiply_add_fusion.2
  372.7 16.3 %convolution_bitcast_fusion = bf16[1024,8,1,64]{0,3,1,2:T(8,128)(2,1)} fusion(bf16[1024,8,64]{0,2,1:T(8,128)(2,1)} %bitcast.128, f32[8,1024,1024]{1,2,0:T(8,128)} %get-tuple-element.78, f32[8,1024]{1,0:T(8,128)S(1)} %log_add_fusion, pred[1024,1024]{0,1:T(8,128)(4,1)S(1)} %fusion.26), kind=kOutput, calls=%fused_computation.69 | convolution fusion | flops 1107296256 | bytes 36732928 | tf_op jit(solution)/shard_map/hqk,qhd->khd/dot_general | solution.py:477
  389.0 1.3 multiply_add_fusion.1
  390.4 0.8 copy-done.6
  392.8 2.5 copy-done.40
  395.3 3.5 fusion.45
  398.9 6.8 multiply_add_fusion
  405.8 28.9 %all-reduce.10.cloned.1.call-done = f32[1024,1024]{1,0:T(8,128)} async-done(((f32[1024,1024]{1,0:T(8,128)}), f32[1024,1024]{1,0:T(8,128)}) %all-reduce.10.cloned.1.call-update) | async-done | bytes 4194320 | tf_op jit(solution)/shard_map/psum | solution.py:571
  434.7 5.7 fusion.40
  440.5 1.0 copy.65
  441.6 5.4 copy.54
  447.0 1.2 copy-done.12
  448.2 3.0 convolution_convert_fusion.3
  451.3 3.4 convert_reduce_fusion.3
  454.7 1.5 copy.74
  456.2 5.1 all-to-all-start.1
  461.3 6.6 convolution_convert_fusion
  468.0 6.2 convolution_convert_fusion.1
  474.2 6.8 convolution_convert_fusion.2
  481.0 149.5 %shard_map.255 = (f32[2,32,1536]{2,1,0:T(8,128)S(1)}, f32[2,32,2048]{2,1,0:T(8,128)S(1)}, f32[2,64,256]{2,1,0:T(8,128)S(1)}, f32[2,256,256]{2,1,0:T(8,128)S(1)}) custom-call(bf16[4,2,2,2,32,1536]{5,4,3,2,1,0:T(8,128)(2,1)S(1)} %bitcast.108, bf16[4,2,2,2,32,2048]{5,4,3,2,1,0:T(8,128)(2,1)} %bitcast.121, bf16[2,2,2,64,1024]{4,3,2,1,0:T(8,128)(2,1)S(1)} %bitcast.109, ...), custom_call_target="tpu_custom_call" | custom-call | tf_op jit(solution)/shard_map/pallas_call | solution.py:421
  630.6 0.6 dynamic-slice
  632.5 0.6 dynamic-slice.4
  633.1 0.8 slice_convert_fusion.1
  634.2 15.1 %all-reduce.7 = (f32[1536]{0:T(1024)S(1)}, f32[2048]{0:T(1024)S(1)}) all-reduce(f32[1536]{0:T(1024)S(1)} %reduce_sum.126, f32[2048]{0:T(1024)S(1)} %copy-done.29), channel_id=3, replica_groups=mesh['dp'=4,'row'=4,'col'=2] {'dp'}, use_global_device_ids=true, to_apply=%region_11.12.clone | all-reduce | flops 3584 | bytes 28672
  650.1 13.2 %all-reduce.6 = (f32[384]{0:T(512)}, f32[512]{0:T(512)}) all-reduce(f32[384]{0:T(512)S(1)} %dynamic-slice.1, f32[512]{0:T(512)S(1)} %dynamic-slice.3), channel_id=1, replica_groups=mesh['dp'=4,'row'=4,'col'=2] {'row'}, use_global_device_ids=true, to_apply=%region_10.11 | all-reduce | flops 896 | bytes 7168 | tf_op jit(solution)/shard_map/psum | solution.py:590
  663.3 37.1 %all-reduce.5 = f32[1024]{0:T(1024)S(1)} all-reduce(f32[1024]{0:T(1024)S(1)} %get-tuple-element.61), channel_id=5, replica_groups=mesh['dp'=4,'row'=4,'col'=2] {'row','dp'}, use_global_device_ids=true, to_apply=%region_16.17.clone | all-reduce | flops 1024 | bytes 8192
  700.6 1.0 copy.66
  701.5 11.8 %psum.34 = f32[4,256]{1,0:T(4,128)S(1)} all-reduce(f32[4,256]{1,0:T(4,128)S(1)} %copy.66), channel_id=1, replica_groups=mesh['dp'=4,'row'=4,'col'=2] {'dp','col'}, use_global_device_ids=true, to_apply=%region_21.22 | all-reduce | flops 1024 | bytes 8192 | tf_op jit(solution)/shard_map/psum | solution.py:586
  713.3 0.6 fusion.43
  713.9 2.3 constant_dynamic-slice_fusion
  716.2 3.2 add_convert_fusion.1
  719.4 0.5 copy.82
  719.9 0.7 copy.83
  720.6 0.8 copy.84
  721.4 0.7 copy.85
  722.1 0.8 copy.86
  (126 shorter events, 3.6 us)
Async XLA Ops:
  164.8 11.8 %copy-start.34 = (f32[4,1,256]{2,1,0:T(1,128)}, f32[4,1,256]{2,1,0:T(1,128)S(1)}, u32[]{:S(2)}) copy-start(f32[4,1,256]{2,1,0:T(1,128)S(1)} %get-tuple-element.63) | copy-start | bytes 12292
  164.8 11.7 %copy-start.36 = (f32[4,1,256]{2,1,0:T(1,128)}, f32[4,1,256]{2,1,0:T(1,128)S(1)}, u32[]{:S(2)}) copy-start(f32[4,1,256]{2,1,0:T(1,128)S(1)} %get-tuple-element.66) | copy-start | bytes 12292
  164.8 68.1 %copy-start.30 = (f32[4,1,256]{2,1,0:T(1,128)}, f32[4,1,256]{2,1,0:T(1,128)S(1)}, u32[]{:S(2)}) copy-start(f32[4,1,256]{2,1,0:T(1,128)S(1)} %get-tuple-element.64) | copy-start | bytes 12292
  164.8 68.1 %copy-start.32 = (f32[4,1,256]{2,1,0:T(1,128)}, f32[4,1,256]{2,1,0:T(1,128)S(1)}, u32[]{:S(2)}) copy-start(f32[4,1,256]{2,1,0:T(1,128)S(1)} %get-tuple-element.65) | copy-start | bytes 12292
  164.8 0.6 copy-start.24
  167.8 65.1 %copy-start.25 = (f32[1024]{0:T(1024)}, f32[1024]{0:T(1024)S(1)}, u32[]{:S(2)}) copy-start(f32[1024]{0:T(1024)S(1)} %get-tuple-element.73) | copy-start | bytes 12292
  167.8 65.1 %copy-start.27 = (f32[1024]{0:T(1024)}, f32[1024]{0:T(1024)S(1)}, u32[]{:S(2)}) copy-start(f32[1024]{0:T(1024)S(1)} %get-tuple-element.74) | copy-start | bytes 12292
  183.8 4.5 copy-start.20
  183.8 4.5 copy-start.22
  187.1 2.6 copy-start.7
  189.9 13.6 %copy-start.1 = (bf16[1024,8,2,64]{0,3,1,2:T(8,128)(2,1)}, bf16[1024,8,2,64]{0,3,1,2:T(8,128)(2,1)S(1)}, u32[]{:S(2)}) copy-start(bf16[1024,8,2,64]{0,3,1,2:T(8,128)(2,1)S(1)} %pad_maximum_fusion) | copy-start | bytes 6291460
  217.7 15.1 %copy-start.2 = (bf16[1024,1024]{1,0:T(8,128)(2,1)S(1)}, bf16[1024,1024]{1,0:T(8,128)(2,1)}, u32[]{:S(2)}) copy-start(bf16[1024,1024]{1,0:T(8,128)(2,1)} %get-tuple-element.25) | copy-start | bytes 6291460
  232.8 50.3 %copy-start.11 = (bf16[8,64,1024]{2,1,0:T(8,128)(2,1)}, bf16[8,64,1024]{2,1,0:T(8,128)(2,1)S(1)}, u32[]{:S(2)}) copy-start(bf16[8,64,1024]{2,1,0:T(8,128)(2,1)S(1)} %convolution_convert_fusion.5) | copy-start | bytes 3145732
  232.9 6.9 copy-start.14
  232.9 6.9 copy-start.39
  239.8 25.8 %copy-start.8 = (f32[1024,2048]{1,0:T(8,128)}, f32[1024,2048]{1,0:T(8,128)S(1)}, u32[]{:S(2)}) copy-start(f32[1024,2048]{1,0:T(8,128)S(1)} %fusion.36) | copy-start | bytes 25165828
  275.5 7.7 %copy-start.18 = (bf16[4,2,64,1024]{3,2,1,0:T(8,128)(2,1)S(1)}, bf16[4,2,64,1024]{3,2,1,0:T(8,128)(2,1)}, u32[]{:S(2)}) copy-start(bf16[4,2,64,1024]{3,2,1,0:T(8,128)(2,1)} %get-tuple-element.28) | copy-start | bytes 3145732
  286.5 155.2 %all-to-all-start = ((f32[1024,4,256]{0,2,1:T(8,128)}), f32[1024,4,256]{0,2,1:T(8,128)}, u32[]{:S(2)}, u32[]{:S(2)}) async-start(f32[1024,4,256]{0,2,1:T(8,128)} %bitcast.114), calls=%async_computation | async-start | bytes 8388608 | tf_op jit(solution)/shard_map/all_to_all | solution.py:567
  291.4 143.3 %all-reduce.10.cloned.1.call-start = ((), (), s32[]{:S(2)}) async-start(), calls=%async_computation.5 | async-start | bytes 8388608 | tf_op jit(solution)/shard_map/psum | solution.py:571
  294.0 24.0 %copy-start.17 = (bf16[1024,512]{0,1:T(8,128)(2,1)}, bf16[1024,512]{0,1:T(8,128)(2,1)S(1)}, u32[]{:S(2)}) copy-start(bf16[1024,512]{0,1:T(8,128)(2,1)S(1)} %convolution_convert_fusion.4) | copy-start | bytes 3145732
  368.2 3.5 copy-start
  368.2 3.5 copy-start.21
  368.2 3.5 copy-start.23
  389.0 2.1 copy-start.6
  389.0 2.2 copy-start.16
  390.4 1.5 copy-start.19
  392.3 3.0 copy-start.40
  392.8 6.0 copy-start.13
  395.3 3.5 copy-start.33
  395.3 3.5 copy-start.35
  395.3 3.5 copy-start.38
  395.3 3.5 copy-start.44
  398.8 6.9 copy-start.10
  405.7 29.0 %copy-start.3 = (bf16[1024,1024]{1,0:T(8,128)(2,1)S(1)}, bf16[1024,1024]{1,0:T(8,128)(2,1)}, u32[]{:S(2)}) copy-start(bf16[1024,1024]{1,0:T(8,128)(2,1)} %get-tuple-element.25) | copy-start | bytes 6291460
  405.7 29.0 %copy-start.26 = (f32[1024]{0:T(1024)S(1)}, f32[1024]{0:T(1024)}, u32[]{:S(2)}) copy-start(f32[1024]{0:T(1024)} %copy-done.25) | copy-start | bytes 12292
  405.7 29.0 %copy-start.28 = (f32[1024]{0:T(1024)S(1)}, f32[1024]{0:T(1024)}, u32[]{:S(2)}) copy-start(f32[1024]{0:T(1024)} %copy-done.27) | copy-start | bytes 12292
  405.8 294.8 %reduce-scatter.7.cloned.1.call-start = ((), (), s32[]{:S(2)}) async-start(), calls=%async_computation.6 | async-start | bytes 655360
  441.6 274.6 %reduce-scatter.5.cloned.1.call-start = ((), (), s32[]{:S(2)}) async-start(), calls=%async_computation.4 | async-start | bytes 6291456 | tf_op jit(solution)/shard_map/reduce_scatter | solution.py:568
  447.0 1.2 copy-start.12
  448.2 3.0 copy-start.5
  454.7 6.6 copy-start.37
  456.2 257.7 %all-to-all-start.1 = ((bf16[1024,4,256]{2,0,1:T(8,128)(2,1)}), bf16[1024,4,256]{2,0,1:T(8,128)(2,1)}, u32[]{:S(2)}, u32[]{:S(2)}) async-start(bf16[1024,4,256]{2,0,1:T(8,128)(2,1)} %bitcast.119), calls=%async_computation.2 | async-start | bytes 4194304 | tf_op jit(solution)/shard_map/all_to_all | solution.py:579
  461.3 6.7 copy-start.9
  461.3 6.7 copy-start.15
  468.0 6.2 copy-start.4
  468.0 6.2 copy-start.31
  468.0 6.2 copy-start.45
  481.0 149.6 %copy-start.42 = (u32[32]{0:T(128)S(1)}, u32[32]{0:T(128)}, u32[]{:S(2)}) copy-start(u32[32]{0:T(128)} %constant.107) | copy-start | bytes 388
  481.0 151.5 %copy-start.41 = (u32[32]{0:T(128)S(1)}, u32[32]{0:T(128)}, u32[]{:S(2)}) copy-start(u32[32]{0:T(128)} %constant.115) | copy-start | bytes 388
  481.0 153.3 %copy-start.29 = (f32[2048]{0:T(1024)S(1)}, f32[2048]{0:T(1024)}, u32[]{:S(2)}) copy-start(f32[2048]{0:T(1024)} %get-tuple-element.52) | copy-start | bytes 24580
  700.6 21.5 %copy-start.43 = (f32[64]{0:T(128)}, f32[64]{0:T(128)S(1)}, u32[]{:S(2)}) copy-start(f32[64]{0:T(128)S(1)} %dynamic-slice.5) | copy-start | bytes 772
Sparse Core Ops, SparseCore 0:
  405.9 28.8 all-reduce.9
  441.7 22.8 reduce-scatter.6
  467.0 10.3 reduce-scatter.4

commit v2 on v1

--- a/solution.py
+++ b/solution.py
@@ -31,8 +31,7 @@
 
 def line_order(row):
     far = row // 2
-    side = row - 3 * far + 2 * far * (3 - row)
-    side = lax.rem(jnp.abs(side), 2)
+    side = row + far * (3 - 2 * row)
     at = lambda place: far * 3 + (1 - 2 * far) * place
     return side, at
 
@@ -62,21 +61,161 @@
 
 
 N_W = 4
-
-
-def slot(name, ref, row, dp, half=None):
-    if name < 2:
-        return ref.at[row, dp] if half is None else ref.at[row, dp, half]
-    columns = pl.ds(pl.multiple_of(row * 256, 256), 256)
-    return ref.at[dp, :, :, columns] if half is None else ref.at[dp, half, :, columns]
-
-
-def gather_kernel(cols, *refs):
-    (tok_ref, cot_ref, small_ref, wq_ref, wu_ref, wd_ref, wp_ref) = refs[:7]
-    (x_ref, c_ref, smalls_ref, gq_ref, gu_ref, gd_ref, gp_ref) = refs[7:14]
-    (z_send, z_recv, s1_send, s1_recv, s2_send, s2_recv, t_send, t_recv, a_send, a_recv, m_send, m_recv, l_sem) = refs[14:]
-    own = (wq_ref, wu_ref, wd_ref, wp_ref)
-    full = (gq_ref, gu_ref, gd_ref, gp_ref)
+QKV, UP, DENSE, DOWN = range(N_W)
+
+
+def nt(left, right):
+    return lax.dot_general(left, right, (((1,), (1,)), ((), ())), preferred_element_type=F32)
+
+
+def nn(left, right):
+    return jnp.dot(left, right, preferred_element_type=F32)
+
+
+def span(start, size, unit):
+    return pl.ds(pl.multiple_of(start, unit), size)
+
+
+def slot(w, ref, row, dp, height, half=None):
+    if w in (QKV, UP):
+        if half is None:
+            return ref.at[span((row * DPS + dp) * height, height, 64), :]
+        return ref.at[span((row * DPS + dp) * height + half * (height // 2), height // 2, 32), :]
+    if half is None:
+        return ref.at[span(dp * height, height, 16), span(row * 256, 256, 256)]
+    if w == DENSE:
+        return ref.at[span(dp * height, height, 16), span(row * 256 + half * 128, 128, 128)]
+    return ref.at[span(dp * height + half * (height // 2), height // 2, 16), span(row * 256, 256, 256)]
+
+
+def half_of(w, ref, half):
+    height = ref.shape[0]
+    if w == DENSE:
+        return ref.at[:, pl.ds(half * 128, 128)]
+    return ref.at[pl.ds(half * (height // 2), height // 2), :]
+
+
+def read_gains(smalls, gains):
+    for r in range(ROWS):
+        for g in range(4):
+            for t in range(2):
+                gains[g : g + 1, pl.ds(r * 256 + t * 128, 128)] = smalls[r * DPS, pl.ds(2 * g + t, 1), :]
+
+
+def read_bias(smalls, bias, first_row, size):
+    per = size // 128
+    for d in range(DPS):
+        for t in range(per):
+            bias[0:1, pl.ds(d * size + t * 128, 128)] = smalls[d, pl.ds(first_row + t, 1), :]
+
+
+def norm_rows(x):
+    center = jnp.mean(x, axis=1, keepdims=True)
+    spread = jnp.mean(x * x, axis=1, keepdims=True) - center * center
+    scale_inv = lax.rsqrt(spread + EPS)
+    return (x - center) * scale_inv, scale_inv
+
+
+def norm_stage(x_ref, gains, which, plain, turned):
+    def body(i, carry):
+        rows = span(i * 128, 128, 128)
+        normed, ignored = norm_rows(x_ref[rows, :].astype(F32))
+        value = (normed * gains[which : which + 1, :] + gains[which + 1 : which + 2, :]).astype(BF)
+        plain[rows, :] = value
+        turned[:, rows] = value.T
+        return carry
+
+    lax.fori_loop(0, SEQ_LEN // 128, body, 0)
+
+
+def project_stage(wq, first, bias_row, angles, q_t, k_t, v_t, k_n, v_n, heads):
+    pair = min(heads, 2)
+    width = 192 * pair
+
+    def body(p, carry):
+        cols = pl.ds(0, width) if heads == pair else span(p * width, width, 128)
+        w_t = wq[:, cols].T
+        bias = jnp.broadcast_to(bias_row[0:1, cols], (8, width)).T[:, 0:1]
+        for j in range(SEQ_LEN // 256):
+            toks = pl.ds(j * 256, 256)
+            mixed = nt(w_t, first[toks, :]) + bias
+            cos, sin = angles[0:8, toks], angles[8:16, toks]
+
+            def turn(base):
+                x1, x2 = mixed[base : base + 8], mixed[base + 8 : base + 16]
+                return jnp.concatenate([x1 * cos - x2 * sin, x2 * cos + x1 * sin, mixed[base + 16 : base + 64]], axis=0)
+
+            for e in range(pair):
+                base, h = 192 * e, pair * p + e
+                q_t[h, :, toks] = (turn(base) * HD ** (-0.5)).astype(BF)
+                keys, values = turn(base + 64).astype(BF), mixed[base + 128 : base + 192].astype(BF)
+                k_t[h, :, toks] = keys
+                v_t[h, :, toks] = values
+                k_n[h, toks, :] = keys.T
+                v_n[h, toks, :] = values.T
+        return carry
+
+    lax.fori_loop(0, heads // pair, body, 0)
+
+
+def upstream_stage(wd, c_ref, up_t, heads):
+    for j in range(SEQ_LEN // 256):
+        toks = pl.ds(j * 256, 256)
+        grad = nt(wd[...], c_ref[toks, :]).astype(BF)
+        for h in range(heads):
+            up_t[h, :, toks] = grad[HD * h : HD * (h + 1)]
+
+
+def attend_head(h, prefix, angles, q_t, k_t, v_t, k_n, v_n, up_t, att_t, gm_t, grad_q, grad_k, grad_v):
+    done = 0
+    for i in range(SEQ_LEN // 256):
+        low = 256 * i
+        seen = max(512, low + 256)
+        spot = pl.ds(low, 256)
+        q, up = q_t[h, :, spot], up_t[h, :, spot]
+        scores = nn(k_n[h, 0:seen, :], q)
+        plain = min(low, seen)
+        keys = lax.broadcasted_iota(jnp.int32, (seen - plain, 256), 0) + plain
+        queries = lax.broadcasted_iota(jnp.int32, (seen - plain, 256), 1) + low
+        masked = jnp.where((keys <= queries) | (keys < prefix), scores[plain:], NEGATIVE)
+        scores = jnp.concatenate([scores[:plain], masked], axis=0) if plain else masked
+        exponent = jnp.exp(scores - jnp.max(scores, axis=0, keepdims=True))
+        probs = exponent * (1.0 / jnp.sum(exponent, axis=0, keepdims=True))
+        weights = probs.astype(BF)
+        att_t[h, :, spot] = nn(v_t[h, :, 0:seen], weights).astype(BF)
+        grad_probs = nn(v_n[h, 0:seen, :], up)
+        inner = jnp.sum(probs * grad_probs, axis=0, keepdims=True)
+        grad_scores = (probs * (grad_probs - inner)).astype(BF)
+        grad_q[:, spot] = nn(k_t[h, :, 0:seen], grad_scores)
+        for total, part in ((grad_v, nt(up, weights)), (grad_k, nt(q, grad_scores))):
+            if done:
+                total[:, 0:done] += part[:, :done]
+            if seen > done:
+                total[:, done:seen] = part[:, done:]
+        done = seen
+    cos, sin = angles[0:8, :], angles[8:16, :]
+
+    def turn_back(grad):
+        g1, g2 = grad[0:8], grad[8:16]
+        return jnp.concatenate([g1 * cos + g2 * sin, g2 * cos - g1 * sin, grad[16:]], axis=0)
+
+    base = h * 192
+    gm_t[span(base, HD, HD), :] = (turn_back(grad_q[...]) * HD ** (-0.5)).astype(BF)
+    gm_t[span(base + HD, HD, HD), :] = turn_back(grad_k[...]).astype(BF)
+    gm_t[span(base + 2 * HD, HD, HD), :] = grad_v[...].astype(BF)
+
+
+def gather_kernel(cols, aligned, *refs):
+    (prefix_ref, tok_ref, cot_ref, small_ref, angles, bias_in) = refs[:6]
+    masters = refs[6:10]
+    (x_out, c_out, smalls_out, gq_ref, gu_ref, gd_ref, gp_ref, wgq_ref, wgd_ref, gm_ref, att_ref, gb_ref) = refs[10:22]
+    own = refs[22:26]
+    stage = refs[26:30]
+    (x_ref, c_ref, smalls, wq, wd, gains, bias_row, first, first_t) = refs[30:39]
+    (q_t, k_t, v_t, k_n, v_n, up_t, att_t, gm_t, grad_q, grad_k, grad_v) = refs[39:50]
+    (z_send, z_recv, s1_send, s1_recv, s2_send, s2_recv, t_send, t_recv, a_send, a_recv, m_send, m_recv, l_sem) = refs[50:]
+    full = (wq, gu_ref, wd, gp_ref)
+    heads = q_t.shape[0]
     dp, row, col, across, along = places()
     side, at = line_order(row)
     order = [row, at(1 - side), at(2), at(3)]
@@ -87,9 +226,10 @@
     n_seq = tok_col // chunk
     n_part = chunk // part
 
+    loads = [pltpu.make_async_copy(masters[w], stage[w], l_sem.at[w]) for w in range(N_W)]
+    for load in loads:
+        load.start()
     greet(peers_of(dp, row, col, cols))
-
-    waits = []
 
     def token_copy(kind, j, i):
         src_ref, dst_ref = ((tok_ref, x_ref), (cot_ref, c_ref))[kind]
@@ -97,7 +237,7 @@
         to_row = start // SEQ_LEN
         piece = lax.rem(start, SEQ_LEN) // part + i
         src = src_ref.at[pl.ds(j * chunk + i * part, part), :]
-        dst = dst_ref.at[pl.ds(pl.multiple_of(piece * part, part), part), pl.ds(pl.multiple_of(row * 256, 256), 256)]
+        dst = dst_ref.at[span(piece * part, part, part), span(row * 256, 256, 256)]
         sends, recvs = t_send.at[kind, j * n_part + i], t_recv.at[kind, row]
         is_here = jnp.logical_and(to_row == row, piece == col)
         far = remote(src, dst, sends, recvs, (dp, to_row, piece))
@@ -112,11 +252,10 @@
                 pl.when(is_here)(near.start)
 
     def part_rows(piece):
-        return pl.ds(pl.multiple_of(piece * part, part), part)
+        return span(piece * part, part, part)
 
     def spread_copy(kind, step):
-        dst_ref = (x_ref, c_ref)[kind]
-        mine = dst_ref.at[part_rows(col), :]
+        mine = (x_ref, c_ref)[kind].at[part_rows(col), :]
         to_col = lax.rem(col + step, cols)
         return remote(mine, mine, a_send.at[kind, step - 1], a_recv.at[kind, step - 1], (dp, row, to_col))
 
@@ -130,33 +269,38 @@
 
     def token_finish(kind):
         dst_ref = (x_ref, c_ref)[kind]
+        for step in range(1, cols):
+            from_col = lax.rem(col + cols - step, cols)
+            theirs = dst_ref.at[part_rows(from_col), :]
+            pltpu.make_async_copy(theirs, theirs, a_recv.at[kind, step - 1]).wait()
+
+    def token_drain(kind):
         for j in range(n_seq):
             for i in range(n_part):
                 is_here, far, near = token_copy(kind, j, i)
                 pl.when(jnp.logical_not(is_here))(far.wait_send)
         for step in range(1, cols):
-            copy = spread_copy(kind, step)
-            copy.wait_send()
-            from_col = lax.rem(col + cols - step, cols)
-            theirs = dst_ref.at[part_rows(from_col), :]
-            pltpu.make_async_copy(theirs, theirs, a_recv.at[kind, step - 1]).wait()
+            spread_copy(kind, step).wait_send()
 
     me = row * DPS + dp
 
     def small_copy(step):
         flat = lax.rem(me + step, ROWS * DPS)
         return remote(
-            small_ref, smalls_ref.at[me], m_send.at[step - 1], m_recv.at[step - 1], (lax.rem(flat, DPS), flat // DPS, col)
+            small_ref, smalls.at[me], m_send.at[step - 1], m_recv.at[step - 1], (lax.rem(flat, DPS), flat // DPS, col)
         )
+
+    def place(w, r, d, half=None):
+        return slot(w, full[w], r, d, own[w].shape[0], half)
 
     def source(w, k, half=None):
         if k == 0:
-            return own[w] if half is None else own[w].at[half]
-        return slot(w, full[w], order[k], dp, half)
+            return own[w] if half is None else half_of(w, own[w], half)
+        return place(w, order[k], dp, half)
 
     def line_copies(w, k):
         src = source(w, k)
-        dst = slot(w, full[w], order[k], dp)
+        dst = place(w, order[k], dp)
         recv = z_recv.at[w, order[k]]
         if k == 0:
             return [
@@ -170,7 +314,7 @@
         out = []
         for half, target in ((0, across), (1, along)):
             out.append(
-                remote(source(w, k, half), slot(w, full[w], order[k], dp, half), s1_send.at[w, k, half],
+                remote(source(w, k, half), place(w, order[k], dp, half), s1_send.at[w, k, half],
                        s1_recv.at[w, k, half], (target, row, col))
             )
         return out
@@ -181,16 +325,16 @@
             if which == 0:
                 src, owner = source(w, k, half), dp
             else:
-                src, owner = slot(w, full[w], order[k], other, half), other
+                src, owner = place(w, order[k], other, half), other
             out.append(
-                remote(src, slot(w, full[w], order[k], owner, half), s2_send.at[w, k, which, half],
+                remote(src, place(w, order[k], owner, half), s2_send.at[w, k, which, half],
                        s2_recv.at[w, k, which, half], (target, row, col))
             )
         return out
 
     def arrived(w, k):
         if k > 0:
-            block = slot(w, full[w], order[k], dp)
+            block = place(w, order[k], dp)
             pltpu.make_async_copy(block, block, z_recv.at[w, order[k]]).wait()
         for cond, copy in line_copies(w, k):
             if cond is None:
@@ -206,10 +350,11 @@
         for copy in second_copies(w, k, 1):
             copy.start()
 
-    def finished(w, k):
-        for which in range(2):
-            for copy in second_copies(w, k, which):
-                copy.wait_recv()
+    def finished(w):
+        for k in range(ROWS):
+            for which in range(2):
+                for copy in second_copies(w, k, which):
+                    copy.wait_recv()
 
     def drained(w, k):
         for cond, copy in line_copies(w, k):
@@ -221,64 +366,180 @@
             copy.wait_send()
 
     def home(w):
-        return pltpu.make_async_copy(own[w], slot(w, full[w], row, dp), l_sem.at[w])
-
-    small_home = pltpu.make_async_copy(small_ref, smalls_ref.at[me], l_sem.at[N_W])
+        return pltpu.make_async_copy(own[w], place(w, row, dp), l_sem.at[w])
+
+    def begin(w):
+        loads[w].wait()
+        own[w][...] = stage[w][...].astype(BF)
+        arrived(w, 0)
+        home(w).start()
+
+    small_home = pltpu.make_async_copy(small_ref, smalls.at[me], l_sem.at[N_W])
     small_home.start()
+    begin(QKV)
     for step in range(1, ROWS * DPS):
         small_copy(step).start()
     token_start(0)
-    for w in range(N_W):
-        arrived(w, 0)
-        home(w).start()
+    begin(DENSE)
+    passed(QKV, 0)
+    begin(UP)
+    begin(DOWN)
+    passed(DENSE, 0)
+    arrived(QKV, 1)
+    arrived(DENSE, 1)
+    passed(QKV, 1)
+    passed(DENSE, 1)
+    passed(UP, 0)
+    passed(DOWN, 0)
+    token_spread(0)
+    arrived(QKV, 2)
+    arrived(DENSE, 2)
     token_start(1)
-    token_spread(0)
-    for w in range(N_W):
-        passed(w, 0)
-        for k in range(1, 4):
-            arrived(w, k)
-        for k in range(1, 4):
-            passed(w, k)
-    token_spread(1)
-    for w in range(N_W):
-        for k in range(4):
-            finished(w, k)
-            drained(w, k)
-        home(w).wait()
+    token_finish(0)
     small_home.wait()
     for step in range(1, ROWS * DPS):
         small_copy(step).wait()
+    read_gains(smalls, gains)
+    if aligned:
+        read_bias(smalls, bias_row, 9, bias_row.shape[1] // DPS)
+    else:
+        bias_row[...] = bias_in[...]
+    norm_stage(x_ref, gains, 0, first, first_t)
+    passed(QKV, 2)
+    passed(DENSE, 2)
+    arrived(QKV, 3)
+    arrived(DENSE, 3)
+    passed(QKV, 3)
+    passed(DENSE, 3)
+    arrived(UP, 1)
+    arrived(DOWN, 1)
+    home(QKV).wait()
+    finished(QKV)
+    keep_x = pltpu.make_async_copy(x_ref, x_out, l_sem.at[N_W])
+    keep_wq = pltpu.make_async_copy(wq, gq_ref, l_sem.at[QKV])
+    keep_x.start()
+    keep_wq.start()
+    project_stage(wq, first, bias_row, angles, q_t, k_t, v_t, k_n, v_n, heads)
+    passed(UP, 1)
+    passed(DOWN, 1)
+    token_spread(1)
+    arrived(UP, 2)
+    home(DENSE).wait()
+    finished(DENSE)
+    token_finish(1)
+    keep_c = pltpu.make_async_copy(c_ref, c_out, l_sem.at[N_W + 1])
+    keep_wd = pltpu.make_async_copy(wd, gd_ref, l_sem.at[DENSE])
+    keep_smalls = pltpu.make_async_copy(smalls, smalls_out, l_sem.at[N_W + 2])
+    keep_c.start()
+    keep_wd.start()
+    keep_smalls.start()
+    upstream_stage(wd, c_ref, up_t, heads)
+    prefix = prefix_ref[0]
+
+    services = [
+        lambda: arrived(DOWN, 2),
+        lambda: passed(UP, 2),
+        lambda: passed(DOWN, 2),
+        lambda: arrived(UP, 3),
+        lambda: arrived(DOWN, 3),
+        lambda: passed(UP, 3),
+        lambda: passed(DOWN, 3),
+    ]
+
+    def head_body(h, carry):
+        for n, service in enumerate(services):
+            if n < heads - 1:
+                pl.when(h == n)(service)
+        attend_head(h, prefix, angles, q_t, k_t, v_t, k_n, v_n, up_t, att_t, gm_t, grad_q, grad_k, grad_v)
+        return carry
+
+    lax.fori_loop(0, heads, head_body, 0)
+    for service in services[max(heads - 1, 0) :]:
+        service()
+
+    width = gm_t.shape[0]
+    wide = min(512, width)
+
+    def qkv_body(i, carry):
+        rows = span(i * 256, 256, 256)
+        for n in range(width // wide):
+            wgq_ref[rows, n * wide : (n + 1) * wide] = nt(first_t[rows, :], gm_t[n * wide : (n + 1) * wide, :]).astype(BF)
+        return carry
+
+    lax.fori_loop(0, D // 256, qkv_body, 0)
+    group = min(heads, 4)
+
+    def dense_body(i, carry):
+        block = att_t[pl.ds(i * group, group)].reshape(group * HD, SEQ_LEN)
+        spot = pl.ds(0, group * HD) if heads == group else span(i * group * HD, group * HD, 128)
+        wgd_ref[spot, :] = nn(block, c_ref[...]).astype(BF)
+        att_ref[:, spot] = block.T
+        return carry
+
+    lax.fori_loop(0, heads // group, dense_body, 0)
+    pair = min(heads, 2) * 192
+
+    def turn_body(p, carry):
+        spot = pl.ds(0, pair) if pair == width else span(p * pair, pair, 128)
+        value = gm_t[spot, :].T
+        gm_ref[:, spot] = value
+        gb_ref[0:1, spot] = jnp.sum(value.astype(F32), axis=0, keepdims=True)
+        return carry
+
+    lax.fori_loop(0, width // pair, turn_body, 0)
+
+    for w in (UP, DOWN):
+        finished(w)
+        home(w).wait()
+    for w in range(N_W):
+        for k in range(ROWS):
+            drained(w, k)
     for kind in range(2):
-        token_finish(kind)
-
-
-def gather(tokens_in, cotangent, small, weights, cols):
+        token_drain(kind)
+    for keep in (keep_x, keep_wq, keep_c, keep_wd, keep_smalls):
+        keep.wait()
+
+
+def gather(prefix_len, tokens_in, cotangent, small, angles, bias, weights, cols, aligned):
     wq, wu, wd, wp = weights
+    n_q, n_u = wq.shape[1], wu.shape[1]
+    heads = n_q // 192
+    width = heads * HD
     any_spec = pl.BlockSpec(memory_space=pl.ANY)
-    shapes = [
-        jax.ShapeDtypeStruct((SEQ_LEN, D), BF),
-        jax.ShapeDtypeStruct((SEQ_LEN, D), BF),
-        jax.ShapeDtypeStruct((ROWS * DPS,) + small.shape, F32),
-        jax.ShapeDtypeStruct((ROWS, DPS) + wq.shape, BF),
-        jax.ShapeDtypeStruct((ROWS, DPS) + wu.shape, BF),
-        jax.ShapeDtypeStruct((DPS,) + wd.shape[:2] + (D,), BF),
-        jax.ShapeDtypeStruct((DPS,) + wp.shape[:2] + (D,), BF),
+    vmem = pl.BlockSpec(memory_space=pltpu.VMEM)
+    smem = pl.BlockSpec(memory_space=pltpu.SMEM)
+    shape = jax.ShapeDtypeStruct
+    smalls = (ROWS * DPS,) + small.shape
+    out_shape = [
+        shape((SEQ_LEN, D), BF), shape((SEQ_LEN, D), BF), shape(smalls, F32),
+        shape((D, n_q), BF), shape((D, n_u), BF), shape((width, D), BF), shape((wp.shape[0] * DPS, D), BF),
+        shape((D, n_q), BF), shape((width, D), BF), shape((SEQ_LEN, n_q), BF), shape((SEQ_LEN, width), BF),
+        shape((1, n_q), F32),
     ]
     tok_col = tokens_in.shape[0]
     pieces = tok_col // (SEQ_LEN // cols)
     dma = pltpu.SemaphoreType.DMA
+    buf = pltpu.VMEM
+    turned = buf((heads, HD, SEQ_LEN), BF)
+    plain = buf((heads, SEQ_LEN, HD), BF)
+    scratch = [buf(w.shape, BF) for w in weights] + [buf(w.shape, F32) for w in weights]
+    scratch += [
+        buf((SEQ_LEN, D), BF), buf((SEQ_LEN, D), BF), buf(smalls, F32), buf((D, n_q), BF), buf((width, D), BF),
+        buf((8, D), F32), buf((1, n_q), F32), buf((SEQ_LEN, D), BF), buf((D, SEQ_LEN), BF),
+        turned, turned, turned, plain, plain, turned, turned, buf((n_q, SEQ_LEN), BF),
+        buf((HD, SEQ_LEN), F32), buf((HD, SEQ_LEN), F32), buf((HD, SEQ_LEN), F32),
+        dma((N_W, 5)), dma((N_W, 4)), dma((N_W, 4, 2)), dma((N_W, 4, 2)), dma((N_W, 4, 2, 2)), dma((N_W, 4, 2, 2)),
+        dma((2, pieces)), dma((2, 4)), dma((2, cols - 1)), dma((2, cols - 1)),
+        dma((ROWS * DPS - 1,)), dma((ROWS * DPS - 1,)), dma((N_W + 3,)),
+    ]
     return pl.pallas_call(
-        functools.partial(gather_kernel, cols),
-        out_shape=shapes,
-        in_specs=[any_spec] * 7,
-        out_specs=[any_spec] * 7,
-        scratch_shapes=[
-            dma((N_W, 5)), dma((N_W, 4)), dma((N_W, 4, 2)), dma((N_W, 4, 2)), dma((N_W, 4, 2, 2)), dma((N_W, 4, 2, 2)),
-            dma((2, pieces)), dma((2, 4)), dma((2, cols - 1)), dma((2, cols - 1)),
-            dma((ROWS * DPS - 1,)), dma((ROWS * DPS - 1,)), dma((N_W + 1,)),
-        ],
-        compiler_params=pltpu.CompilerParams(collective_id=0, has_side_effects=True),
-    )(tokens_in, cotangent, small, wq, wu, wd, wp)
+        functools.partial(gather_kernel, cols, aligned),
+        out_shape=out_shape,
+        in_specs=[smem, any_spec, any_spec, any_spec, vmem, vmem] + [any_spec] * 4,
+        out_specs=[any_spec] * 7 + [vmem] * 5,
+        scratch_shapes=scratch,
+        compiler_params=pltpu.CompilerParams(collective_id=0, has_side_effects=True, vmem_limit_bytes=60 << 20),
+    )(prefix_len, tokens_in, cotangent, small, angles, bias, wq, wu, wd, wp)
 
 
 def lead(name, y, x, half):
@@ -364,10 +625,14 @@
 
         lax.fori_loop(0, height // step, body, 0)
 
-    sequence = [(w, half) for w in (0, 1, 2, 3) for half in range(2)]
-    for w, half in sequence:
+    sequence = [(w, half) for w in (2, 0, 1, 3) for half in range(2)]
+
+    def begin(w, half):
         first(w, half).start()
         fetch(w, half).start()
+
+    for w, half in sequence[:4]:
+        begin(w, half)
 
     def stage_two(w, half):
         fetch(w, half).wait()
@@ -391,6 +656,8 @@
     for i in range(n + lag3):
         if i < n:
             stage_two(*sequence[i])
+            if i + 4 < n:
+                begin(*sequence[i + 4])
         if 0 <= i - lag2 < n:
             stage_three(*sequence[i - lag2])
         if 0 <= i - lag3 < n:
@@ -438,51 +705,6 @@
     return (jnp.cos(turned), jnp.sin(turned))
 
 
-def rotate(paired, cos_table, sin_table):
-    half_rot = cos_table.shape[1]
-    cos_wide = cos_table[:, None, None, :]
-    sin_wide = sin_table[:, None, None, :]
-    first_half = paired[..., :half_rot]
-    second_half = paired[..., half_rot : 2 * half_rot]
-    return jnp.concatenate(
-        [
-            first_half * cos_wide - second_half * sin_wide,
-            second_half * cos_wide + first_half * sin_wide,
-            paired[..., 2 * half_rot :],
-        ],
-        axis=-1,
-    )
-
-
-def score_block(queries, key_rows, prefix_end):
-    scores = jnp.einsum("qhd,khd->hqk", queries, key_rows, preferred_element_type=F32) * HD ** (-0.5)
-    at = jnp.arange(SEQ_LEN)
-    visible = (at[None, :] <= at[:, None]) | (at[None, :] < prefix_end)
-    return jnp.where(visible[None], scores, NEGATIVE)
-
-
-def attend_forward(queries, key_rows, value_rows, prefix_end):
-    scores = score_block(queries, key_rows, prefix_end)
-    highest = jnp.max(scores, axis=-1, keepdims=True)
-    exp_total = jnp.sum(jnp.exp(scores - highest), axis=-1, keepdims=True)
-    log_sum = highest + jnp.log(exp_total)
-    weights = jnp.exp(scores - log_sum).astype(BF)
-    outputs = jnp.einsum("hqk,khd->qhd", weights, value_rows, preferred_element_type=F32)
-    return (outputs, log_sum[..., 0])
-
-
-def attend_backward(queries, key_rows, value_rows, prefix_end, log_sum, upstream):
-    scores = score_block(queries, key_rows, prefix_end)
-    chances = jnp.exp(scores - log_sum[..., None])
-    grad_values = jnp.einsum("hqk,qhd->khd", chances.astype(BF), upstream, preferred_element_type=F32)
-    grad_chances = jnp.einsum("qhd,khd->hqk", upstream, value_rows, preferred_element_type=F32)
-    inner_sum = jnp.sum(chances * grad_chances, axis=-1, keepdims=True)
-    grad_scores = (chances * (grad_chances - inner_sum)).astype(BF)
-    grad_queries = jnp.einsum("hqk,khd->qhd", grad_scores, key_rows, preferred_element_type=F32) * HD ** (-0.5)
-    grad_keys = jnp.einsum("hqk,qhd->khd", grad_scores, queries, preferred_element_type=F32) * HD ** (-0.5)
-    return (grad_queries, grad_keys, grad_values)
-
-
 def contract_rows(left_side, right_side):
     return lax.dot_general(left_side, right_side, (((0,), (0,)), ((), ())), preferred_element_type=F32)
 
@@ -499,61 +721,46 @@
     heads = n_q // (3 * HD)
     width_att = heads * HD
 
-    weights = (
-        qkv_weight.astype(BF).reshape(2, 32, n_q),
-        up_weight.astype(BF).reshape(2, 32, n_u),
-        dense_weight.astype(BF).reshape(2, h_d // 2, 256),
-        down_weight.astype(BF).reshape(2, h_p // 2, 256),
-    )
-    pieces = (first_gain, first_shift, second_gain, second_shift, dense_bias, down_bias, qkv_bias, up_bias)
-    small = jnp.concatenate(pieces)
+    out_part = dense_bias.astype(BF).astype(F32) + down_bias.astype(BF).astype(F32)
+    q_part, u_part = qkv_bias.astype(BF).astype(F32), up_bias.astype(BF).astype(F32)
+    n_qb, n_ub = q_part.shape[0], u_part.shape[0]
+    aligned = n_qb % 128 == 0 and n_ub % 128 == 0
+    small = jnp.concatenate((first_gain, first_shift, second_gain, second_shift, out_part, out_part, q_part, u_part))
     size = -(-small.shape[0] // 1024) * 1024
     small = jnp.pad(small, (0, size - small.shape[0])).reshape(size // 128, 128)
-    own_x, own_cot, smalls, wq, wu, wd, wp = gather(tokens_in, cotangent, small, weights, cols)
-    wq = wq.reshape(D, n_q)
-    wu = wu.reshape(D, n_u)
-    wd = wd.reshape(width_att, D)
-    wp = wp.reshape(h_p * DPS, D)
+    if aligned:
+        q_bias = jnp.zeros((1, n_q), F32)
+    else:
+        q_bias = lax.all_gather(q_part, "dp", axis=0, tiled=True).reshape(1, n_q)
+    cos_table, sin_table = angles_table()
+    angles = jnp.concatenate([cos_table.T, sin_table.T], axis=0)
+    own_x, own_cot, smalls, wq, wu, wd, wp, wgrad_q, wgrad_d, grad_mixed, attended, sum_q = gather(
+        prefix_len, tokens_in, cotangent, small, angles, q_bias, (qkv_weight, up_weight, dense_weight, down_weight), cols,
+        aligned
+    )
     flat = smalls.reshape(ROWS, DPS, size)
     gains = [flat[:, 0, 256 * i : 256 * (i + 1)].reshape(D) for i in range(4)]
-    out_bias = [flat[:, :, 1024 + 64 * i : 1088 + 64 * i].reshape(D).astype(BF).astype(F32) for i in range(2)]
-    n_qb, n_ub = qkv_bias.shape[0], up_bias.shape[0]
-    q_bias = flat[0, :, 1152 : 1152 + n_qb].reshape(n_q).astype(BF).astype(F32)
-    u_bias = flat[0, :, 1152 + n_qb : 1152 + n_qb + n_ub].reshape(n_u).astype(BF).astype(F32)
+    out_bias = flat[:, :, 1024:1088].reshape(D)
+    u_bias = flat[0, :, 1152 + n_qb : 1152 + n_qb + n_ub].reshape(n_u)
 
     wide = own_x.astype(F32)
     center = jnp.mean(wide, axis=1, keepdims=True)
     spread = jnp.mean(wide * wide, axis=1, keepdims=True) - center * center
     scale_inv = lax.rsqrt(spread + EPS)
     normed = (wide - center) * scale_inv
-    first_in = (normed * gains[0] + gains[1]).astype(BF)
     second_in = (normed * gains[2] + gains[3]).astype(BF)
 
-    mixed = jnp.dot(first_in, wq, preferred_element_type=F32) + q_bias
     hidden_pre = jnp.dot(second_in, wu, preferred_element_type=F32) + u_bias
-    mixed_heads = mixed.reshape(SEQ_LEN, heads, 3, HD)
-    cos_table, sin_table = angles_table()
-    turned = rotate(mixed_heads[:, :, :2, :], cos_table, sin_table).astype(BF)
-    queries, key_rows = turned[:, :, 0, :], turned[:, :, 1, :]
-    value_rows = mixed_heads[:, :, 2, :].astype(BF)
-    outputs, log_sums = attend_forward(queries, key_rows, value_rows, prefix_len[0])
-    attended = outputs.reshape(SEQ_LEN, width_att).astype(BF)
     hidden = jax.nn.gelu(hidden_pre, approximate=False).astype(BF)
     branch = jnp.dot(attended, wd, preferred_element_type=F32) + jnp.dot(hidden, wp, preferred_element_type=F32)
-
-    upstream = contract_cols(own_cot, wd).astype(BF).reshape(SEQ_LEN, heads, HD)
     grad_hidden = contract_cols(own_cot, wp)
     ignored, gelu_back = jax.vjp(functools.partial(jax.nn.gelu, approximate=False), hidden_pre)
     grad_hidden_pre = gelu_back(grad_hidden)[0].astype(BF)
-    grad_q, grad_k, grad_v = attend_backward(queries, key_rows, value_rows, prefix_len[0], log_sums, upstream)
-    ignored, rotate_back = jax.vjp(lambda paired: rotate(paired, cos_table, sin_table), mixed_heads[:, :, :2, :])
-    grad_pair = rotate_back(jnp.stack([grad_q, grad_k], axis=2))[0]
-    grad_mixed = jnp.concatenate([grad_pair, grad_v[:, :, None, :]], axis=2).reshape(SEQ_LEN, n_q).astype(BF)
 
     grads = (
-        contract_rows(first_in, grad_mixed).astype(BF).reshape(ROWS, 2, 2, 2, 32, n_q),
+        wgrad_q.reshape(ROWS, 2, 2, 2, 32, n_q),
         contract_rows(second_in, grad_hidden_pre).astype(BF).reshape(ROWS, 2, 2, 2, 32, n_u),
-        contract_rows(attended, own_cot).astype(BF).reshape(2, 2, 2, h_d // 2, D),
+        wgrad_d.reshape(2, 2, 2, h_d // 2, D),
         contract_rows(hidden, own_cot).astype(BF).reshape(2, 2, 2, h_p // 2, D),
     )
     out_q, out_u, out_d, out_p = scatter(grads, cols)
@@ -579,15 +786,15 @@
     grad_tokens = lax.all_to_all(grad_tokens, "row", split_axis=1, concat_axis=0, tiled=True)
     grad_tokens = lax.dynamic_slice_in_dim(grad_tokens, lax.axis_index("col") * tok_col, tok_col, 0)
     row = lax.axis_index("row")
-    here = [lax.dynamic_slice_in_dim(b, row * 256, 256, 0) for b in out_bias]
-    layer_out = (tokens_in.astype(F32) + branch_sum + here[0] + here[1]).astype(BF)
+    here = lax.dynamic_slice_in_dim(out_bias, row * 256, 256, 0)
+    layer_out = (tokens_in.astype(F32) + branch_sum + here).astype(BF)
 
     gain_sums = lax.psum_scatter(
         lax.psum(gain_rows, ("dp", "col")), "row", scatter_dimension=1, tiled=True
     )
     out_b = lax.psum_scatter(jnp.sum(own_cot.astype(F32), axis=0), ("row", "dp"), scatter_dimension=0, tiled=True)
     q_b = lax.psum_scatter(
-        lax.psum(jnp.sum(grad_mixed.astype(F32), axis=0), "row"), "dp", scatter_dimension=0, tiled=True
+        lax.psum(sum_q[0], "row"), "dp", scatter_dimension=0, tiled=True
     )
     u_b = lax.psum_scatter(
         lax.psum(jnp.sum(grad_hidden_pre.astype(F32), axis=0), "row"), "dp", scatter_dimension=0, tiled=True

time: 735 us -> 598 us (0.81)
  matrix products: 178 us -> 72.9 us
  other arithmetic: 83.7 us -> 25.6 us
  waiting for transfers between devices: 29 us -> 80.8 us
  local copies, waits for them, and re-layouts: 35.9 us -> 19.8 us
  Pallas kernels: 298 us -> 287 us
    dot_general x7 -> x0, matrix products: 99.5 us -> none  [the longest x1 24 us: attend_backward(): jnp.einsum('qhd,khd->hqk', upstream, value_rows, preferred_element_type=F32)]
    all_to_all x1, waiting for transfers between devices: 0.01 us -> 52.2 us  [to_owner(): lax.all_to_all(partial, 'row', split_axis=1, concat_axis=0, tiled=True)]
    convert_element_type x8 -> x3, other arithmetic: 39.2 us -> 4.2 us  [the longest x1 2.83 us: shards(): layer_out = (tokens_in.astype(F32) + branch_sum + here).astype(BF)]
    reduce_sum x2 -> x0, other arithmetic: 14.7 us -> none  [the longest x1 14.2 us: attend_forward(): exp_total = jnp.sum(jnp.exp(scores - highest), axis=-1, keepdims=True)]
    pallas_call x1, Pallas kernels: 150 us -> 140 us  [scatter(): pl.pallas_call(functools.partial(scatter_kernel, cols, None), out_shape=o...]
    dot_general x4 -> x2, matrix products: 22.6 us -> 16.1 us  [contract_rows(): lax.dot_general(left_side, right_side, (((0,), (0,)), ((), ())), preferre...]
    dot_general x4 -> x3, matrix products: 38.5 us -> 38.1 us  [contract_cols(): lax.dot_general(left_side, right_side, (((1,), (1,)), ((), ())), preferre...]
  transfers between devices with their start and end apart: 5 -> 5, of which waited for: 1 -> 2; matrix products, arithmetic and copies ran while one was open for 21% -> 9% of each run, Pallas kernels for 20% -> 24%
where the time goes in v2:
time: 598 us; the launch traced here: 590 us
  Pallas kernels  287 us (48%)
  waiting for transfers between devices  80.8 us (14%)
  blocking collectives  76.5 us (13%)
  matrix products  72.9 us (12%)
  other arithmetic  25.6 us (4%)
  local copies, waits for them, and re-layouts  19.8 us (3%)
  between operations  17.2 us (3%)
  starting transfers between devices  10.2 us (2%)
    pallas_call x1, Pallas kernels, gather(): pl.pallas_call(functools.partial(gather_kernel, cols, aligned), out_shape...  147 us
    pallas_call x1, Pallas kernels, scatter(): pl.pallas_call(functools.partial(scatter_kernel, cols, None), out_shape=o...  140 us
    all_to_all x1, waiting for transfers between devices, to_owner(): lax.all_to_all(partial, 'row', split_axis=1, concat_axis=0, tiled=True)  52.2 us
    unnamed x2, blocking collectives  51.5 us
    dot_general x3, matrix products, contract_cols(): lax.dot_general(left_side, right_side, (((1,), (1,)), ((), ())), preferre...  38.1 us
    psum x1, waiting for transfers between devices, shards(): combined = lax.psum(combined, 'col')  28.6 us
    dot_general x2, matrix products, contract_rows(): lax.dot_general(left_side, right_side, (((0,), (0,)), ((), ())), preferre...  16.1 us
    psum x1, blocking collectives, shards(): lax.psum(sum_q[0], 'row')  13.2 us
  transfers between devices with their start and end apart: 5, of which 2 were waited for; matrix products, arithmetic and copies ran while one was open for 9% of the time, Pallas kernels for 24%

profile of v2, /device:TPU:0, one launch (start us, length us, event | category | flops | bytes accessed | tf_op | source)
XLA Modules:
  0.0 589.6 jit_solution(11572244057475463639)
XLA Ops:
  7.8 0.7 convert_convert_fusion.1
  8.5 0.7 convert_convert_fusion
  9.2 0.2 fusion.22
  9.4 0.7 convert_add_fusion.1
  10.1 0.6 pad_maximum_fusion.refs_4_
  10.7 1.4 concatenate.6
  12.1 0.6 broadcast_in_dim.2.refs_5_
  12.7 146.7 %shard_map.254 = (bf16[1024,1024]{1,0:T(8,128)(2,1)}, bf16[1024,1024]{1,0:T(8,128)(2,1)}, f32[16,16,128]{2,1,0:T(8,128)}, bf16[1024,1536]{1,0:T(8,128)(2,1)}, bf...) custom-call(s32[1]{0:T(128)S(6)} %copy.45.refs_0_, ...), custom_call_target="tpu_custom_call" | custom-call | tf_op jit(solution)/shard_map/pallas_call | solution.py:535
  159.4 0.9 reshape.104
  160.4 2.3 convert_reduce_fusion.1
  162.7 7.4 %fusion.24 = f32[1024,2048]{1,0:T(8,128)S(1)} fusion(bf16[1024,2048]{1,0:T(8,128)(2,1)} %get-tuple-element.34, bf16[1024,1024]{1,0:T(8,128)(2,1)} %get-tuple-element.32, f32[1024]{0:T(1024)S(1)} %bitcast.72, f32[1024]{0:T(1024)S(1)} %bitcast.74, f32[1024]{0:T(1024)S(1)} %get-tuple-element.75, f32[1024]{0:T(1024)S(1)} %get-tuple-element.74), kind=kOutput, calls=%fused_computation.59 | convolution fusion | flops 4301258752 | bytes 14696448 | tf_op jit(solution)/shard_map/dot_general | solution.py:753
  170.1 0.0 copy-start.3
  170.1 0.0 copy-done.7
  170.1 0.0 copy-done.12
  170.1 24.9 %convert_reduce_fusion = (f32[2048]{0:T(1024)S(1)}, bf16[1024,2048]{1,0:T(8,128)(2,1)}, f32[1024,2048]{1,0:T(8,128)}) fusion(f32[1024,2048]{1,0:T(8,128)S(1)} %fusion.24, f32[2048]{0:T(1024)S(1)} %bitcast.66, bf16[1024,1024]{1,0:T(8,128)(2,1)S(1)} %copy-done.7, bf16[2048,1024]{1,0:T(8,128)(2,1)S(1)} %copy-done.12), kind=kOutput, calls=%fused_computation.2 | convolution fusion | flops 4452251648 | bytes 27279360 | tf_op jit(solution)/shard_map/dot_general | solution.py:713
  195.1 8.0 %multiply_convert_fusion = bf16[1024,2048]{1,0:T(8,128)(2,1)S(1)} fusion(f32[1024,2048]{1,0:T(8,128)} %get-tuple-element.64, f32[1024,2048]{1,0:T(8,128)} %copy-done.3, f32[2048]{0:T(1024)S(1)} %bitcast.67), kind=kLoop, calls=%fused_computation.4 | loop fusion | flops 8388608 | bytes 20979712 | tf_op jit(solution)/shard_map/convert_element_type | solution.py:754
  203.1 0.0 copy-start.4
  203.1 0.0 copy-start.8
  203.1 0.0 copy-start.9
  203.1 8.0 %fusion.30 = f32[1024,1024]{0,1:T(8,128)S(1)} fusion(bf16[1024,2048]{1,0:T(8,128)(2,1)S(1)} %multiply_convert_fusion, bf16[2048,1024]{1,0:T(8,128)(2,1)} %get-tuple-element.35), kind=kOutput, calls=%fused_computation.63 | convolution fusion | flops 4294967296 | bytes 12582912 | tf_op jit(solution)/shard_map/dot_general | solution.py:755
  211.2 3.3 convolution_add_fusion
  214.4 4.9 all-to-all-start
  219.4 0.3 all-reduce.7.cloned.1.call-start
  219.7 6.4 %fusion.31 = f32[1024,1024]{1,0:T(8,128)S(1)} fusion(bf16[1024,1536]{1,0:T(8,128)(2,1)} %get-tuple-element.37, bf16[1024,1536]{1,0:T(8,128)(2,1)} %get-tuple-element.38), kind=kOutput, calls=%fused_computation.64 | convolution fusion | flops 3221225472 | bytes 10485760 | tf_op jit(solution)/shard_map/dot_general | solution.py:713
  226.1 6.8 %multiply_add_fusion = (f32[1024,1024]{1,0:T(8,128)}, f32[1024,1024]{1,0:T(8,128)}) fusion(f32[1024,1024]{1,0:T(8,128)S(1)} %fusion.31, f32[1024]{0:T(1024)S(1)} %bitcast.77, f32[1024]{0:T(1024)S(1)} %bitcast.75, bf16[1024,2048]{1,0:T(8,128)(2,1)S(1)} %copy-done.16, bf16[1024,2048]{1,0:T(8,128)(2,1)S(1)} %copy-done.11), kind=kOutput, calls=%fused_computation.38 | convolution fusion | flops 4298113024 | bytes 20979712 | tf_op jit(solution)/shard_map/dot_general | solution.py:713
  232.9 0.0 all-reduce.7.cloned.1.call-update
  232.9 0.0 reduce-scatter.7.cloned.1.call-start
  233.0 28.6 %all-reduce.7.cloned.1.call-done = f32[1024,1024]{1,0:T(8,128)} async-done(((f32[1024,1024]{1,0:T(8,128)}), f32[1024,1024]{1,0:T(8,128)}) %all-reduce.7.cloned.1.call-update) | async-done | bytes 4194320 | tf_op jit(solution)/shard_map/psum | solution.py:778
  261.6 5.7 fusion.26
  267.3 1.0 copy.33
  268.4 0.0 reduce-scatter.7.cloned.1.call-update
  268.4 0.0 reduce-scatter.5.cloned.1.call-start
  268.4 52.2 %all-to-all-done = f32[1024,4,256]{0,2,1:T(8,128)} async-done(((f32[1024,4,256]{0,2,1:T(8,128)}), f32[1024,4,256]{0,2,1:T(8,128)}, u32[]{:S(2)}, u32[]{:S(2)}) %all-to-all-start) | async-done | bytes 4194336 | tf_op jit(solution)/shard_map/all_to_all | solution.py:774
  320.6 5.4 copy.31
  326.0 0.0 reduce-scatter.5.cloned.1.call-update
  326.0 3.8 convert_reduce_fusion.2
  329.9 0.0 copy-start.14
  329.9 0.0 copy-start.13
  329.9 1.5 copy.38
  331.4 4.9 all-to-all-start.1
  336.3 0.6 dynamic-slice.4
  336.9 0.6 dynamic-slice
  338.8 0.1 reshape.105
  338.8 9.5 %convolution_convert_fusion = bf16[2048,1024]{1,0:T(8,128)(2,1)} fusion(bf16[1024,2048]{1,0:T(8,128)(2,1)} %copy-done.4, bf16[1024,1024]{1,0:T(8,128)(2,1)} %get-tuple-element.36), kind=kOutput, calls=%fused_computation.39 | convolution fusion | flops 4297064448 | bytes 10485760 | tf_op jit(solution)/shard_map/dot_general | solution.py:709
  348.4 6.5 %convolution_convert_fusion.1 = bf16[1024,2048]{1,0:T(8,128)(2,1)} fusion(bf16[1024,2048]{1,0:T(8,128)(2,1)S(1)} %copy-done.17, bf16[1024,1024]{1,0:T(8,128)(2,1)S(1)} %copy-done.2, f32[1024]{0:T(1024)S(1)} %bitcast.73, f32[1024]{0:T(1024)S(1)} %bitcast.76, f32[1024]{0:T(1024)S(1)} %get-tuple-element.75, f32[1024]{0:T(1024)S(1)} %get-tuple-element.74), kind=kOutput, calls=%fused_computation.40 | convolution fusion | flops 4303355904 | bytes 10502144 | tf_op jit(solution)/shard_map/dot_general | solution.py:709
  354.9 140.0 %shard_map.255 = (f32[2,32,1536]{2,1,0:T(8,128)S(1)}, f32[2,32,2048]{2,1,0:T(8,128)S(1)}, f32[2,64,256]{2,1,0:T(8,128)S(1)}, f32[2,256,256]{2,1,0:T(8,128)S(1)}) custom-call(bf16[4,2,2,2,32,1536]{5,4,3,2,1,0:T(8,128)(2,1)S(1)} %bitcast.51, bf16[4,2,2,2,32,2048]{5,4,3,2,1,0:T(8,128)(2,1)} %bitcast.62, bf16[2,2,2,64,1024]{4,3,2,1,0:T(8,128)(2,1)S(1)} %bitcast.52, ...), custom_call_target="tpu_custom_call" | custom-call | tf_op jit(solution)/shard_map/pallas_call | solution.py:688
  495.6 0.1 dynamic_slice.6
  495.7 15.0 %all-reduce.4 = (f32[1536]{0:T(1024)S(1)}, f32[2048]{0:T(1024)S(1)}) all-reduce(f32[1536]{0:T(1024)S(1)} %reduce, f32[2048]{0:T(1024)S(1)} %get-tuple-element.62), channel_id=3, replica_groups=mesh['dp'=4,'row'=4,'col'=2] {'dp'}, use_global_device_ids=true, to_apply=%region_7.8.clone | all-reduce | flops 3584 | bytes 28672
  510.7 0.1 dynamic-slice.1
  510.7 0.1 dynamic-slice.3
  510.8 13.2 %all-reduce.3 = (f32[384]{0:T(512)}, f32[512]{0:T(512)}) all-reduce(f32[384]{0:T(512)S(1)} %dynamic-slice.1, f32[512]{0:T(512)S(1)} %dynamic-slice.3), channel_id=1, replica_groups=mesh['dp'=4,'row'=4,'col'=2] {'row'}, use_global_device_ids=true, to_apply=%region_6.7 | all-reduce | flops 896 | bytes 7168 | tf_op jit(solution)/shard_map/psum | solution.py:797
  524.0 36.5 %all-reduce.2 = f32[1024]{0:T(1024)S(1)} all-reduce(f32[1024]{0:T(1024)S(1)} %get-tuple-element.65), channel_id=5, replica_groups=mesh['dp'=4,'row'=4,'col'=2] {'row','dp'}, use_global_device_ids=true, to_apply=%region_12.13.clone | all-reduce | flops 1024 | bytes 8192
  560.6 0.1 dynamic-slice.5
  560.6 1.0 copy.34
  561.6 11.8 %psum.34 = f32[4,256]{1,0:T(4,128)S(1)} all-reduce(f32[4,256]{1,0:T(4,128)S(1)} %copy.34), channel_id=1, replica_groups=mesh['dp'=4,'row'=4,'col'=2] {'dp','col'}, use_global_device_ids=true, to_apply=%region_17.18 | all-reduce | flops 1024 | bytes 8192 | tf_op jit(solution)/shard_map/psum | solution.py:793
  573.4 0.6 fusion.29
  574.0 0.0 all-to-all-done.1
  574.0 2.3 constant_dynamic-slice_fusion
  576.3 2.8 add_convert_fusion.1
  579.1 0.5 copy.46
  579.6 0.7 copy.47
  580.3 0.8 copy.48
  581.1 0.7 copy.49
  581.8 0.8 copy.50
  (39 shorter events, 0.1 us)
Async XLA Ops:
  162.7 7.4 %copy-start.7 = (bf16[1024,1024]{1,0:T(8,128)(2,1)S(1)}, bf16[1024,1024]{1,0:T(8,128)(2,1)}, u32[]{:S(2)}) copy-start(bf16[1024,1024]{1,0:T(8,128)(2,1)} %get-tuple-element.36) | copy-start | bytes 6291460
  162.7 7.4 %copy-start.12 = (bf16[2048,1024]{1,0:T(8,128)(2,1)S(1)}, bf16[2048,1024]{1,0:T(8,128)(2,1)}, u32[]{:S(2)}) copy-start(bf16[2048,1024]{1,0:T(8,128)(2,1)} %get-tuple-element.35) | copy-start | bytes 12582916
  170.1 25.0 %copy-start.3 = (f32[1024,2048]{1,0:T(8,128)}, f32[1024,2048]{1,0:T(8,128)S(1)}, u32[]{:S(2)}) copy-start(f32[1024,2048]{1,0:T(8,128)S(1)} %fusion.24) | copy-start | bytes 25165828
  203.1 8.0 %copy-start.4 = (bf16[1024,2048]{1,0:T(8,128)(2,1)}, bf16[1024,2048]{1,0:T(8,128)(2,1)S(1)}, u32[]{:S(2)}) copy-start(bf16[1024,2048]{1,0:T(8,128)(2,1)S(1)} %multiply_convert_fusion) | copy-start | bytes 12582916
  203.1 8.0 %copy-start.8 = (bf16[512,1024]{1,0:T(8,128)(2,1)S(1)}, bf16[512,1024]{1,0:T(8,128)(2,1)}, u32[]{:S(2)}) copy-start(bf16[512,1024]{1,0:T(8,128)(2,1)} %get-tuple-element.31) | copy-start | bytes 3145732
  203.1 8.0 %copy-start.9 = (bf16[1024,512]{1,0:T(8,128)(2,1)S(1)}, bf16[1024,512]{1,0:T(8,128)(2,1)}, u32[]{:S(2)}) copy-start(bf16[1024,512]{1,0:T(8,128)(2,1)} %get-tuple-element.30) | copy-start | bytes 3145732
  214.4 106.2 %all-to-all-start = ((f32[1024,4,256]{0,2,1:T(8,128)}), f32[1024,4,256]{0,2,1:T(8,128)}, u32[]{:S(2)}, u32[]{:S(2)}) async-start(f32[1024,4,256]{0,2,1:T(8,128)} %bitcast.58), calls=%async_computation | async-start | bytes 8388608 | tf_op jit(solution)/shard_map/all_to_all | solution.py:774
  219.4 42.2 %all-reduce.7.cloned.1.call-start = ((), (), s32[]{:S(2)}) async-start(), calls=%async_computation.5 | async-start | bytes 8388608 | tf_op jit(solution)/shard_map/psum | solution.py:778
  219.6 6.5 %copy-start.11 = (bf16[1024,2048]{1,0:T(8,128)(2,1)S(1)}, bf16[1024,2048]{1,0:T(8,128)(2,1)}, u32[]{:S(2)}) copy-start(bf16[1024,2048]{1,0:T(8,128)(2,1)} %get-tuple-element.34) | copy-start | bytes 12582916
  219.6 6.5 %copy-start.16 = (bf16[1024,2048]{1,0:T(8,128)(2,1)S(1)}, bf16[1024,2048]{1,0:T(8,128)(2,1)}, u32[]{:S(2)}) copy-start(bf16[1024,2048]{1,0:T(8,128)(2,1)} %get-tuple-element.63) | copy-start | bytes 12582916
  226.1 6.8 %copy-start.5 = (f32[1024,1024]{1,0:T(8,128)}, f32[1024,1024]{1,0:T(8,128)S(1)}, u32[]{:S(2)}) copy-start(f32[1024,1024]{1,0:T(8,128)S(1)} %fusion.31) | copy-start | bytes 12582916
  232.9 28.7 %copy-start.2 = (bf16[1024,1024]{1,0:T(8,128)(2,1)S(1)}, bf16[1024,1024]{1,0:T(8,128)(2,1)}, u32[]{:S(2)}) copy-start(bf16[1024,1024]{1,0:T(8,128)(2,1)} %get-tuple-element.32) | copy-start | bytes 6291460
  232.9 327.7 %reduce-scatter.7.cloned.1.call-start = ((), (), s32[]{:S(2)}) async-start(), calls=%async_computation.6 | async-start | bytes 655360
  268.4 307.9 %reduce-scatter.5.cloned.1.call-start = ((), (), s32[]{:S(2)}) async-start(), calls=%async_computation.4 | async-start | bytes 6291456 | tf_op jit(solution)/shard_map/reduce_scatter | solution.py:775
  329.9 6.4 %copy-start.14 = (u32[32]{0:T(128)S(1)}, u32[32]{0:T(128)}, u32[]{:S(2)}) copy-start(u32[32]{0:T(128)} %constant.103) | copy-start | bytes 388
  329.9 7.0 %copy-start.13 = (u32[32]{0:T(128)S(1)}, u32[32]{0:T(128)}, u32[]{:S(2)}) copy-start(u32[32]{0:T(128)} %constant.95) | copy-start | bytes 388
  331.4 242.6 %all-to-all-start.1 = ((bf16[1024,4,256]{2,0,1:T(8,128)(2,1)}), bf16[1024,4,256]{2,0,1:T(8,128)(2,1)}, u32[]{:S(2)}, u32[]{:S(2)}) async-start(bf16[1024,4,256]{2,0,1:T(8,128)(2,1)} %bitcast.60), calls=%async_computation.2 | async-start | bytes 4194304 | tf_op jit(solution)/shard_map/all_to_all | solution.py:786
  338.8 9.6 %copy-start.17 = (bf16[1024,2048]{1,0:T(8,128)(2,1)S(1)}, bf16[1024,2048]{1,0:T(8,128)(2,1)}, u32[]{:S(2)}) copy-start(bf16[1024,2048]{1,0:T(8,128)(2,1)} %get-tuple-element.63) | copy-start | bytes 12582916
  348.4 6.5 %copy-start = (bf16[1024,1536]{1,0:T(8,128)(2,1)S(1)}, bf16[1024,1536]{1,0:T(8,128)(2,1)}, u32[]{:S(2)}) copy-start(bf16[1024,1536]{1,0:T(8,128)(2,1)} %get-tuple-element.39) | copy-start | bytes 9437188
  348.4 6.5 %copy-start.1 = (bf16[512,1024]{1,0:T(8,128)(2,1)S(1)}, bf16[512,1024]{1,0:T(8,128)(2,1)}, u32[]{:S(2)}) copy-start(bf16[512,1024]{1,0:T(8,128)(2,1)} %get-tuple-element.40) | copy-start | bytes 3145732
  354.9 140.6 %copy-start.10 = (f32[1,1536]{1,0:T(1,128)S(1)}, f32[1,1536]{1,0:T(1,128)}, u32[]{:S(2)}) copy-start(f32[1,1536]{1,0:T(1,128)} %get-tuple-element.42) | copy-start | bytes 18436
  354.9 221.3 %copy-start.6 = (bf16[2048,256]{1,0:T(8,128)(2,1)S(1)}, bf16[2048,256]{1,0:T(8,128)(2,1)}, u32[]{:S(2)}) copy-start(bf16[2048,256]{1,0:T(8,128)(2,1)} %refs_1_.1) | copy-start | bytes 3145732
  560.6 21.2 %copy-start.15 = (f32[64]{0:T(128)}, f32[64]{0:T(128)S(1)}, u32[]{:S(2)}) copy-start(f32[64]{0:T(128)S(1)} %dynamic-slice.5) | copy-start | bytes 772
Sparse Core Ops, SparseCore 0:
  233.0 28.4 all-reduce.6
  268.5 35.5 reduce-scatter.6
  326.1 9.8 reduce-scatter.4

commit v3 on v2

--- a/solution.py
+++ b/solution.py
@@ -208,12 +208,12 @@
 def gather_kernel(cols, aligned, *refs):
     (prefix_ref, tok_ref, cot_ref, small_ref, angles, bias_in) = refs[:6]
     masters = refs[6:10]
-    (x_out, c_out, smalls_out, gq_ref, gu_ref, gd_ref, gp_ref, wgq_ref, wgd_ref, gm_ref, att_ref, gb_ref) = refs[10:22]
-    own = refs[22:26]
-    stage = refs[26:30]
-    (x_ref, c_ref, smalls, wq, wd, gains, bias_row, first, first_t) = refs[30:39]
-    (q_t, k_t, v_t, k_n, v_n, up_t, att_t, gm_t, grad_q, grad_k, grad_v) = refs[39:50]
-    (z_send, z_recv, s1_send, s1_recv, s2_send, s2_recv, t_send, t_recv, a_send, a_recv, m_send, m_recv, l_sem) = refs[50:]
+    (x_out, c_out, smalls_out, gq_ref, gu_ref, gd_ref, gp_ref, wgq_out, wgd_out, gm_out, att_out) = refs[10:21]
+    own = refs[21:25]
+    stage = refs[25:29]
+    (x_ref, c_ref, smalls, wq, wd, gains, bias_row, first, first_t) = refs[29:38]
+    (q_t, k_t, v_t, k_n, v_n, up_t, att_t, gm_t, grad_q, grad_k, grad_v, wgq_ref, wgd_ref, att_ref) = refs[38:52]
+    (z_send, z_recv, s1_send, s1_recv, s2_send, s2_recv, t_send, t_recv, a_send, a_recv, m_send, m_recv, l_sem) = refs[52:]
     full = (wq, gu_ref, wd, gp_ref)
     heads = q_t.shape[0]
     dp, row, col, across, along = places()
@@ -459,6 +459,8 @@
 
     width = gm_t.shape[0]
     wide = min(512, width)
+    keep_gm = pltpu.make_async_copy(gm_t, gm_out, l_sem.at[N_W + 3])
+    keep_gm.start()
 
     def qkv_body(i, carry):
         rows = span(i * 256, 256, 256)
@@ -467,6 +469,8 @@
         return carry
 
     lax.fori_loop(0, D // 256, qkv_body, 0)
+    keep_wgq = pltpu.make_async_copy(wgq_ref, wgq_out, l_sem.at[N_W + 4])
+    keep_wgq.start()
     group = min(heads, 4)
 
     def dense_body(i, carry):
@@ -477,16 +481,10 @@
         return carry
 
     lax.fori_loop(0, heads // group, dense_body, 0)
-    pair = min(heads, 2) * 192
-
-    def turn_body(p, carry):
-        spot = pl.ds(0, pair) if pair == width else span(p * pair, pair, 128)
-        value = gm_t[spot, :].T
-        gm_ref[:, spot] = value
-        gb_ref[0:1, spot] = jnp.sum(value.astype(F32), axis=0, keepdims=True)
-        return carry
-
-    lax.fori_loop(0, width // pair, turn_body, 0)
+    keep_wgd = pltpu.make_async_copy(wgd_ref, wgd_out, l_sem.at[N_W + 5])
+    keep_att = pltpu.make_async_copy(att_ref, att_out, l_sem.at[N_W + 6])
+    keep_wgd.start()
+    keep_att.start()
 
     for w in (UP, DOWN):
         finished(w)
@@ -496,7 +494,7 @@
             drained(w, k)
     for kind in range(2):
         token_drain(kind)
-    for keep in (keep_x, keep_wq, keep_c, keep_wd, keep_smalls):
+    for keep in (keep_x, keep_wq, keep_c, keep_wd, keep_smalls, keep_gm, keep_wgq, keep_wgd, keep_att):
         keep.wait()
 
 
@@ -513,8 +511,7 @@
     out_shape = [
         shape((SEQ_LEN, D), BF), shape((SEQ_LEN, D), BF), shape(smalls, F32),
         shape((D, n_q), BF), shape((D, n_u), BF), shape((width, D), BF), shape((wp.shape[0] * DPS, D), BF),
-        shape((D, n_q), BF), shape((width, D), BF), shape((SEQ_LEN, n_q), BF), shape((SEQ_LEN, width), BF),
-        shape((1, n_q), F32),
+        shape((D, n_q), BF), shape((width, D), BF), shape((n_q, SEQ_LEN), BF), shape((SEQ_LEN, width), BF),
     ]
     tok_col = tokens_in.shape[0]
     pieces = tok_col // (SEQ_LEN // cols)
@@ -528,28 +525,25 @@
         buf((8, D), F32), buf((1, n_q), F32), buf((SEQ_LEN, D), BF), buf((D, SEQ_LEN), BF),
         turned, turned, turned, plain, plain, turned, turned, buf((n_q, SEQ_LEN), BF),
         buf((HD, SEQ_LEN), F32), buf((HD, SEQ_LEN), F32), buf((HD, SEQ_LEN), F32),
+        buf((D, n_q), BF), buf((width, D), BF), buf((SEQ_LEN, width), BF),
         dma((N_W, 5)), dma((N_W, 4)), dma((N_W, 4, 2)), dma((N_W, 4, 2)), dma((N_W, 4, 2, 2)), dma((N_W, 4, 2, 2)),
         dma((2, pieces)), dma((2, 4)), dma((2, cols - 1)), dma((2, cols - 1)),
-        dma((ROWS * DPS - 1,)), dma((ROWS * DPS - 1,)), dma((N_W + 3,)),
+        dma((ROWS * DPS - 1,)), dma((ROWS * DPS - 1,)), dma((N_W + 7,)),
     ]
     return pl.pallas_call(
         functools.partial(gather_kernel, cols, aligned),
         out_shape=out_shape,
         in_specs=[smem, any_spec, any_spec, any_spec, vmem, vmem] + [any_spec] * 4,
-        out_specs=[any_spec] * 7 + [vmem] * 5,
+        out_specs=[any_spec] * 11,
         scratch_shapes=scratch,
         compiler_params=pltpu.CompilerParams(collective_id=0, has_side_effects=True, vmem_limit_bytes=60 << 20),
     )(prefix_len, tokens_in, cotangent, small, angles, bias, wq, wu, wd, wp)
 
 
-def lead(name, y, x, half):
-    return (slice(None), y, x, half) if name < 2 else (y, x, half)
-
-
 def add_into(dst, src):
     shape = dst.shape
     outer, height = shape[:-2], shape[-2]
-    step = 32
+    step = min(32, height)
     per = height // step
     total = math.prod(outer) * per
 
@@ -558,143 +552,485 @@
         for size in reversed(outer):
             index.append(lax.rem(rest, size))
             rest = rest // size
-        where = tuple(reversed(index)) + (pl.ds(pl.multiple_of(lax.rem(i, per) * step, step), step),)
+        where = tuple(reversed(index)) + (span(lax.rem(i, per) * step, step, step),)
         dst[where] = (dst[where].astype(F32) + src[where].astype(F32)).astype(BF)
         return carry
 
     lax.fori_loop(0, total, body, 0)
 
 
-def scatter_kernel(cols, heights, *refs):
-    g_refs = refs[:4]
-    out_refs = refs[4:8]
-    mine = (refs[8:10], refs[10:12], refs[12:14], refs[14:16])
-    got1 = (refs[16:18], refs[18:20], refs[20:22], refs[22:24])
-    got2 = (refs[24:26], refs[26:28], refs[28:30], refs[30:32])
-    got3 = (refs[32:34], refs[34:36], refs[36:38], refs[38:40])
-    l_sem, s1_send, s1_recv, s2_send, s2_recv, s3_send, s3_recv = refs[40:]
+def pieces_of(n_q, n_u, h_d, h_p):
+    out = [(DENSE, 0, h_d // 2)]
+    for w, n in ((QKV, n_q), (UP, n_u)):
+        size = 512 if n % 512 == 0 else n
+        out += [(w, start, size) for start in range(0, n, size)]
+    half = h_p // 2
+    size = 64 if half % 64 == 0 else half
+    return out + [(DOWN, start, size) for start in range(0, half, size)]
+
+
+def gelu_parts(x):
+    below = 0.5 * (1.0 + lax.erf(x * (0.5**0.5)))
+    density = jnp.exp(-0.5 * x * x) * (1.0 / math.sqrt(2.0 * math.pi))
+    return x * below, below + x * density
+
+
+def scatter_kernel(cols, aligned, pieces, *refs):
+    n_p = len(pieces)
+    (x_in, c_in, smalls, wu_in, wp_in, wq_in, wd_in, gq_in, gd_in, gm_in, att_in, ub_in) = refs[:12]
+    (lo_out, gt_out, oq, ou, od, op, sm_out) = refs[12:19]
+    (wu, wp, x_ref, c_ref, second, second_t, hid_t, ghp, gu, gp, branch, comb, branch_got, comb_got) = refs[19:33]
+    (gains, bias_row, out_bias, sm, sm_got, gain_sum, att_spare, wq_spare) = refs[33:41]
+    mine_q, mine_d = refs[41:43], refs[43:45]
+    base = 45
+    got1 = [refs[base + 2 * i : base + 2 * i + 2] for i in range(n_p)]
+    base += 2 * n_p
+    got2 = [refs[base + 2 * i : base + 2 * i + 2] for i in range(n_p)]
+    base += 2 * n_p
+    got_end = [refs[base + 2 * i : base + 2 * i + 2] for i in range(n_p)]
+    base += 2 * n_p
+    got_mid = [refs[base + 2 * i : base + 2 * i + 2] for i in range(n_p)]
+    base += 2 * n_p
+    got_back = [refs[base + 2 * i : base + 2 * i + 2] for i in range(n_p)]
+    base += 2 * n_p
+    (l_sem, f_sem, s1_send, s1_recv, s2_send, s2_recv, e_send, e_recv, m_send, m_recv, b_send, b_recv, d_send, d_recv,
+     t_send, t_recv, v_send, v_recv) = refs[base:]
     dp, row, col, across, along = places()
     x, y = lax.rem(dp, 2), dp // 2
-
-    greet(peers_of(dp, row, col, cols))
-
-    def first(w, half):
+    side, at = line_order(row)
+    far_end = row // 2
+    middle, end = side == 1, side == 0
+    n_q, n_u = wq_in.shape[1], wu_in.shape[1]
+    tok_col = lo_out.shape[0]
+    part = SEQ_LEN // cols
+    width = ghp.shape[1]
+    blocks = n_u // width
+
+    def load(src, dst, n):
+        return pltpu.make_async_copy(src, dst, l_sem.at[n])
+
+    att_width = att_in.shape[1]
+    att_buf = ghp.at[:, pl.ds(0, att_width)] if att_width % 128 == 0 else att_spare
+    wq_buf = wu.at[:, pl.ds(0, n_q)] if n_q % 128 == 0 else wq_spare
+    loads = [
+        load(x_in, x_ref, 0), load(att_in, att_buf, 1), load(wd_in, hid_t.at[pl.ds(0, att_width), :], 2),
+        load(c_in, c_ref, 3), load(wu_in, wu.at[:, pl.ds(0, n_u)], 4), load(wp_in, wp.at[pl.ds(0, n_u), :], 5),
+    ]
+    for one in loads:
+        one.start()
+    group = [(dp, lax.rem(row + step, ROWS), lax.rem(col + other, cols)) for step in range(ROWS) for other in range(cols)]
+    greet([(across, row, col), (along, row, col)] + group[1:])
+
+    def view(i, half, other):
+        w, start, size = pieces[i]
         if half == 0:
-            src, target = g_refs[w].at[lead(w, 1 - y, slice(None), 0)], along
+            place_y, place_x = (1 - y if other else y), slice(None)
         else:
-            src, target = g_refs[w].at[lead(w, slice(None), 1 - x, 1)], across
-        return remote(src, got1[w][half], s1_send.at[w, half], s1_recv.at[w, half], (target, row, col))
-
-    def fetch(w, half):
-        src = g_refs[w].at[lead(w, y, slice(None), 0)] if half == 0 else g_refs[w].at[lead(w, slice(None), x, 1)]
-        return pltpu.make_async_copy(src, mine[w][half], l_sem.at[w, half])
-
-    def keep(w, half, other):
-        which = (x if half == 0 else y)
+            place_y, place_x = slice(None), (1 - x if other else x)
+        cut = pl.ds(start, size)
+        if w in (QKV, UP):
+            if w == QKV and not other:
+                return mine_q[half].at[:, :, :, cut]
+            return (gq_in if w == QKV else gu).at[:, place_y, place_x, half, :, cut]
+        if w == DENSE and not other:
+            return mine_d[half].at[:, cut, :]
+        return (gd_in if w == DENSE else gp).at[place_y, place_x, half, cut, :]
+
+    def fetch(i, half):
+        w, start, size = pieces[i]
+        place_y, place_x = (y, slice(None)) if half == 0 else (slice(None), x)
+        cut = pl.ds(start, size)
+        src = gq_in.at[:, place_y, place_x, half, :, cut] if w == QKV else gd_in.at[place_y, place_x, half, cut, :]
+        return pltpu.make_async_copy(src, view(i, half, False), f_sem.at[i, half])
+
+    def first(i, half):
+        target = along if half == 0 else across
+        return remote(view(i, half, True), got1[i][half], s1_send.at[i, half], s1_recv.at[i, half], (target, row, col))
+
+    def keep(i, half, other):
+        which = x if half == 0 else y
         which = 1 - which if other else which
-        return mine[w][half].at[:, which] if w < 2 else mine[w][half].at[which]
-
-    def second(w, half):
+        kept = view(i, half, False)
+        return kept.at[:, which] if pieces[i][0] in (QKV, UP) else kept.at[which]
+
+    def second_copy(i, half):
         target = across if half == 0 else along
-        return remote(keep(w, half, True), got2[w][half], s2_send.at[w, half], s2_recv.at[w, half], (target, row, col))
-
-    def block(w, half, r):
-        kept = keep(w, half, False)
-        if w < 2:
-            return kept.at[r]
-        return kept.at[:, pl.ds(pl.multiple_of(r * 256, 256), 256)]
-
-    def third(w, half, step):
-        to_row = lax.rem(row + step, ROWS)
-        return remote(
-            block(w, half, to_row), got3[w][half].at[step - 1], s3_send.at[w, half, step - 1],
-            s3_recv.at[w, half, step - 1], (dp, to_row, col)
-        )
-
-    def total(w, half):
-        height = out_refs[w].shape[1]
-        step = 32
+        return remote(keep(i, half, True), got2[i][half], s2_send.at[i, half], s2_recv.at[i, half], (target, row, col))
+
+    def lines(i, ref, start, count):
+        if pieces[i][0] in (QKV, UP):
+            return ref.at[pl.ds(start, count)]
+        return ref.at[:, span(start * 256, count * 256, 256)]
+
+    def end_copy(i, half):
+        src = lines(i, keep(i, half, False), 1 - far_end, 3)
+        return remote(src, got_end[i][half], e_send.at[i, half], e_recv.at[i, half], (dp, at(1), col))
+
+    def mid_copy(i, half):
+        src = lines(i, keep(i, half, False), 2 * (1 - far_end), 2)
+        return remote(src, got_mid[i][half], m_send.at[i, half], m_recv.at[i, half], (dp, at(2), col))
+
+    def back_copy(i, half):
+        src = lines(i, keep(i, half, False), at(0), 1)
+        return remote(src, got_back[i][half], b_send.at[i, half], b_recv.at[i, half], (dp, at(0), col))
+
+    def begin(i):
+        for half in range(2):
+            first(i, half).start()
+            if pieces[i][0] in (QKV, DENSE):
+                fetch(i, half).start()
+
+    def stage_two(i):
+        for half in range(2):
+            if pieces[i][0] in (QKV, DENSE):
+                fetch(i, half).wait()
+            first(i, half).wait_recv()
+            add_into(view(i, half, False), got1[i][half])
+            second_copy(i, half).start()
+
+    def stage_three(i):
+        for half in range(2):
+            second_copy(i, half).wait_recv()
+            add_into(keep(i, half, False), got2[i][half])
+
+            @pl.when(end)
+            def _():
+                end_copy(i, half).start()
+
+    def stage_four(i):
+        @pl.when(middle)
+        def _():
+            for half in range(2):
+                end_copy(i, half).wait_recv()
+                add_into(lines(i, keep(i, half, False), 2 * (1 - far_end), 2), lines(i, got_end[i][half], 1 - far_end, 2))
+                mid_copy(i, half).start()
+
+    def stage_five(i):
+        @pl.when(middle)
+        def _():
+            for half in range(2):
+                mid_copy(i, half).wait_recv()
+                add_into(lines(i, keep(i, half, False), at(0), 1), lines(i, got_mid[i][half], far_end, 1))
+                back_copy(i, half).start()
+
+    def stage_six(i):
+        w, start, size = pieces[i]
+        out = (oq, ou, od, op)[w]
+        for half in range(2):
+            mine = lines(i, keep(i, half, False), row, 1)
+
+            def total(others):
+                if w in (QKV, UP):
+                    value = mine[0].astype(F32)
+                    for other in others:
+                        value = value + other[0].astype(F32)
+                    out[half, :, pl.ds(start, size)] = value
+                else:
+                    value = mine[...].astype(F32)
+                    for other in others:
+                        value = value + other[...].astype(F32)
+                    out[half, pl.ds(start, size), :] = value
+
+            @pl.when(end)
+            def _():
+                back_copy(i, half).wait_recv()
+                total([got_back[i][half]])
+
+            @pl.when(middle)
+            def _():
+                total([lines(i, got_end[i][half], 2 * far_end, 1), lines(i, got_mid[i][half], 1 - far_end, 1)])
+
+    def drain(i):
+        for half in range(2):
+            first(i, half).wait_send()
+            second_copy(i, half).wait_send()
+
+            @pl.when(end)
+            def _():
+                end_copy(i, half).wait_send()
+
+            @pl.when(middle)
+            def _():
+                mid_copy(i, half).wait_send()
+                back_copy(i, half).wait_send()
+
+    ahead, lag = 2, (0, 2, 3, 4, 5)
+    stages = (stage_two, stage_three, stage_four, stage_five, stage_six)
+
+    def step(s):
+        for stage, late in zip(stages, lag):
+            if 0 <= s - late < n_p:
+                stage(s - late)
+            if stage is stage_two and ahead <= s + ahead < n_p:
+                begin(s + ahead)
+
+    def part_rows(piece):
+        return span(piece * part, part, part)
+
+    def col_copy(kind, n):
+        other = lax.rem(col + n, cols)
+        src = (branch, comb)[kind].at[part_rows(other), :]
+        dst = (branch_got, comb_got)[kind].at[n - 1]
+        return remote(src, dst, d_send.at[kind, n - 1], d_recv.at[kind, n - 1], (dp, row, other))
+
+    start = row * SEQ_LEN + col * part
+    owner, offset = start // tok_col, lax.rem(start, tok_col)
+
+    def out_copy(kind, r):
+        src = second.at[pl.ds(kind * part, part), pl.ds(r * 256, 256)]
+        dst = (lo_out, gt_out)[kind].at[span(offset, part, part), :]
+        recv = t_recv.at[kind, offset // part]
+        here = jnp.logical_and(row == r, owner == col)
+        far = remote(src, dst, t_send.at[kind, r], recv, (dp, r, owner))
+        return here, far, pltpu.make_async_copy(src, dst, recv)
+
+    def out_start(kind):
+        for r in range(ROWS):
+            here, far, near = out_copy(kind, r)
+            pl.when(jnp.logical_not(here))(far.start)
+            pl.when(here)(near.start)
+
+    def out_finish(kind):
+        for r in range(ROWS):
+            here, far, near = out_copy(kind, r)
+            pl.when(jnp.logical_not(here))(far.wait_send)
+        out = (lo_out, gt_out)[kind]
+        for n in range(tok_col // part):
+            block = out.at[pl.ds(n * part, part), :]
+            pltpu.make_async_copy(block, block, t_recv.at[kind, n]).wait()
+
+    height = min(128, part)
+
+    def finish_rows(kind):
+        for n in range(1, cols):
+            col_copy(kind, n).wait_recv()
 
         def body(i, carry):
-            rows = pl.ds(pl.multiple_of(i * step, step), step)
-            value = block(w, half, row)[rows, :].astype(F32)
-            for s in range(3):
-                value = value + got3[w][half][s, rows, :].astype(F32)
-            out_refs[w][half, rows, :] = value
+            here = span(i * height, height, height)
+            rows = span(col * part + i * height, height, height)
+            value = (branch, comb)[kind][rows, :]
+            for n in range(1, cols):
+                value = value + (branch_got, comb_got)[kind][n - 1, here, :]
+            wide = x_ref[rows, :].astype(F32)
+            if kind == 0:
+                value = wide + value + out_bias[0:1, :]
+            else:
+                normed, scale_inv = norm_rows(wide)
+                mean = jnp.mean(value, axis=1, keepdims=True)
+                cross = jnp.mean(value * normed, axis=1, keepdims=True)
+                value = c_ref[rows, :].astype(F32) + scale_inv * (value - mean - normed * cross)
+            second[span(kind * part + i * height, height, height), :] = value.astype(BF)
             return carry
 
-        lax.fori_loop(0, height // step, body, 0)
-
-    sequence = [(w, half) for w in (2, 0, 1, 3) for half in range(2)]
-
-    def begin(w, half):
-        first(w, half).start()
-        fetch(w, half).start()
-
-    for w, half in sequence[:4]:
-        begin(w, half)
-
-    def stage_two(w, half):
-        fetch(w, half).wait()
-        first(w, half).wait_recv()
-        add_into(mine[w][half], got1[w][half])
-        second(w, half).start()
-
-    def stage_three(w, half):
-        second(w, half).wait()
-        add_into(keep(w, half, False), got2[w][half])
-        for step in range(1, ROWS):
-            third(w, half, step).start()
-
-    def stage_four(w, half):
-        for step in range(1, ROWS):
-            third(w, half, step).wait()
-        total(w, half)
-
-    lag2, lag3 = 2, 4
-    n = len(sequence)
-    for i in range(n + lag3):
-        if i < n:
-            stage_two(*sequence[i])
-            if i + 4 < n:
-                begin(*sequence[i + 4])
-        if 0 <= i - lag2 < n:
-            stage_three(*sequence[i - lag2])
-        if 0 <= i - lag3 < n:
-            stage_four(*sequence[i - lag3])
-    for w, half in sequence:
-        first(w, half).wait_send()
-
-
-def scatter(grads, cols):
+        lax.fori_loop(0, part // height, body, 0)
+
+    def small_copy(n):
+        if n < 2:
+            return remote(sm.at[n], sm_got.at[n], v_send.at[n], v_recv.at[n], ((across, along)[n], row, col))
+        if n < 5:
+            target = (dp, lax.rem(row + n - 1, ROWS), col)
+            return remote(sm.at[2], sm_got.at[n], v_send.at[n], v_recv.at[n], target)
+        target = (dp, row, lax.rem(col + n - 4, cols))
+        return remote(sm.at[3], sm_got.at[n], v_send.at[n], v_recv.at[n], target)
+
+    def small_step(n):
+        if n > 0:
+            waits = ((0,), (1,), (2, 3, 4), tuple(range(5, 4 + cols)))[n - 1]
+            for m in waits:
+                small_copy(m).wait_recv()
+            value = sm[n - 1]
+            if n < 4:
+                for m in waits:
+                    value = value + sm_got[m]
+                sm[n] = value
+            else:
+                sm_out[...] = value
+                value = value[0:4]
+                for m in waits:
+                    value = value + sm_got[m, 0:4, :]
+                sm_out[0:4, :] = value
+        for m in ((0,), (1,), (2, 3, 4), tuple(range(5, 4 + cols)), ())[n]:
+            small_copy(m).start()
+
+    for i in range(min(ahead, n_p)):
+        begin(i)
+
+    read_gains(smalls, gains)
+    lanes = lax.broadcasted_iota(jnp.int32, (1, 128), 1)
+    for r in range(ROWS):
+        for d in range(0, DPS, 2):
+            pair = jnp.where(lanes < 64, smalls[r * DPS + d, 8:9, :], smalls[r * DPS + d + 1, 8:9, :])
+            out_bias[0:1, pl.ds(r * 256 + d * 64, 128)] = pair
+    if aligned:
+        read_bias(smalls, bias_row, 9 + n_q // (DPS * 128), n_u // DPS)
+    else:
+        bias_row[...] = ub_in[...]
+    loads[0].wait()
+    norm_stage(x_ref, gains, 2, second, second_t)
+    loads[1].wait()
+    loads[2].wait()
+    for j in range(SEQ_LEN // 256):
+        rows = pl.ds(j * 256, 256)
+        branch[rows, :] = nn(att_buf[rows, :], hid_t[0:att_width, :])
+    for one in loads[3:]:
+        one.wait()
+    sm[0] = jnp.zeros(sm.shape[1:], F32)
+
+    def feed(n):
+        cut = span(n * width, width, width)
+
+        def body(j, carry):
+            rows = span(j * 256, 256, 256)
+            pre = nn(second[rows, :], wu[:, cut]) + bias_row[0:1, cut]
+            grad = nt(c_ref[rows, :], wp[cut, :])
+            hidden, slope = gelu_parts(pre)
+            hidden = hidden.astype(BF)
+            grad = (grad * slope).astype(BF)
+            hid_t[0:width, rows] = hidden.T
+            ghp[rows, 0:width] = grad
+            branch[rows, :] += nn(hidden, wp[cut, :])
+            back = nt(grad, wu[:, cut])
+
+            @pl.when(n == 0)
+            def _():
+                comb[rows, :] = back
+
+            @pl.when(n > 0)
+            def _():
+                comb[rows, :] += back
+
+            sm[0, 6:7, cut] += jnp.sum(grad.astype(F32), axis=0, keepdims=True)
+            return carry
+
+        lax.fori_loop(0, SEQ_LEN // 256, body, 0)
+
+        def up_body(r, carry):
+            value = nn(second_t[span(r * 256, 256, 256), :], ghp[:, 0:width]).astype(BF)
+            gu[r, :, :, :, :, cut] = value.reshape(2, 2, 2, 32, width)
+            return carry
+
+        lax.fori_loop(0, ROWS, up_body, 0)
+        h = gp.shape[3]
+        if blocks == DPS:
+            for half in range(2):
+                gp[n // 2, lax.rem(n, 2), half] = nn(hid_t[half * h : (half + 1) * h, :], c_ref[...]).astype(BF)
+        else:
+            gp[...] = nn(hid_t[0:width, :], c_ref[...]).astype(BF).reshape(2, 2, 2, h, D)
+
+    def feed_body(n, carry):
+        feed(n)
+        for s in range(blocks):
+            pl.when(n == s)(functools.partial(step, s))
+        return carry
+
+    lax.fori_loop(0, blocks, feed_body, 0)
+    load_wq = load(wq_in, wq_buf, 4)
+    load_gm = load(gm_in, wp.at[pl.ds(0, n_q), :], 5)
+    load_wq.start()
+    load_gm.start()
+    for n in range(1, cols):
+        col_copy(0, n).start()
+    step(blocks)
+    load_wq.wait()
+    load_gm.wait()
+    for n in range(8):
+        gain_sum[n : n + 1, :] = jnp.zeros((1, D), F32)
+
+    def first_body(j, carry):
+        rows = span(j * 256, 256, 256)
+        grad = wp[0:n_q, rows].T
+        grad_first = nt(grad, wq_buf[...])
+        grad_second = comb[rows, :]
+        normed, ignored = norm_rows(x_ref[rows, :].astype(F32))
+        for n, value in enumerate((normed * grad_first, grad_first, normed * grad_second, grad_second,
+                                   c_ref[rows, :].astype(F32))):
+            gain_sum[n : n + 1, :] += jnp.sum(value, axis=0, keepdims=True)
+        sm[0, 5:6, 0:n_q] += jnp.sum(grad.astype(F32), axis=0, keepdims=True)
+        comb[rows, :] = gains[0:1, :] * grad_first + gains[2:3, :] * grad_second
+        return carry
+
+    lax.fori_loop(0, SEQ_LEN // 256, first_body, 0)
+    for n in range(1, cols):
+        col_copy(1, n).start()
+    sm[0, 0:5, 0:D] = gain_sum[0:5, :]
+    small_step(0)
+    finish_rows(0)
+    out_start(0)
+    step(blocks + 1)
+    finish_rows(1)
+    out_start(1)
+    small_step(1)
+    step(blocks + 2)
+    small_step(2)
+    step(blocks + 3)
+    small_step(3)
+    step(blocks + 4)
+    small_step(4)
+    for s in range(blocks + 5, n_p + lag[-1]):
+        step(s)
+    for i in range(n_p):
+        drain(i)
+    for kind in range(2):
+        out_finish(kind)
+        for n in range(1, cols):
+            col_copy(kind, n).wait_send()
+    for n in range(4 + cols):
+        small_copy(n).wait_send()
+
+
+def scatter(own_x, own_cot, smalls, wu, wp, wq, wd, wgrad_q, wgrad_d, grad_mixed, attended, u_bias, cols, aligned, tok_col):
     any_spec = pl.BlockSpec(memory_space=pl.ANY)
     vmem = pl.BlockSpec(memory_space=pltpu.VMEM)
     dma = pltpu.SemaphoreType.DMA
-    outs, mine, got1, got2, got3 = [], [], [], [], []
-    for w, grad in enumerate(grads):
-        h, n = grad.shape[-2:]
-        if w < 2:
-            outs.append(jax.ShapeDtypeStruct((2, h, n), F32))
-            mine += [pltpu.VMEM((ROWS, 2, h, n), BF)] * 2
-            got1 += [pltpu.VMEM((ROWS, 2, h, n), BF)] * 2
-            got2 += [pltpu.VMEM((ROWS, h, n), BF)] * 2
-            got3 += [pltpu.VMEM((3, h, n), BF)] * 2
-        else:
-            outs.append(jax.ShapeDtypeStruct((2, h, 256), F32))
-            mine += [pltpu.VMEM((2, h, n), BF)] * 2
-            got1 += [pltpu.VMEM((2, h, n), BF)] * 2
-            got2 += [pltpu.VMEM((h, n), BF)] * 2
-            got3 += [pltpu.VMEM((3, h, 256), BF)] * 2
+    buf = pltpu.VMEM
+    shape = jax.ShapeDtypeStruct
+    n_q, n_u = wq.shape[1], wu.shape[1]
+    h_d, h_p = wd.shape[0] // DPS, wp.shape[0] // DPS
+    pieces = pieces_of(n_q, n_u, h_d, h_p)
+    n_p = len(pieces)
+    part = SEQ_LEN // cols
+    width = 512 if n_u % (DPS * 512) == 0 and n_u == DPS * 512 else n_u
+    most = max(n_q, n_u)
+    line = max(most, D)
+    block = max(width, wd.shape[0])
+    scratch = [
+        buf((D, most), BF), buf((most, D), BF), buf((SEQ_LEN, D), BF), buf((SEQ_LEN, D), BF), buf((SEQ_LEN, D), BF),
+        buf((D, SEQ_LEN), BF), buf((block, SEQ_LEN), BF), buf((SEQ_LEN, block), BF),
+        buf((ROWS, 2, 2, 2, 32, n_u), BF), buf((2, 2, 2, h_p // 2, D), BF), buf((SEQ_LEN, D), F32), buf((SEQ_LEN, D), F32),
+        buf((cols - 1, part, D), F32), buf((cols - 1, part, D), F32),
+        buf((8, D), F32), buf((1, n_u), F32), buf((1, D), F32), buf((4, 8, line), F32), buf((4 + cols, 8, line), F32),
+        buf((8, D), F32), buf((SEQ_LEN, wd.shape[0]) if wd.shape[0] % 128 else (8, 128), BF),
+        buf((D, n_q) if n_q % 128 else (8, 128), BF),
+    ]
+    scratch += [buf((ROWS, 2, 32, n_q), BF)] * 2 + [buf((2, h_d // 2, D), BF)] * 2
+    wide = [w in (QKV, UP) for w, start, size in pieces]
+    sizes = [size for w, start, size in pieces]
+    for lead, count in (((ROWS, 2), None), ((ROWS,), None), ((3,), 3), ((2,), 2), ((1,), 1)):
+        for is_wide, size in zip(wide, sizes):
+            if is_wide:
+                one = lead + (32, size)
+            elif count is None:
+                one = ((2,) if len(lead) == 2 else ()) + (size, D)
+            else:
+                one = (size, 256 * count)
+            scratch += [buf(one, BF)] * 2
+    scratch += [
+        dma((6,)), dma((n_p, 2)), dma((n_p, 2)), dma((n_p, 2)), dma((n_p, 2)), dma((n_p, 2)), dma((n_p, 2)), dma((n_p, 2)),
+        dma((n_p, 2)), dma((n_p, 2)), dma((n_p, 2)), dma((n_p, 2)), dma((2, cols - 1)), dma((2, cols - 1)),
+        dma((2, ROWS)), dma((2, tok_col // part)), dma((4 + cols,)), dma((4 + cols,)),
+    ]
     return pl.pallas_call(
-        functools.partial(scatter_kernel, cols, None),
-        out_shape=outs,
-        in_specs=[any_spec] * 4,
-        out_specs=[vmem] * 4,
-        scratch_shapes=mine + got1 + got2 + got3 + [
-            dma((N_W, 2)), dma((N_W, 2)), dma((N_W, 2)), dma((N_W, 2)), dma((N_W, 2)), dma((N_W, 2, 3)), dma((N_W, 2, 3)),
+        functools.partial(scatter_kernel, cols, aligned, pieces),
+        out_shape=[
+            shape((tok_col, 256), BF), shape((tok_col, 256), BF), shape((2, 32, n_q), F32), shape((2, 32, n_u), F32),
+            shape((2, h_d // 2, 256), F32), shape((2, h_p // 2, 256), F32), shape((8, line), F32),
         ],
-        compiler_params=pltpu.CompilerParams(collective_id=1, has_side_effects=True, vmem_limit_bytes=48 << 20),
-    )(*grads)
+        in_specs=[any_spec] * 2 + [vmem] + [any_spec] * 8 + [vmem],
+        out_specs=[any_spec] * 2 + [vmem] * 5,
+        scratch_shapes=scratch,
+        compiler_params=pltpu.CompilerParams(collective_id=1, has_side_effects=True, vmem_limit_bytes=63 << 20),
+    )(own_x, own_cot, smalls, wu, wp, wq, wd, wgrad_q.reshape(ROWS, 2, 2, 2, 32, n_q),
+      wgrad_d.reshape(2, 2, 2, h_d // 2, D), grad_mixed, attended, u_bias)
 
 
 def angles_table():
@@ -705,21 +1041,11 @@
     return (jnp.cos(turned), jnp.sin(turned))
 
 
-def contract_rows(left_side, right_side):
-    return lax.dot_general(left_side, right_side, (((0,), (0,)), ((), ())), preferred_element_type=F32)
-
-
-def contract_cols(left_side, right_side):
-    return lax.dot_general(left_side, right_side, (((1,), (1,)), ((), ())), preferred_element_type=F32)
-
-
 def shards(cols, tokens_in, prefix_len, first_gain, first_shift, second_gain, second_shift, qkv_weight, qkv_bias,
            up_weight, up_bias, dense_weight, dense_bias, down_weight, down_bias, cotangent):
     tok_col = tokens_in.shape[0]
     n_q, n_u = qkv_weight.shape[1], up_weight.shape[1]
     h_d, h_p = dense_weight.shape[0], down_weight.shape[0]
-    heads = n_q // (3 * HD)
-    width_att = heads * HD
 
     out_part = dense_bias.astype(BF).astype(F32) + down_bias.astype(BF).astype(F32)
     q_part, u_part = qkv_bias.astype(BF).astype(F32), up_bias.astype(BF).astype(F32)
@@ -729,76 +1055,24 @@
     size = -(-small.shape[0] // 1024) * 1024
     small = jnp.pad(small, (0, size - small.shape[0])).reshape(size // 128, 128)
     if aligned:
-        q_bias = jnp.zeros((1, n_q), F32)
+        q_bias, u_bias = jnp.zeros((1, n_q), F32), jnp.zeros((1, n_u), F32)
     else:
         q_bias = lax.all_gather(q_part, "dp", axis=0, tiled=True).reshape(1, n_q)
+        u_bias = lax.all_gather(u_part, "dp", axis=0, tiled=True).reshape(1, n_u)
     cos_table, sin_table = angles_table()
     angles = jnp.concatenate([cos_table.T, sin_table.T], axis=0)
-    own_x, own_cot, smalls, wq, wu, wd, wp, wgrad_q, wgrad_d, grad_mixed, attended, sum_q = gather(
+    own_x, own_cot, smalls, wq, wu, wd, wp, wgrad_q, wgrad_d, grad_mixed, attended = gather(
         prefix_len, tokens_in, cotangent, small, angles, q_bias, (qkv_weight, up_weight, dense_weight, down_weight), cols,
         aligned
     )
-    flat = smalls.reshape(ROWS, DPS, size)
-    gains = [flat[:, 0, 256 * i : 256 * (i + 1)].reshape(D) for i in range(4)]
-    out_bias = flat[:, :, 1024:1088].reshape(D)
-    u_bias = flat[0, :, 1152 + n_qb : 1152 + n_qb + n_ub].reshape(n_u)
-
-    wide = own_x.astype(F32)
-    center = jnp.mean(wide, axis=1, keepdims=True)
-    spread = jnp.mean(wide * wide, axis=1, keepdims=True) - center * center
-    scale_inv = lax.rsqrt(spread + EPS)
-    normed = (wide - center) * scale_inv
-    second_in = (normed * gains[2] + gains[3]).astype(BF)
-
-    hidden_pre = jnp.dot(second_in, wu, preferred_element_type=F32) + u_bias
-    hidden = jax.nn.gelu(hidden_pre, approximate=False).astype(BF)
-    branch = jnp.dot(attended, wd, preferred_element_type=F32) + jnp.dot(hidden, wp, preferred_element_type=F32)
-    grad_hidden = contract_cols(own_cot, wp)
-    ignored, gelu_back = jax.vjp(functools.partial(jax.nn.gelu, approximate=False), hidden_pre)
-    grad_hidden_pre = gelu_back(grad_hidden)[0].astype(BF)
-
-    grads = (
-        wgrad_q.reshape(ROWS, 2, 2, 2, 32, n_q),
-        contract_rows(second_in, grad_hidden_pre).astype(BF).reshape(ROWS, 2, 2, 2, 32, n_u),
-        wgrad_d.reshape(2, 2, 2, h_d // 2, D),
-        contract_rows(hidden, own_cot).astype(BF).reshape(2, 2, 2, h_p // 2, D),
+    layer_out, grad_tokens, out_q, out_u, out_d, out_p, sums = scatter(
+        own_x, own_cot, smalls, wu, wp, wq, wd, wgrad_q, wgrad_d, grad_mixed, attended, u_bias, cols, aligned, tok_col
     )
-    out_q, out_u, out_d, out_p = scatter(grads, cols)
-
-    grad_first = contract_cols(grad_mixed, wq)
-    grad_second = contract_cols(grad_hidden_pre, wu)
-    combined = grad_first * gains[0] + grad_second * gains[2]
-    part = SEQ_LEN // cols
-
-    def to_owner(partial):
-        moved = lax.all_to_all(partial, "row", split_axis=1, concat_axis=0, tiled=True)
-        return lax.psum_scatter(moved, "col", scatter_dimension=0, tiled=True)
-
-    branch_sum = to_owner(branch)
-    combined = lax.psum(combined, "col")
-    gain_rows = jnp.stack([
-        jnp.sum(normed * grad_first, axis=0), jnp.sum(grad_first, axis=0),
-        jnp.sum(normed * grad_second, axis=0), jnp.sum(grad_second, axis=0),
-    ])
-    line_total = jnp.mean(combined, axis=1, keepdims=True)
-    cross_total = jnp.mean(combined * normed, axis=1, keepdims=True)
-    grad_tokens = (own_cot.astype(F32) + scale_inv * (combined - line_total - normed * cross_total)).astype(BF)
-    grad_tokens = lax.all_to_all(grad_tokens, "row", split_axis=1, concat_axis=0, tiled=True)
-    grad_tokens = lax.dynamic_slice_in_dim(grad_tokens, lax.axis_index("col") * tok_col, tok_col, 0)
-    row = lax.axis_index("row")
-    here = lax.dynamic_slice_in_dim(out_bias, row * 256, 256, 0)
-    layer_out = (tokens_in.astype(F32) + branch_sum + here).astype(BF)
-
-    gain_sums = lax.psum_scatter(
-        lax.psum(gain_rows, ("dp", "col")), "row", scatter_dimension=1, tiled=True
-    )
-    out_b = lax.psum_scatter(jnp.sum(own_cot.astype(F32), axis=0), ("row", "dp"), scatter_dimension=0, tiled=True)
-    q_b = lax.psum_scatter(
-        lax.psum(sum_q[0], "row"), "dp", scatter_dimension=0, tiled=True
-    )
-    u_b = lax.psum_scatter(
-        lax.psum(jnp.sum(grad_hidden_pre.astype(F32), axis=0), "row"), "dp", scatter_dimension=0, tiled=True
-    )
+    dp, row = lax.axis_index("dp"), lax.axis_index("row")
+    gain_sums = lax.dynamic_slice(sums, (0, row * 256), (4, 256))
+    out_b = lax.dynamic_slice(sums, (4, (row * DPS + dp) * 64), (1, 64))[0]
+    q_b = lax.dynamic_slice(sums, (5, dp * n_qb), (1, n_qb))[0]
+    u_b = lax.dynamic_slice(sums, (6, dp * n_ub), (1, n_ub))[0]
     return (
         layer_out, grad_tokens, out_q.reshape(64, n_q), q_b, out_u.reshape(64, n_u), u_b,
         out_d.reshape(h_d, 256), out_b, out_p.reshape(h_p, 256), out_b,

time: 598 us -> 317 us (0.53); the launches traced: 590 us -> 316 us
  waiting for transfers between devices: 80.8 us -> 0 us
  blocking collectives: 76.5 us -> 0 us
  matrix products: 72.9 us -> 0 us
  other arithmetic: 25.6 us -> 2.89 us
  between operations: 17.2 us -> 1.36 us
  starting transfers between devices: 10.2 us -> 0 us
  Pallas kernels: 287 us -> 296 us
    dot_general x8 -> x0, matrix products: 72.9 us -> none  [the longest x3 38.1 us: contract_cols(): lax.dot_general(left_side, right_side, (((1,), (1,)), ((), ())), preferre...]
    all_to_all x2 -> x0, waiting for transfers between devices: 52.2 us -> none  [the longest x1 52.2 us: to_owner(): lax.all_to_all(partial, 'row', split_axis=1, concat_axis=0, tiled=True)]
    unnamed x2 -> x0, blocking collectives: 51.5 us -> none
    psum x1 -> x0, waiting for transfers between devices: 28.6 us -> none  [shards(): combined = lax.psum(combined, 'col')]
    psum x2 -> x0, blocking collectives: 25 us -> none  [the longest x1 13.2 us: shards(): lax.psum(sum_q[0], 'row')]
    pallas_call x1, Pallas kernels: 140 us -> 152 us  [scatter(): pl.pallas_call(functools.partial(scatter_kernel, cols, aligned, pieces),...]
    reduce_sum x3 -> x0, other arithmetic: 11.8 us -> none  [the longest x1 5.74 us: shards(): line_total = jnp.mean(combined, axis=1, keepdims=True)]
    convert_element_type x2 -> x0, other arithmetic: 10.8 us -> none  [the longest x1 7.98 us: shards(): hidden = jax.nn.gelu(hidden_pre, approximate=False).astype(BF)]
  transfers between devices with their start and end apart: 5 -> 0, of which waited for: 2 -> 0; matrix products, arithmetic and copies ran while one was open for 9% -> 0% of each run, Pallas kernels for 24% -> 0%
where the time goes in v3:
time: 317 us; the launch traced here: 316 us
  Pallas kernels  296 us (93%)
  local copies, waits for them, and re-layouts  15.8 us (5%)
    pallas_call x1, Pallas kernels, scatter(): pl.pallas_call(functools.partial(scatter_kernel, cols, aligned, pieces),...  152 us
    pallas_call x1, Pallas kernels, gather(): pl.pallas_call(functools.partial(gather_kernel, cols, aligned), out_shape...  144 us
    unnamed x17, local copies, waits for them, and re-layouts  8.1 us

profile of v3, /device:TPU:0, one launch (start us, length us, event | category | flops | bytes accessed | tf_op | source)
XLA Modules:
  0.0 316.0 jit_solution(6617497240058243096)
XLA Ops:
  0.7 0.2 fusion.1
  0.9 0.6 pad_maximum_fusion.refs_4_
  1.5 0.7 convert_convert_fusion
  2.2 0.7 convert_convert_fusion.1
  2.9 0.7 convert_add_fusion
  3.5 1.4 concatenate.6
  5.6 0.6 broadcast_in_dim.8.refs_5_
  6.2 143.7 %shard_map.254 = (bf16[1024,1024]{1,0:T(8,128)(2,1)}, bf16[1024,1024]{1,0:T(8,128)(2,1)}, f32[16,16,128]{2,1,0:T(8,128)}, bf16[1024,1536]{1,0:T(8,128)(2,1)}, bf...) custom-call(s32[1]{0:T(128)S(6)} %copy.36.refs_0_, ...), custom_call_target="tpu_custom_call" | custom-call | tf_op jit(solution)/shard_map/pallas_call | solution.py:533
  149.8 0.6 broadcast_in_dim.9.refs_11_
  150.4 152.3 %shard_map.255 = (bf16[2048,256]{1,0:T(8,128)(2,1)}, bf16[2048,256]{1,0:T(8,128)(2,1)}, f32[2,32,1536]{2,1,0:T(8,128)}, f32[2,32,2048]{2,1,0:T(8,128)}, f32[2,64...) custom-call(bf16[1024,1024]{1,0:T(8,128)(2,1)} %get-tuple-element.32.refs_0_, ...), custom_call_target="tpu_custom_call" | custom-call | tf_op jit(solution)/shard_map/pallas_call | solution.py:1022
  302.8 0.0 copy-start.2
  302.8 0.0 copy-start.1
  302.8 0.0 copy-start.3
  302.8 0.8 dynamic-slice_bitcast_fusion
  303.7 0.0 copy-start.4
  303.7 1.5 fusion.2
  305.2 1.4 constant_dynamic-slice_fusion
  306.5 1.4 dynamic-slice_reduce_fusion
  307.9 0.5 copy.37
  308.4 0.0 copy-start
  308.4 2.3 copy.38
  310.7 2.3 copy.39
  313.0 0.0 copy-done.2
  313.0 0.7 copy.40
  313.7 0.0 copy-done.1
  313.7 0.8 copy.41
  314.5 0.0 copy-done.3
  314.5 0.7 copy.42
  315.2 0.0 copy-done.4
  315.2 0.0 copy-done
  315.2 0.8 copy.43
  (1 shorter events, 0.0 us)
Async XLA Ops:
  302.8 10.2 %copy-start.2 = (f32[2,32,1536]{2,1,0:T(8,128)S(1)}, f32[2,32,1536]{2,1,0:T(8,128)}, u32[]{:S(2)}) copy-start(f32[2,32,1536]{2,1,0:T(8,128)} %get-tuple-element.45) | copy-start | bytes 1179652
  302.8 10.9 %copy-start.1 = (f32[2,32,2048]{2,1,0:T(8,128)S(1)}, f32[2,32,2048]{2,1,0:T(8,128)}, u32[]{:S(2)}) copy-start(f32[2,32,2048]{2,1,0:T(8,128)} %get-tuple-element.47) | copy-start | bytes 1572868
  302.8 11.7 %copy-start.3 = (f32[2,64,256]{2,1,0:T(8,128)S(1)}, f32[2,64,256]{2,1,0:T(8,128)}, u32[]{:S(2)}) copy-start(f32[2,64,256]{2,1,0:T(8,128)} %get-tuple-element.48) | copy-start | bytes 393220
  303.7 11.5 %copy-start.4 = (f32[64]{0:T(128)}, f32[64]{0:T(128)S(1)}, u32[]{:S(2)}) copy-start(f32[64]{0:T(128)S(1)} %dynamic-slice_bitcast_fusion) | copy-start | bytes 772
  308.4 6.8 %copy-start = (f32[2,256,256]{2,1,0:T(8,128)S(1)}, f32[2,256,256]{2,1,0:T(8,128)}, u32[]{:S(2)}) copy-start(f32[2,256,256]{2,1,0:T(8,128)} %get-tuple-element.49) | copy-start | bytes 1572868

commit v4 on v3

v4 whole, which is shorter than its diff:
```python
import functools
import math

import jax
import jax.numpy as jnp
import numpy as np
from jax import lax
from jax.experimental import pallas as pl
from jax.experimental.pallas import tpu as pltpu
from jax.sharding import PartitionSpec as P

D = 1024
HD = 64
ROT = 16
FF = 4096
SEQ_LEN = 1024
EPS = 1e-05
NEGATIVE = -1e30
ROWS = 4
DPS = 4
MESH = pl.DeviceIdType.MESH
BF = jnp.bfloat16
F32 = jnp.float32


def places():
    dp, row, col = lax.axis_index("dp"), lax.axis_index("row"), lax.axis_index("col")
    across = dp + 1 - 2 * lax.rem(dp, 2)
    along = lax.rem(dp + 2, 4)
    return dp, row, col, across, along


def line_order(row):
    far = row // 2
    side = row + far * (3 - 2 * row)
    at = lambda place: far * 3 + (1 - 2 * far) * place
    return side, at


def greet(targets):
    barrier = pltpu.get_barrier_semaphore()
    for target in targets:
        pl.semaphore_signal(barrier, inc=1, device_id=target, device_id_type=MESH)
    pl.semaphore_wait(barrier, len(targets))


def peers_of(dp, row, col, cols):
    group = []
    for step in range(1, ROWS * cols):
        flat = lax.rem(row * cols + col + step, ROWS * cols)
        group.append((dp, flat // cols, lax.rem(flat, cols)))
    for step in range(1, DPS):
        for other in range(ROWS):
            group.append((lax.rem(dp + step, DPS), lax.rem(row + other, ROWS), col))
    return group


def remote(src, dst, send, recv, target):
    return pltpu.make_async_remote_copy(
        src_ref=src, dst_ref=dst, send_sem=send, recv_sem=recv, device_id=target, device_id_type=MESH
    )


N_W = 4
QKV, UP, DENSE, DOWN = range(N_W)
BEFORE = (
    "b1", "z10", "b0", "b3", "b2", "z20", "s10", "z11", "s11", "z12", "z30", "m", "s12", "z13", "s30", "t0", "z31",
    "p10", "p11", "s31", "s13", "s00", "p31", "z32", "t1", "p12", "p13", "s32", "z33", "s20", "d0", "z00", "p30",
    "z21", "s33", "N", "p32",
)
BETWEEN = (
    ("d1",),
    (),
    (),
    ("z01", "p33",),
    ("s01",),
    ("s21",),
    ("z02", "p00",),
    ("s02", "z22", "z23",),
    (),
    ("z03",),
    (),
    ("s23",),
    (),
    ("p23", "s22", "p20", "p21",),
    (),
    ("p22", "p02", "s03",),
    ("p01",),
    (),
    (),
    ("p03",),
)


def nt(left, right):
    return lax.dot_general(left, right, (((1,), (1,)), ((), ())), preferred_element_type=F32)


def nn(left, right):
    return jnp.dot(left, right, preferred_element_type=F32)


def span(start, size, unit):
    return pl.ds(pl.multiple_of(start, unit), size)


def slot(w, ref, row, dp, height, half=None):
    if w in (QKV, UP):
        if half is None:
            return ref.at[span((row * DPS + dp) * height, height, 64), :]
        return ref.at[span((row * DPS + dp) * height + half * (height // 2), height // 2, 32), :]
    if half is None:
        return ref.at[span(dp * height, height, 16), span(row * 256, 256, 256)]
    if w == DENSE:
        return ref.at[span(dp * height, height, 16), span(row * 256 + half * 128, 128, 128)]
    return ref.at[span(dp * height + half * (height // 2), height // 2, 16), span(row * 256, 256, 256)]


def half_of(w, ref, half):
    height = ref.shape[0]
    if w == DENSE:
        return ref.at[:, pl.ds(half * 128, 128)]
    return ref.at[pl.ds(half * (height // 2), height // 2), :]


def read_gains(smalls, gains):
    for r in range(ROWS):
        for g in range(4):
            for t in range(2):
                gains[g : g + 1, pl.ds(r * 256 + t * 128, 128)] = smalls[r * DPS, pl.ds(2 * g + t, 1), :]


def rounded(value):
    return value.astype(BF).astype(F32)


def read_bias(smalls, bias, first_row, size):
    per = size // 128
    for d in range(DPS):
        for t in range(per):
            bias[0:1, pl.ds(d * size + t * 128, 128)] = rounded(smalls[d, pl.ds(first_row + t, 1), :])


def norm_rows(x):
    center = jnp.mean(x, axis=1, keepdims=True)
    spread = jnp.mean(x * x, axis=1, keepdims=True) - center * center
    scale_inv = lax.rsqrt(spread + EPS)
    return (x - center) * scale_inv, scale_inv


def norm_stage(x_ref, gains, outs):
    def body(i, carry):
        rows = span(i * 128, 128, 128)
        normed, ignored = norm_rows(x_ref[rows, :].astype(F32))
        for which, plain, turned in outs:
            value = (normed * gains[which : which + 1, :] + gains[which + 1 : which + 2, :]).astype(BF)
            plain[rows, :] = value
            turned[:, rows] = value.T
        return carry

    lax.fori_loop(0, SEQ_LEN // 128, body, 0)


def project_stage(wq, first, bias_row, angles, q_t, k_t, v_t, heads):
    pair = min(heads, 2)
    width = 192 * pair

    def body(p, carry):
        cols = pl.ds(0, width) if heads == pair else span(p * width, width, 128)
        w_t = wq[:, cols].T
        bias = jnp.broadcast_to(bias_row[0:1, cols], (8, width)).T[:, 0:1]
        for j in range(SEQ_LEN // 256):
            toks = pl.ds(j * 256, 256)
            mixed = nt(w_t, first[toks, :]) + bias
            cos, sin = angles[0:8, toks], angles[8:16, toks]

            def turn(base):
                x1, x2 = mixed[base : base + 8], mixed[base + 8 : base + 16]
                return jnp.concatenate([x1 * cos - x2 * sin, x2 * cos + x1 * sin, mixed[base + 16 : base + 64]], axis=0)

            for e in range(pair):
                base, h = 192 * e, pair * p + e
                q_t[h, :, toks] = (turn(base) * HD ** (-0.5)).astype(BF)
                k_t[h, :, toks] = turn(base + 64).astype(BF)
                v_t[h, :, toks] = mixed[base + 128 : base + 192].astype(BF)
        return carry

    lax.fori_loop(0, heads // pair, body, 0)


def upstream_stage(wd, c_ref, up_t, heads):
    for j in range(SEQ_LEN // 256):
        toks = pl.ds(j * 256, 256)
        grad = nt(wd[...], c_ref[toks, :]).astype(BF)
        for h in range(heads):
            up_t[h, :, toks] = grad[HD * h : HD * (h + 1)]


def attend_head(h, prefix, angles, q_t, k_t, v_t, up_t, att_t, gm_t, grad_q, grad_k, grad_v, middle):
    keys_plain, values_plain = k_t[h].T, v_t[h].T
    done = 0
    for i in range(SEQ_LEN // 256):
        if i == 2:
            middle()
        low = 256 * i
        seen = max(512, low + 256)
        spot = pl.ds(low, 256)
        q, up = q_t[h, :, spot], up_t[h, :, spot]
        scores = nn(keys_plain[0:seen], q)
        plain = min(low, seen)
        keys = lax.broadcasted_iota(jnp.int32, (seen - plain, 256), 0) + plain
        queries = lax.broadcasted_iota(jnp.int32, (seen - plain, 256), 1) + low
        masked = jnp.where((keys <= queries) | (keys < prefix), scores[plain:], NEGATIVE)
        scores = jnp.concatenate([scores[:plain], masked], axis=0) if plain else masked
        exponent = jnp.exp(scores - jnp.max(scores, axis=0, keepdims=True))
        probs = exponent * (1.0 / jnp.sum(exponent, axis=0, keepdims=True))
        weights = probs.astype(BF)
        att_t[h, :, spot] = nn(v_t[h, :, 0:seen], weights).astype(BF)
        grad_probs = nn(values_plain[0:seen], up)
        inner = jnp.sum(probs * grad_probs, axis=0, keepdims=True)
        grad_scores = (probs * (grad_probs - inner)).astype(BF)
        grad_q[:, spot] = nn(k_t[h, :, 0:seen], grad_scores)
        for total, part in ((grad_v, nt(up, weights)), (grad_k, nt(q, grad_scores))):
            if done:
                total[:, 0:done] += part[:, :done]
            if seen > done:
                total[:, done:seen] = part[:, done:]
        done = seen
    cos, sin = angles[0:8, :], angles[8:16, :]

    def turn_back(grad):
        g1, g2 = grad[0:8], grad[8:16]
        return jnp.concatenate([g1 * cos + g2 * sin, g2 * cos - g1 * sin, grad[16:]], axis=0)

    base = h * 192
    gm_t[span(base, HD, HD), :] = (turn_back(grad_q[...]) * HD ** (-0.5)).astype(BF)
    gm_t[span(base + HD, HD, HD), :] = turn_back(grad_k[...]).astype(BF)
    gm_t[span(base + 2 * HD, HD, HD), :] = grad_v[...].astype(BF)


def gelu_parts(x):
    below = 0.5 * (1.0 + lax.erf(x * (0.5**0.5)))
    density = jnp.exp(-0.5 * x * x) * (1.0 / math.sqrt(2.0 * math.pi))
    return x * below, below + x * density


def gather_kernel(cols, aligned, *refs):
    (tok_ref, cot_ref, small_ref, bias_in) = refs[:4]
    masters = refs[4:8]
    (x_out, c_out, smalls_out, gq_ref, gd_ref, first_out, first_t_out, gu_out, gp_out, branch_out, comb_out, sum_out) = refs[8:20]
    own = refs[20:24]
    stage = refs[24:28]
    (x_ref, c_ref, smalls, wu, wp, gains, bias_row, second, second_t) = refs[28:37]
    (hidden, slope, ghp, gu, gp, branch, comb) = refs[37:44]
    (z_send, z_recv, s1_send, s1_recv, s2_send, s2_recv, t_send, t_recv, a_send, a_recv, m_send, m_recv, l_sem) = refs[44:]
    full = (gq_ref, wu, gd_ref, wp)
    n_q, n_u = gq_ref.shape[1], wu.shape[1]
    width = ghp.shape[1]
    blocks = n_u // width
    dp, row, col, across, along = places()
    side, at = line_order(row)
    order = [row, at(1 - side), at(2), at(3)]
    middle = side == 1
    tok_col = tok_ref.shape[0]
    part = SEQ_LEN // cols
    chunk = min(tok_col, SEQ_LEN)
    n_seq = tok_col // chunk
    n_part = chunk // part

    loads = [pltpu.make_async_copy(masters[w], stage[w], l_sem.at[w]) for w in range(N_W)]
    for load in loads:
        load.start()
    greet(peers_of(dp, row, col, cols))

    def token_copy(kind, j, i):
        src_ref, dst_ref = ((tok_ref, x_ref), (cot_ref, c_ref))[kind]
        n = j * n_part + i
        if n_seq > 1:
            j = lax.rem(j + (n_seq - 1) * (1 - col), n_seq)
        start = col * tok_col + j * chunk
        to_row = start // SEQ_LEN
        piece = lax.rem(start, SEQ_LEN) // part + i
        src = src_ref.at[span(j * chunk + i * part, part, part), :]
        dst = dst_ref.at[span(piece * part, part, part), span(row * 256, 256, 256)]
        sends, recvs = t_send.at[kind, n], t_recv.at[kind, row]
        is_here = jnp.logical_and(to_row == row, piece == col)
        far = remote(src, dst, sends, recvs, (dp, to_row, piece))
        near = pltpu.make_async_copy(src, dst, recvs)
        return is_here, far, near

    def token_start(kind):
        for j in range(n_seq):
            for i in range(n_part):
                is_here, far, near = token_copy(kind, j, i)
                pl.when(jnp.logical_not(is_here))(far.start)
                pl.when(is_here)(near.start)

    def part_rows(piece):
        return span(piece * part, part, part)

    def spread_copy(kind, step):
        mine = (x_ref, c_ref)[kind].at[part_rows(col), :]
        to_col = lax.rem(col + step, cols)
        return remote(mine, mine, a_send.at[kind, step - 1], a_recv.at[kind, step - 1], (dp, row, to_col))

    def token_spread(kind):
        dst_ref = (x_ref, c_ref)[kind]
        for other in range(ROWS):
            block = dst_ref.at[part_rows(col), pl.ds(other * 256, 256)]
            pltpu.make_async_copy(block, block, t_recv.at[kind, other]).wait()
        for step in range(1, cols):
            spread_copy(kind, step).start()

    def token_finish(kind):
        dst_ref = (x_ref, c_ref)[kind]
        for step in range(1, cols):
            from_col = lax.rem(col + cols - step, cols)
            theirs = dst_ref.at[part_rows(from_col), :]
            pltpu.make_async_copy(theirs, theirs, a_recv.at[kind, step - 1]).wait()

    def token_drain(kind):
        for j in range(n_seq):
            for i in range(n_part):
                is_here, far, near = token_copy(kind, j, i)
                pl.when(jnp.logical_not(is_here))(far.wait_send)
        for step in range(1, cols):
            spread_copy(kind, step).wait_send()

    me = row * DPS + dp

    def small_copy(step):
        flat = lax.rem(me + step, ROWS * DPS)
        return remote(
            small_ref, smalls.at[me], m_send.at[step - 1], m_recv.at[step - 1], (lax.rem(flat, DPS), flat // DPS, col)
        )

    def place(w, r, d, half=None):
        return slot(w, full[w], r, d, own[w].shape[0], half)

    def source(w, k, half=None):
        if k == 0:
            return own[w] if half is None else half_of(w, own[w], half)
        return place(w, order[k], dp, half)

    def line_copies(w, k):
        src = source(w, k)
        dst = place(w, order[k], dp)
        recv = z_recv.at[w, order[k]]
        if k == 0:
            return [
                (None, remote(src, dst, z_send.at[w, 0], recv, (dp, at(1 - side), col))),
                (middle, remote(src, dst, z_send.at[w, 1], recv, (dp, at(2), col))),
            ]
        onward = at(2) if k == 1 else at(0)
        return [(middle, remote(src, dst, z_send.at[w, k + 1], recv, (dp, onward, col)))]

    def first_copies(w, k):
        out = []
        for half, target in ((0, across), (1, along)):
            out.append(
                remote(source(w, k, half), place(w, order[k], dp, half), s1_send.at[w, k, half],
                       s1_recv.at[w, k, half], (target, row, col))
            )
        return out

    def second_copies(w, k, which):
        out = []
        for half, target, other in ((0, along, across), (1, across, along)):
            if which == 0:
                src, owner = source(w, k, half), dp
            else:
                src, owner = place(w, order[k], other, half), other
            out.append(
                remote(src, place(w, order[k], owner, half), s2_send.at[w, k, which, half],
                       s2_recv.at[w, k, which, half], (target, row, col))
            )
        return out

    def onward(w, k):
        if k > 0:
            block = place(w, order[k], dp)
            pltpu.make_async_copy(block, block, z_recv.at[w, order[k]]).wait()
        for cond, copy in line_copies(w, k):
            if cond is None:
                copy.start()
            else:
                pl.when(cond)(copy.start)

    def sideways(w, k):
        for copy in first_copies(w, k) + second_copies(w, k, 0):
            copy.start()

    def arrived(w, k):
        onward(w, k)
        sideways(w, k)

    def passed(w, k):
        for copy in first_copies(w, k):
            copy.wait_recv()
        for copy in second_copies(w, k, 1):
            copy.start()

    def finished(w):
        for k in range(ROWS):
            for which in range(2):
                for copy in second_copies(w, k, which):
                    copy.wait_recv()

    def drained(w, k):
        for cond, copy in line_copies(w, k):
            if cond is None:
                copy.wait_send()
            else:
                pl.when(cond)(copy.wait_send)
        for copy in first_copies(w, k) + second_copies(w, k, 0) + second_copies(w, k, 1):
            copy.wait_send()

    def home(w):
        return pltpu.make_async_copy(own[w], place(w, row, dp), l_sem.at[w])

    def begin(w):
        loads[w].wait()
        own[w][...] = stage[w][...].astype(BF)
        home(w).start()

    small_home = pltpu.make_async_copy(small_ref, smalls.at[me], l_sem.at[N_W])
    kept = []

    def keep(src, dst):
        copy = pltpu.make_async_copy(src, dst, l_sem.at[N_W + 1 + len(kept)])
        copy.start()
        kept.append(copy)

    def smalls_start():
        small_home.start()
        for step in range(1, ROWS * DPS):
            small_copy(step).start()

    def norm():
        small_home.wait()
        for step in range(1, ROWS * DPS):
            small_copy(step).wait()
        read_gains(smalls, gains)
        if aligned:
            read_bias(smalls, bias_row, 9 + n_q // (DPS * 128), n_u // DPS)
        else:
            bias_row[...] = bias_in[...]
        branch[...] = jnp.zeros(branch.shape, F32)
        comb[...] = jnp.zeros(comb.shape, F32)
        token_finish(0)
        first, first_t = hidden.at[:, pl.ds(0, D)], hidden.at[:, pl.ds(D, D)]
        norm_stage(x_ref, gains, ((0, first, first_t), (2, second, second_t)))
        keep(x_ref, x_out)
        keep(smalls, smalls_out)
        keep(first, first_out)
        keep(first_t, first_t_out)

    def act(word):
        kind, rest = word[0], [int(d) for d in word[1:]]
        {
            "b": begin, "z": onward, "s": sideways, "p": passed, "t": token_start, "d": token_spread, "m": smalls_start,
            "N": norm,
        }[kind](*rest)

    def serve_at(when, unit):
        if blocks == DPS and BETWEEN[unit]:

            @pl.when(when)
            def _():
                for word in BETWEEN[unit]:
                    act(word)

    for word in BEFORE:
        act(word)
    if blocks < DPS:
        for words in BETWEEN:
            for word in words:
                act(word)
    home(UP).wait()
    finished(UP)
    for copy in kept[2:4]:
        copy.wait()

    def forward_block(n, carry):
        cut = span(n * width, width, width)

        def body(j, carry):
            rows = span(j * 256, 256, 256)
            value, slant = gelu_parts(nn(second[rows, :], wu[:, cut]) + bias_row[0:1, cut])
            hidden[rows, cut] = value.astype(BF)
            slope[rows, cut] = slant
            return carry

        lax.fori_loop(0, SEQ_LEN // 256, body, 0)
        for m in range(DPS):
            serve_at(n == m, m)
        return carry

    lax.fori_loop(0, blocks, forward_block, 0)
    token_finish(1)
    keep(c_ref, c_out)
    h = gp.shape[3]

    def down_block(n, carry):
        cut = span(n * width, width, width)
        turned = hidden[:, cut].T
        if blocks == DPS:
            for half in range(2):
                gp[n // 2, lax.rem(n, 2), half] = nn(turned[half * h : (half + 1) * h, :], c_ref[...]).astype(BF)
        else:
            gp[...] = nn(turned, c_ref[...]).astype(BF).reshape(2, 2, 2, h, D)
        for m in range(DPS):
            serve_at(n == m, DPS + m)
        return carry

    lax.fori_loop(0, blocks, down_block, 0)
    keep(gp, gp_out)
    home(DOWN).wait()
    finished(DOWN)
    sum_out[...] = jnp.zeros(sum_out.shape, F32)

    def backward_block(n, carry):
        cut = span(n * width, width, width)

        def body(j, carry):
            rows = span(j * 256, 256, 256)
            grad = (nt(c_ref[rows, :], wp[cut, :]) * slope[rows, cut]).astype(BF)
            ghp[rows, :] = grad
            branch[rows, :] += nn(hidden[rows, cut], wp[cut, :])
            comb[rows, :] += nt(grad, wu[:, cut])
            sum_out[0:1, cut] += jnp.sum(grad.astype(F32), axis=0, keepdims=True)
            return carry

        for part_of in range(2):
            lax.fori_loop(2 * part_of, 2 * part_of + 2, body, 0)
            for m in range(DPS):
                serve_at(n == m, 2 * DPS + 3 * m + part_of)

        def up_body(r, carry):
            value = nn(second_t[span(r * 256, 256, 256), :], ghp[...]).astype(BF)
            gu[r, :, :, :, :, cut] = value.reshape(2, 2, 2, 32, width)
            return carry

        lax.fori_loop(0, ROWS, up_body, 0)
        for m in range(DPS):
            serve_at(n == m, 2 * DPS + 3 * m + 2)
        return carry

    lax.fori_loop(0, blocks, backward_block, 0)
    for src, dst in ((gu, gu_out), (branch, branch_out), (comb, comb_out)):
        keep(src, dst)
    for w in (QKV, DENSE):
        home(w).wait()
        finished(w)
    for w in range(N_W):
        for k in range(ROWS):
            drained(w, k)
    for kind in range(2):
        token_drain(kind)
    for copy in kept[:2] + kept[4:]:
        copy.wait()


def gather(tokens_in, cotangent, small, bias, weights, cols, aligned):
    wq, wu, wd, wp = weights
    n_q, n_u = wq.shape[1], wu.shape[1]
    att_width, h_p = wd.shape[0] * DPS, wp.shape[0]
    width = 512 if n_u == DPS * 512 else n_u
    any_spec = pl.BlockSpec(memory_space=pl.ANY)
    vmem = pl.BlockSpec(memory_space=pltpu.VMEM)
    shape = jax.ShapeDtypeStruct
    smalls = (ROWS * DPS,) + small.shape
    square = (SEQ_LEN, D)
    up_shape, down_shape = (ROWS, 2, 2, 2, 32, n_u), (2, 2, 2, h_p // 2, D)
    out_shape = [
        shape(square, BF), shape(square, BF), shape(smalls, F32), shape((D, n_q), BF), shape((att_width, D), BF),
        shape(square, BF), shape(square, BF), shape(up_shape, BF), shape(down_shape, BF), shape(square, F32),
        shape(square, F32), shape((1, n_u), F32),
    ]
    tok_col = tokens_in.shape[0]
    pieces = tok_col // (SEQ_LEN // cols)
    dma = pltpu.SemaphoreType.DMA
    buf = pltpu.VMEM
    scratch = [buf(w.shape, BF) for w in weights] + [buf(w.shape, F32) for w in weights]
    scratch += [
        buf(square, BF), buf(square, BF), buf(smalls, F32), buf((D, n_u), BF), buf((n_u, D), BF),
        buf((8, D), F32), buf((1, n_u), F32), buf(square, BF), buf(square, BF),
        buf((SEQ_LEN, max(n_u, 2 * D)), BF), buf((SEQ_LEN, n_u), F32), buf((SEQ_LEN, width), BF), buf(up_shape, BF), buf(down_shape, BF), buf(square, F32),
        buf(square, F32),
        dma((N_W, 5)), dma((N_W, 4)), dma((N_W, 4, 2)), dma((N_W, 4, 2)), dma((N_W, 4, 2, 2)), dma((N_W, 4, 2, 2)),
        dma((2, pieces)), dma((2, 4)), dma((2, cols - 1)), dma((2, cols - 1)),
        dma((ROWS * DPS - 1,)), dma((ROWS * DPS - 1,)), dma((N_W + 10,)),
    ]
    return pl.pallas_call(
        functools.partial(gather_kernel, cols, aligned),
        out_shape=out_shape,
        in_specs=[any_spec] * 3 + [vmem] + [any_spec] * 4,
        out_specs=[any_spec] * 11 + [vmem],
        scratch_shapes=scratch,
        compiler_params=pltpu.CompilerParams(collective_id=0, has_side_effects=True, vmem_limit_bytes=60 << 20),
    )(tokens_in, cotangent, small, bias, wq, wu, wd, wp)


BEFORE_HEADS = (
    "f0", "f1", "J", "f2", "U",
)
AMONG_HEADS = (
    (),
    (),
    (),
    ("g0", "f3",),
    (),
    (),
    (),
    ("g1",),
    ("f4",),
    ("h0", "g2",),
    (),
    ("h1", "g3", "g4", "q0",),
    (),
    ("h2", "h3",),
    (),
    ("f5", "q1",),
)
AFTER_HEADS = (
    "q2", "h4", "T", "q3", "r0", "q4", "r1", "g5", "f6", "u0", "X", "W", "g6", "r2", "f7", "u1", "f8", "h5", "G",
    "g7", "h6", "Y", "g8", "f9", "u2", "r3", "h7", "f10", "q5", "h8", "v0", "q6", "g9", "v1", "f11", "v2", "q7",
    "h9", "u3", "g10", "h10", "g11", "q8", "r4", "r5", "q9", "r6", "u4", "v3", "u5", "r7", "r8", "q10", "h11",
    "q11", "u6", "u7", "u8", "r9", "u9", "r10", "v4", "u10", "r11", "u11",
)
PIECES = 12


def add_into(dst, src):
    shape = dst.shape
    outer, height = shape[:-2], shape[-2]
    step = min(32, height)
    per = height // step
    total = math.prod(outer) * per

    def body(i, carry):
        index, rest = [], i // per
        for size in reversed(outer):
            index.append(lax.rem(rest, size))
            rest = rest // size
        where = tuple(reversed(index)) + (span(lax.rem(i, per) * step, step, step),)
        dst[where] = (dst[where].astype(F32) + src[where].astype(F32)).astype(BF)
        return carry

    lax.fori_loop(0, total, body, 0)


def pieces_of(n_q, n_u, h_d, h_p):
    out = []

    def columns(w, n):
        size = 512 if n % 512 == 0 else n
        out.extend((w, start, size) for start in range(0, n, size))

    columns(UP, n_u)
    half = h_p // 2
    size = 64 if half % 64 == 0 else half
    out.extend((DOWN, start, size) for start in range(0, half, size))
    out.append((DENSE, 0, h_d // 2))
    columns(QKV, n_q)
    return out


def scatter_kernel(cols, aligned, pieces, *refs):
    n_p = len(pieces)
    (prefix_ref, smalls, angles, bias_in, sum_u, x_in, c_in, wq_in, wd_in, first_in, first_t_in, gu_in, gp_in, branch_in,
     comb_in) = refs[:15]
    (lo_out, gt_out, oq, ou, od, op, sm_out) = refs[15:22]
    (wq, wd, x_ref, c_ref, first, first_t, q_t, k_t, v_t, up_t, att_t, gm_t, grad_q, grad_k, grad_v) = refs[22:37]
    (gq, gd, att, total_ref, branch_got, comb_got, gains, bias_row, out_bias, sm, sm_got, gain_sum) = refs[37:49]
    mine_u, mine_p = refs[49:51], refs[51:53]
    base = 53

    def buffers(start):
        return [refs[start + 2 * i : start + 2 * i + 2] for i in range(n_p)]

    got1, got2, got_end, got_mid = [buffers(base + 2 * n_p * n) for n in range(4)]
    (l_sem, f_sem, s1_send, s1_recv, s2_send, s2_recv, e_send, e_recv, m_send, m_recv, b_send, b_recv, d_send, d_recv,
     t_send, t_recv, v_send, v_recv) = refs[base + 8 * n_p :]
    dp, row, col, across, along = places()
    x, y = lax.rem(dp, 2), dp // 2
    side, at = line_order(row)
    far_end = row // 2
    middle, end = side == 1, side == 0
    n_q, n_u = wq_in.shape[1], sum_u.shape[1]
    heads = q_t.shape[0]
    tok_col = lo_out.shape[0]
    part = SEQ_LEN // cols

    def load(src, dst, n):
        return pltpu.make_async_copy(src, dst, l_sem.at[n])

    loads = [load(first_in, first, 0), load(wq_in, wq, 1), load(wd_in, wd, 2), load(c_in, c_ref, 3), load(first_t_in, first_t, 4),
             load(x_in, x_ref, 5), load(branch_in, total_ref, 6)]
    for one in loads:
        one.start()
    group = [(dp, lax.rem(row + step, ROWS), lax.rem(col + other, cols)) for step in range(ROWS) for other in range(cols)]
    greet([(across, row, col), (along, row, col)] + group[1:])

    def view(i, half, other):
        w, start, size = pieces[i]
        if half == 0:
            place_y, place_x = (1 - y if other else y), slice(None)
        else:
            place_y, place_x = slice(None), (1 - x if other else x)
        cut = pl.ds(start, size)
        if w in (QKV, UP):
            if w == UP and not other:
                return mine_u[half].at[:, :, :, cut]
            return (gu_in if w == UP else gq).at[:, place_y, place_x, half, :, cut]
        if w == DOWN and not other:
            return mine_p[half].at[:, cut, :]
        return (gp_in if w == DOWN else gd).at[place_y, place_x, half, cut, :]

    def fetch(i, half):
        w, start, size = pieces[i]
        place_y, place_x = (y, slice(None)) if half == 0 else (slice(None), x)
        cut = pl.ds(start, size)
        src = gu_in.at[:, place_y, place_x, half, :, cut] if w == UP else gp_in.at[place_y, place_x, half, cut, :]
        return pltpu.make_async_copy(src, view(i, half, False), f_sem.at[i, half])

    def first_copy(i, half):
        target = along if half == 0 else across
        return remote(view(i, half, True), got1[i][half], s1_send.at[i, half], s1_recv.at[i, half], (target, row, col))

    def keep(i, half, other):
        which = x if half == 0 else y
        which = 1 - which if other else which
        kept = view(i, half, False)
        return kept.at[:, which] if pieces[i][0] in (QKV, UP) else kept.at[which]

    def second_copy(i, half):
        target = across if half == 0 else along
        return remote(keep(i, half, True), got2[i][half], s2_send.at[i, half], s2_recv.at[i, half], (target, row, col))

    def lines(i, ref, start, count):
        if pieces[i][0] in (QKV, UP):
            return ref.at[pl.ds(start, count)]
        return ref.at[:, span(start * 256, count * 256, 256)]

    def end_copy(i, half):
        src = lines(i, keep(i, half, False), 1 - far_end, 3)
        return remote(src, got_end[i][half], e_send.at[i, half], e_recv.at[i, half], (dp, at(1), col))

    def mid_copy(i, half):
        src = lines(i, keep(i, half, False), 2 * (1 - far_end), 2)
        return remote(src, got_mid[i][half], m_send.at[i, half], m_recv.at[i, half], (dp, at(2), col))

    def back_copy(i, half):
        src = lines(i, keep(i, half, False), at(0), 1)
        return remote(src, lines(i, got_mid[i][half], 0, 1), b_send.at[i, half], b_recv.at[i, half], (dp, at(0), col))

    def begin(i):
        for half in range(2):
            first_copy(i, half).start()
            if pieces[i][0] in (UP, DOWN):
                fetch(i, half).start()

    def stage_two(i):
        for half in range(2):
            if pieces[i][0] in (UP, DOWN):
                fetch(i, half).wait()
            first_copy(i, half).wait_recv()
            add_into(view(i, half, False), got1[i][half])
            second_copy(i, half).start()

    def stage_three(i):
        for half in range(2):
            second_copy(i, half).wait_recv()
            add_into(keep(i, half, False), got2[i][half])

            @pl.when(end)
            def _():
                end_copy(i, half).start()

    def stage_four(i):
        @pl.when(middle)
        def _():
            for half in range(2):
                end_copy(i, half).wait_recv()
                add_into(lines(i, keep(i, half, False), 2 * (1 - far_end), 2), lines(i, got_end[i][half], 1 - far_end, 2))
                mid_copy(i, half).start()

    def stage_five(i):
        @pl.when(middle)
        def _():
            for half in range(2):
                mid_copy(i, half).wait_recv()
                add_into(lines(i, keep(i, half, False), at(0), 1), lines(i, got_mid[i][half], far_end, 1))
                back_copy(i, half).start()

    def stage_six(i):
        w, start, size = pieces[i]
        out = (oq, ou, od, op)[w]
        for half in range(2):
            mine = lines(i, keep(i, half, False), row, 1)

            def total(others):
                if w in (QKV, UP):
                    value = mine[0].astype(F32)
                    for other in others:
                        value = value + other[0].astype(F32)
                    out[half, :, pl.ds(start, size)] = value
                else:
                    value = mine[...].astype(F32)
                    for other in others:
                        value = value + other[...].astype(F32)
                    out[half, pl.ds(start, size), :] = value

            @pl.when(end)
            def _():
                back_copy(i, half).wait_recv()
                total([lines(i, got_mid[i][half], 0, 1)])

            @pl.when(middle)
            def _():
                total([lines(i, got_end[i][half], 2 * far_end, 1), lines(i, got_mid[i][half], 1 - far_end, 1)])

    def drain(i):
        for half in range(2):
            first_copy(i, half).wait_send()
            second_copy(i, half).wait_send()

            @pl.when(end)
            def _():
                end_copy(i, half).wait_send()

            @pl.when(middle)
            def _():
                mid_copy(i, half).wait_send()
                back_copy(i, half).wait_send()

    def part_rows(piece):
        return span(piece * part, part, part)

    def col_copy(kind, n):
        other = lax.rem(col + n, cols)
        src = total_ref.at[part_rows(other), :]
        dst = (branch_got, comb_got)[kind].at[n - 1]
        return remote(src, dst, d_send.at[kind, n - 1], d_recv.at[kind, n - 1], (dp, row, other))

    start = row * SEQ_LEN + col * part
    owner, offset = start // tok_col, lax.rem(start, tok_col)

    def out_copy(kind, r):
        src = first.at[pl.ds(kind * part, part), span(r * 256, 256, 256)]
        dst = (lo_out, gt_out)[kind].at[span(offset, part, part), :]
        recv = t_recv.at[kind, offset // part]
        here = jnp.logical_and(row == r, owner == col)
        far = remote(src, dst, t_send.at[kind, r], recv, (dp, r, owner))
        return here, far, pltpu.make_async_copy(src, dst, recv)

    def out_start(kind):
        for r in (at(1 - side), at(2), at(3), row):
            here, far, near = out_copy(kind, r)
            pl.when(jnp.logical_not(here))(far.start)
            pl.when(here)(near.start)

    def out_finish(kind):
        for r in range(ROWS):
            here, far, near = out_copy(kind, r)
            pl.when(jnp.logical_not(here))(far.wait_send)
        out = (lo_out, gt_out)[kind]
        for n in range(tok_col // part):
            block = out.at[pl.ds(n * part, part), :]
            pltpu.make_async_copy(block, block, t_recv.at[kind, n]).wait()

    height = min(128, part)

    def finish_rows(kind):
        for n in range(1, cols):
            col_copy(kind, n).wait_recv()

        def body(i, carry):
            here = span(i * height, height, height)
            rows = span(col * part + i * height, height, height)
            value = total_ref[rows, :]
            for n in range(1, cols):
                value = value + (branch_got, comb_got)[kind][n - 1, here, :]
            wide = x_ref[rows, :].astype(F32)
            if kind == 0:
                value = wide + value + out_bias[0:1, :]
            else:
                normed, scale_inv = norm_rows(wide)
                mean = jnp.mean(value, axis=1, keepdims=True)
                cross = jnp.mean(value * normed, axis=1, keepdims=True)
                value = c_ref[rows, :].astype(F32) + scale_inv * (value - mean - normed * cross)
            first[span(kind * part + i * height, height, height), :] = value.astype(BF)
            return carry

        lax.fori_loop(0, part // height, body, 0)

    def small_copy(n):
        if n < 2:
            return remote(sm.at[n], sm_got.at[n], v_send.at[n], v_recv.at[n], ((across, along)[n], row, col))
        if n < 5:
            target = (dp, lax.rem(row + n - 1, ROWS), col)
            return remote(sm.at[2], sm_got.at[n], v_send.at[n], v_recv.at[n], target)
        target = (dp, row, lax.rem(col + n - 4, cols))
        return remote(sm.at[3], sm_got.at[n], v_send.at[n], v_recv.at[n], target)

    def small_step(n):
        if n > 0:
            waits = ((0,), (1,), (2, 3, 4), tuple(range(5, 4 + cols)))[n - 1]
            for m in waits:
                small_copy(m).wait_recv()
            value = sm[n - 1]
            if n < 4:
                for m in waits:
                    value = value + sm_got[m]
                sm[n] = value
            else:
                sm_out[...] = value
                value = value[0:4]
                for m in waits:
                    value = value + sm_got[m, 0:4, :]
                sm_out[0:4, :] = value
        for m in ((0,), (1,), (2, 3, 4), tuple(range(5, 4 + cols)), ())[n]:
            small_copy(m).start()

    def project():
        read_gains(smalls, gains)
        lanes = lax.broadcasted_iota(jnp.int32, (1, 128), 1)
        for r in range(ROWS):
            for d in range(0, DPS, 2):
                both = [rounded(smalls[r * DPS + d + n, 8:9, :]) for n in range(2)]
                both = [value + pltpu.roll(value, 64, 1) for value in both]
                out_bias[0:1, pl.ds(r * 256 + d * 64, 128)] = jnp.where(lanes < 64, both[0], both[1])
        if aligned:
            read_bias(smalls, bias_row, 9, n_q // DPS)
        else:
            bias_row[...] = bias_in[...]
        sm[0] = jnp.zeros(sm.shape[1:], F32)
        sm[0, 6:7, 0:n_u] = sum_u[...]
        loads[0].wait()
        loads[1].wait()
        project_stage(wq, first, bias_row, angles, q_t, k_t, v_t, heads)

    def upstream():
        loads[2].wait()
        loads[3].wait()
        upstream_stage(wd, c_ref, up_t, heads)

    def attended():
        group_h = min(heads, 4)

        def turn_body(i, carry):
            block = att_t[pl.ds(i * group_h, group_h)].reshape(group_h * HD, SEQ_LEN)
            spot = pl.ds(0, group_h * HD) if heads == group_h else span(i * group_h * HD, group_h * HD, 128)
            att[:, spot] = block.T
            return carry

        lax.fori_loop(0, heads // group_h, turn_body, 0)
        loads[6].wait()

        def out_body(j, carry):
            rows = span(j * 256, 256, 256)
            total_ref[rows, :] += nn(att[rows, :], wd[...])
            return carry

        lax.fori_loop(0, SEQ_LEN // 256, out_body, 0)
        for n in range(1, cols):
            col_copy(0, n).start()

    def weight_grads():
        all_heads = att_t[...].reshape(heads * HD, SEQ_LEN)
        gd[...] = nn(all_heads, c_ref[...]).astype(BF).reshape(gd.shape)
        loads[4].wait()
        wide = min(512, n_q)

        def qkv_body(r, carry):
            rows = span(r * 256, 256, 256)
            for n in range(n_q // wide):
                cut = pl.ds(n * wide, wide)
                gq[r, :, :, :, :, cut] = nt(first_t[rows, :], gm_t[cut, :]).astype(BF).reshape(2, 2, 2, 32, wide)
            return carry

        lax.fori_loop(0, ROWS, qkv_body, 0)

    load_comb = load(comb_in, total_ref, 6)

    def output_home():
        loads[5].wait()
        finish_rows(0)
        out_start(0)
        for n in range(1, cols):
            col_copy(0, n).wait_send()
        load_comb.start()

    def features():
        load_comb.wait()
        for n in range(8):
            gain_sum[n : n + 1, :] = jnp.zeros((1, D), F32)

        def body(j, carry):
            rows = span(j * 256, 256, 256)
            grad = gm_t[:, rows].T
            grad_first = nt(grad, wq[...])
            grad_second = total_ref[rows, :]
            normed, ignored = norm_rows(x_ref[rows, :].astype(F32))
            for n, value in enumerate((normed * grad_first, grad_first, normed * grad_second, grad_second,
                                       c_ref[rows, :].astype(F32))):
                gain_sum[n : n + 1, :] += jnp.sum(value, axis=0, keepdims=True)
            sm[0, 5:6, 0:n_q] += jnp.sum(grad.astype(F32), axis=0, keepdims=True)
            total_ref[rows, :] = gains[0:1, :] * grad_first + gains[2:3, :] * grad_second
            return carry

        lax.fori_loop(0, SEQ_LEN // 256, body, 0)
        for n in range(1, cols):
            col_copy(1, n).start()
        sm[0, 0:5, 0:D] = gain_sum[0:5, :]

    def gradient_home():
        finish_rows(1)
        out_start(1)

    stages = {"f": begin, "g": stage_two, "h": stage_three, "q": stage_four, "r": stage_five, "u": stage_six}
    others = {"J": project, "U": upstream, "T": attended, "W": weight_grads, "X": output_home, "G": features, "Y": gradient_home}

    def act(word):
        kind, rest = word[0], word[1:]
        if kind in others:
            others[kind]()
        elif kind == "v":
            small_step(int(rest))
        else:
            stages[kind](int(rest))

    plan = (BEFORE_HEADS, AMONG_HEADS, AFTER_HEADS)
    if n_p != PIECES:
        late = [i for i in range(n_p) if pieces[i][0] in (QKV, DENSE)]
        early = [i for i in range(n_p) if i not in late]
        after = ["T", "W", "X", "G", "Y"] + ["f%d" % i for i in late] + [s + str(i) for s in "ghqru" for i in range(n_p)]
        plan = (["f%d" % i for i in early] + ["J", "U"], ((),) * 16, after + ["v%d" % i for i in range(5)])
    before_heads, among_heads, after_heads = plan

    def serve_at(when, unit):
        if among_heads[unit]:

            @pl.when(when)
            def _():
                for word in among_heads[unit]:
                    act(word)

    for word in before_heads:
        act(word)
    prefix = prefix_ref[0]
    units = len(among_heads) // 2

    def head_body(h, carry):
        for n in range(min(units, heads)):
            serve_at(h == n, 2 * n)

        def middle():
            for n in range(min(units, heads)):
                serve_at(h == n, 2 * n + 1)

        attend_head(h, prefix, angles, q_t, k_t, v_t, up_t, att_t, gm_t, grad_q, grad_k, grad_v, middle)
        return carry

    lax.fori_loop(0, heads, head_body, 0)
    for unit in range(2 * min(units, heads), 2 * units):
        for word in among_heads[unit]:
            act(word)
    for word in after_heads:
        act(word)
    for i in range(n_p):
        drain(i)
    for kind in range(2):
        out_finish(kind)
    for n in range(1, cols):
        col_copy(1, n).wait_send()
    for n in range(4 + cols):
        small_copy(n).wait_send()


def scatter(prefix_len, smalls, angles, bias, sum_u, own_x, own_cot, wq, wd, first, first_t, gu, gp, branch, comb, cols, aligned,
            tok_col):
    any_spec = pl.BlockSpec(memory_space=pl.ANY)
    vmem = pl.BlockSpec(memory_space=pltpu.VMEM)
    smem = pl.BlockSpec(memory_space=pltpu.SMEM)
    dma = pltpu.SemaphoreType.DMA
    buf = pltpu.VMEM
    shape = jax.ShapeDtypeStruct
    n_q, n_u = wq.shape[1], sum_u.shape[1]
    heads = n_q // 192
    h_d, h_p = wd.shape[0] // DPS, 2 * gp.shape[3]
    pieces = pieces_of(n_q, n_u, h_d, h_p)
    n_p = len(pieces)
    part = SEQ_LEN // cols
    line = max(n_q, n_u, D)
    square = (SEQ_LEN, D)
    turned = buf((heads, HD, SEQ_LEN), BF)
    scratch = [
        buf((D, n_q), BF), buf(wd.shape, BF), buf(square, BF), buf(square, BF), buf(square, BF), buf(square, BF),
        turned, turned, turned, turned, turned, buf((n_q, SEQ_LEN), BF),
        buf((HD, SEQ_LEN), F32), buf((HD, SEQ_LEN), F32), buf((HD, SEQ_LEN), F32),
        buf((ROWS, 2, 2, 2, 32, n_q), BF), buf((2, 2, 2, h_d // 2, D), BF), buf((SEQ_LEN, heads * HD), BF), buf(square, F32),
        buf((cols - 1, part, D), F32), buf((cols - 1, part, D), F32),
        buf((8, D), F32), buf((1, n_q), F32), buf((1, D), F32), buf((4, 8, line), F32), buf((4 + cols, 8, line), F32),
        buf((8, D), F32),
    ]
    scratch += [buf((ROWS, 2, 32, n_u), BF)] * 2 + [buf((2, h_p // 2, D), BF)] * 2
    for lead, count in (((ROWS, 2), None), ((ROWS,), None), ((3,), 3), ((2,), 2)):
        for w, start, size in pieces:
            if w in (QKV, UP):
                one = lead + (32, size)
            elif count is None:
                one = ((2,) if len(lead) == 2 else ()) + (size, D)
            else:
                one = (size, 256 * count)
            scratch += [buf(one, BF)] * 2
    scratch += [
        dma((7,)), dma((n_p, 2)), dma((n_p, 2)), dma((n_p, 2)), dma((n_p, 2)), dma((n_p, 2)), dma((n_p, 2)), dma((n_p, 2)),
        dma((n_p, 2)), dma((n_p, 2)), dma((n_p, 2)), dma((n_p, 2)), dma((2, cols - 1)), dma((2, cols - 1)),
        dma((2, ROWS)), dma((2, tok_col // part)), dma((4 + cols,)), dma((4 + cols,)),
    ]
    return pl.pallas_call(
        functools.partial(scatter_kernel, cols, aligned, pieces),
        out_shape=[
            shape((tok_col, 256), BF), shape((tok_col, 256), BF), shape((2, 32, n_q), F32), shape((2, 32, n_u), F32),
            shape((2, h_d // 2, 256), F32), shape((2, h_p // 2, 256), F32), shape((8, line), F32),
        ],
        in_specs=[smem, vmem, vmem, vmem, vmem] + [any_spec] * 10,
        out_specs=[any_spec] * 2 + [vmem] * 5,
        scratch_shapes=scratch,
        compiler_params=pltpu.CompilerParams(collective_id=1, has_side_effects=True, vmem_limit_bytes=63 << 20),
    )(prefix_len, smalls, angles, bias, sum_u, own_x, own_cot, wq, wd, first, first_t, gu, gp, branch, comb)


def angles_table():
    half_rot = ROT // 2
    rates = np.exp(np.arange(half_rot, dtype=np.float32) * np.float32(-2.0 * math.log(10000.0) / ROT))
    turned = rates.astype(np.float32)[:, None] * np.arange(SEQ_LEN, dtype=np.float32)[None, :]
    return np.concatenate([np.cos(turned), np.sin(turned)], axis=0).astype(np.float32)


def shards(cols, tokens_in, prefix_len, first_gain, first_shift, second_gain, second_shift, qkv_weight, qkv_bias,
           up_weight, up_bias, dense_weight, dense_bias, down_weight, down_bias, cotangent):
    tok_col = tokens_in.shape[0]
    n_q, n_u = qkv_weight.shape[1], up_weight.shape[1]
    h_d, h_p = dense_weight.shape[0], down_weight.shape[0]

    n_qb, n_ub = qkv_bias.shape[0], up_bias.shape[0]
    aligned = n_qb % 128 == 0 and n_ub % 128 == 0
    small = jnp.concatenate((first_gain, first_shift, second_gain, second_shift, dense_bias, down_bias, qkv_bias, up_bias))
    size = -(-small.shape[0] // 1024) * 1024
    small = jnp.pad(small, (0, size - small.shape[0])).reshape(size // 128, 128)
    if aligned:
        q_bias = u_bias = small
    else:
        q_bias = lax.all_gather(rounded(qkv_bias), "dp", axis=0, tiled=True).reshape(1, n_q)
        u_bias = lax.all_gather(rounded(up_bias), "dp", axis=0, tiled=True).reshape(1, n_u)
    own_x, own_cot, smalls, wq, wd, first, first_t, gu, gp, branch, comb, sum_u = gather(
        tokens_in, cotangent, small, u_bias, (qkv_weight, up_weight, dense_weight, down_weight), cols, aligned
    )
    layer_out, grad_tokens, out_q, out_u, out_d, out_p, sums = scatter(
        prefix_len, smalls, jnp.asarray(angles_table()), q_bias, sum_u, own_x, own_cot, wq, wd, first, first_t, gu, gp, branch,
        comb, cols, aligned, tok_col
    )
    dp, row = lax.axis_index("dp"), lax.axis_index("row")
    gain_sums = lax.dynamic_slice(sums, (0, row * 256), (4, 256))
    out_b = lax.dynamic_slice(sums, (4, (row * DPS + dp) * 64), (1, 64))[0]
    q_b = lax.dynamic_slice(sums, (5, dp * n_qb), (1, n_qb))[0]
    u_b = lax.dynamic_slice(sums, (6, dp * n_ub), (1, n_ub))[0]
    return (
        layer_out, grad_tokens, out_q.reshape(64, n_q), q_b, out_u.reshape(64, n_u), u_b,
        out_d.reshape(h_d, 256), out_b, out_p.reshape(h_p, 256), out_b,
        gain_sums[0], gain_sums[1], gain_sums[2], gain_sums[3],
    )


def solution(mesh):
    in_specs = (
        P(("dp", "col"), "row"), P(("dp", "row")), P("row"), P("row"), P("row"), P("row"),
        P(("row", "dp"), "col"), P(("col", "dp")), P(("row", "dp"), "col"), P(("col", "dp")),
        P(("col", "dp"), "row"), P(("row", "dp")), P(("col", "dp"), "row"), P(("row", "dp")),
        P(("dp", "col"), "row"),
    )
    out_specs = (
        P(("dp", "col"), "row"), P(("dp", "col"), "row"), P(("row", "dp"), "col"), P(("col", "dp")),
        P(("row", "dp"), "col"), P(("col", "dp")), P(("col", "dp"), "row"), P(("row", "dp")),
        P(("col", "dp"), "row"), P(("row", "dp")), P("row"), P("row"), P("row"), P("row"),
    )
    body = functools.partial(shards, mesh.shape["col"])
    return jax.shard_map(body, mesh=mesh, in_specs=in_specs, out_specs=out_specs, check_vma=False)
```

time: 317 us -> 293 us (0.924)
  Pallas kernels: 296 us -> 277 us
    pallas_call x1, Pallas kernels: 152 us -> 140 us  [scatter(): pl.pallas_call(functools.partial(scatter_kernel, cols, aligned, pieces),...]
    pallas_call x1, Pallas kernels: 144 us -> 137 us  [gather(): pl.pallas_call(functools.partial(gather_kernel, cols, aligned), out_shape...]
where the time goes in v4:
time: 293 us
  Pallas kernels  277 us (95%)
  local copies, waits for them, and re-layouts  14.6 us (5%)
    pallas_call x1, Pallas kernels, scatter(): pl.pallas_call(functools.partial(scatter_kernel, cols, aligned, pieces),...  140 us
    pallas_call x1, Pallas kernels, gather(): pl.pallas_call(functools.partial(gather_kernel, cols, aligned), out_shape...  137 us
    unnamed x17, local copies, waits for them, and re-layouts  8.1 us

profile of v4, /device:TPU:0, one launch (start us, length us, event | category | flops | bytes accessed | tf_op | source)
XLA Modules:
  0.0 293.0 jit_solution(11655847030054539697)
XLA Ops:
  0.6 1.5 concatenate.3
  2.1 137.0 %shard_map.263 = (bf16[1024,1024]{1,0:T(8,128)(2,1)}, bf16[1024,1024]{1,0:T(8,128)(2,1)}, f32[16,16,128]{2,1,0:T(8,128)}, bf16[1024,1536]{1,0:T(8,128)(2,1)}, bf...) custom-call(bf16[2048,256]{1,0:T(8,128)(2,1)} %refs_0_.2, ...), custom_call_target="tpu_custom_call" | custom-call | tf_op jit(solution)/shard_map/pallas_call | solution.py:594
  139.8 140.0 %shard_map.264 = (bf16[2048,256]{1,0:T(8,128)(2,1)}, bf16[2048,256]{1,0:T(8,128)(2,1)}, f32[2,32,1536]{2,1,0:T(8,128)}, f32[2,32,2048]{2,1,0:T(8,128)}, f32[2,64...) custom-call(s32[1]{0:T(128)S(6)} %copy.37.refs_0_, f32[16,16,128]{2,1,0:T(8,128)} %get-tuple-element.33.refs_1_, ...), custom_call_target="tpu_custom_call" | custom-call | tf_op jit(solution)/shard_map/pallas_call | solution.py:1123
  279.7 0.0 copy-start.2
  279.8 0.0 copy-start.1
  279.8 0.0 copy-start.3
  279.8 0.8 dynamic-slice_bitcast_fusion
  280.6 0.0 copy-start.4
  280.6 1.5 fusion
  282.1 1.4 constant_dynamic-slice_fusion
  283.5 1.4 dynamic-slice_reduce_fusion
  284.9 0.5 copy.38
  285.4 0.0 copy-start
  285.4 2.3 copy.39
  287.7 2.3 copy.40
  289.9 0.0 copy-done.2
  289.9 0.7 copy.41
  290.7 0.0 copy-done.1
  290.7 0.8 copy.42
  291.5 0.0 copy-done.3
  291.5 0.7 copy.43
  292.2 0.0 copy-done.4
  292.2 0.0 copy-done
  292.2 0.8 copy.44
Async XLA Ops:
  279.7 10.2 %copy-start.2 = (f32[2,32,1536]{2,1,0:T(8,128)S(1)}, f32[2,32,1536]{2,1,0:T(8,128)}, u32[]{:S(2)}) copy-start(f32[2,32,1536]{2,1,0:T(8,128)} %get-tuple-element.47) | copy-start | bytes 1179652
  279.8 10.9 %copy-start.1 = (f32[2,32,2048]{2,1,0:T(8,128)S(1)}, f32[2,32,2048]{2,1,0:T(8,128)}, u32[]{:S(2)}) copy-start(f32[2,32,2048]{2,1,0:T(8,128)} %get-tuple-element.49) | copy-start | bytes 1572868
  279.8 11.7 %copy-start.3 = (f32[2,64,256]{2,1,0:T(8,128)S(1)}, f32[2,64,256]{2,1,0:T(8,128)}, u32[]{:S(2)}) copy-start(f32[2,64,256]{2,1,0:T(8,128)} %get-tuple-element.50) | copy-start | bytes 393220
  280.6 11.5 %copy-start.4 = (f32[64]{0:T(128)}, f32[64]{0:T(128)S(1)}, u32[]{:S(2)}) copy-start(f32[64]{0:T(128)S(1)} %dynamic-slice_bitcast_fusion) | copy-start | bytes 772
  285.4 6.8 %copy-start = (f32[2,256,256]{2,1,0:T(8,128)S(1)}, f32[2,256,256]{2,1,0:T(8,128)}, u32[]{:S(2)}) copy-start(f32[2,256,256]{2,1,0:T(8,128)} %get-tuple-element.51) | copy-start | bytes 1572868

commit v5 on v4

--- a/solution.py
+++ b/solution.py
@@ -63,33 +63,48 @@
 
 N_W = 4
 QKV, UP, DENSE, DOWN = range(N_W)
-BEFORE = (
+GATHER_PLAN = (
     "b1", "z10", "b0", "b3", "b2", "z20", "s10", "z11", "s11", "z12", "z30", "m", "s12", "z13", "s30", "t0", "z31",
     "p10", "p11", "s31", "s13", "s00", "p31", "z32", "t1", "p12", "p13", "s32", "z33", "s20", "d0", "z00", "p30",
-    "z21", "s33", "N", "p32",
+    "z21", "s33", "N0", "N1", "N2", "N3", "N4", "N5", "N6", "N7", "p32", "P0", "d1", "P1", "P2", "P3", "z01",
+    "p33", "D0", "s01", "D1", "s21", "D2", "z02", "p00", "D3", "s02", "z22", "z23", "B0", "B1", "z03", "B2", "B3",
+    "s23", "B4", "B5", "p23", "s22", "p20", "p21", "B6", "B7", "p22", "p02", "s03", "B8", "p01", "B9", "B10",
+    "B11", "p03",
 )
-BETWEEN = (
-    ("d1",),
-    (),
-    (),
-    ("z01", "p33",),
-    ("s01",),
-    ("s21",),
-    ("z02", "p00",),
-    ("s02", "z22", "z23",),
-    (),
-    ("z03",),
-    (),
-    ("s23",),
-    (),
-    ("p23", "s22", "p20", "p21",),
-    (),
-    ("p22", "p02", "s03",),
-    ("p01",),
-    (),
-    (),
-    ("p03",),
-)
+
+
+def run(words, loops, act):
+    i = 0
+    while i < len(words):
+        kind = words[i][0]
+        if kind not in loops:
+            act(words[i])
+            i += 1
+            continue
+        count, body = loops[kind]
+        groups = [[]]
+        i += 1
+        while len(groups) < count:
+            if words[i][0] == kind:
+                groups.append([])
+            else:
+                groups[-1].append(words[i])
+            i += 1
+
+        def served(index, first=0, stride=1):
+            for n, group in enumerate(groups[first::stride]):
+                if group:
+
+                    @pl.when(index == n)
+                    def _():
+                        for word in group:
+                            act(word)
+
+        body(served)
+
+
+def parts_of(kind, count):
+    return ["%s%d" % (kind, n) for n in range(count)]
 
 
 def nt(left, right):
@@ -148,7 +163,7 @@
     return (x - center) * scale_inv, scale_inv
 
 
-def norm_stage(x_ref, gains, outs):
+def norm_stage(x_ref, gains, outs, served):
     def body(i, carry):
         rows = span(i * 128, 128, 128)
         normed, ignored = norm_rows(x_ref[rows, :].astype(F32))
@@ -156,12 +171,13 @@
             value = (normed * gains[which : which + 1, :] + gains[which + 1 : which + 2, :]).astype(BF)
             plain[rows, :] = value
             turned[:, rows] = value.T
+        served(i)
         return carry
 
     lax.fori_loop(0, SEQ_LEN // 128, body, 0)
 
 
-def project_stage(wq, first, bias_row, angles, q_t, k_t, v_t, heads):
+def project_stage(wq, first, bias_row, angles, q_t, k_t, v_t, heads, served):
     pair = min(heads, 2)
     width = 192 * pair
 
@@ -183,6 +199,7 @@
                 q_t[h, :, toks] = (turn(base) * HD ** (-0.5)).astype(BF)
                 k_t[h, :, toks] = turn(base + 64).astype(BF)
                 v_t[h, :, toks] = mixed[base + 128 : base + 192].astype(BF)
+        served(p)
         return carry
 
     lax.fori_loop(0, heads // pair, body, 0)
@@ -196,12 +213,10 @@
             up_t[h, :, toks] = grad[HD * h : HD * (h + 1)]
 
 
-def attend_head(h, prefix, angles, q_t, k_t, v_t, up_t, att_t, gm_t, grad_q, grad_k, grad_v, middle):
+def attend_head(h, prefix, angles, q_t, k_t, v_t, up_t, att_t, gm_t, grad_q, grad_k, grad_v, served):
     keys_plain, values_plain = k_t[h].T, v_t[h].T
     done = 0
     for i in range(SEQ_LEN // 256):
-        if i == 2:
-            middle()
         low = 256 * i
         seen = max(512, low + 256)
         spot = pl.ds(low, 256)
@@ -215,9 +230,10 @@
         exponent = jnp.exp(scores - jnp.max(scores, axis=0, keepdims=True))
         probs = exponent * (1.0 / jnp.sum(exponent, axis=0, keepdims=True))
         weights = probs.astype(BF)
-        att_t[h, :, spot] = nn(v_t[h, :, 0:seen], weights).astype(BF)
+        outputs = nn(v_t[h, :, 0:seen], weights)
+        att_t[h, :, spot] = outputs.astype(BF)
+        inner = jnp.sum(outputs * up.astype(F32), axis=0, keepdims=True)
         grad_probs = nn(values_plain[0:seen], up)
-        inner = jnp.sum(probs * grad_probs, axis=0, keepdims=True)
         grad_scores = (probs * (grad_probs - inner)).astype(BF)
         grad_q[:, spot] = nn(k_t[h, :, 0:seen], grad_scores)
         for total, part in ((grad_v, nt(up, weights)), (grad_k, nt(q, grad_scores))):
@@ -226,6 +242,7 @@
             if seen > done:
                 total[:, done:seen] = part[:, done:]
         done = seen
+        served(h, i, SEQ_LEN // 256)
     cos, sin = angles[0:8, :], angles[8:16, :]
 
     def turn_back(grad):
@@ -436,7 +453,7 @@
         for step in range(1, ROWS * DPS):
             small_copy(step).start()
 
-    def norm():
+    def norm(served):
         small_home.wait()
         for step in range(1, ROWS * DPS):
             small_copy(step).wait()
@@ -449,7 +466,7 @@
         comb[...] = jnp.zeros(comb.shape, F32)
         token_finish(0)
         first, first_t = hidden.at[:, pl.ds(0, D)], hidden.at[:, pl.ds(D, D)]
-        norm_stage(x_ref, gains, ((0, first, first_t), (2, second, second_t)))
+        norm_stage(x_ref, gains, ((0, first, first_t), (2, second, second_t)), served)
         keep(x_ref, x_out)
         keep(smalls, smalls_out)
         keep(first, first_out)
@@ -459,94 +476,87 @@
         kind, rest = word[0], [int(d) for d in word[1:]]
         {
             "b": begin, "z": onward, "s": sideways, "p": passed, "t": token_start, "d": token_spread, "m": smalls_start,
-            "N": norm,
         }[kind](*rest)
 
-    def serve_at(when, unit):
-        if blocks == DPS and BETWEEN[unit]:
-
-            @pl.when(when)
-            def _():
-                for word in BETWEEN[unit]:
-                    act(word)
-
-    for word in BEFORE:
-        act(word)
-    if blocks < DPS:
-        for words in BETWEEN:
-            for word in words:
-                act(word)
-    home(UP).wait()
-    finished(UP)
-    for copy in kept[2:4]:
-        copy.wait()
-
-    def forward_block(n, carry):
-        cut = span(n * width, width, width)
-
-        def body(j, carry):
-            rows = span(j * 256, 256, 256)
-            value, slant = gelu_parts(nn(second[rows, :], wu[:, cut]) + bias_row[0:1, cut])
-            hidden[rows, cut] = value.astype(BF)
-            slope[rows, cut] = slant
+    def forward(served):
+        home(UP).wait()
+        finished(UP)
+        for copy in kept[2:4]:
+            copy.wait()
+
+        def block(n, carry):
+            cut = span(n * width, width, width)
+
+            def body(j, carry):
+                rows = span(j * 256, 256, 256)
+                value, slant = gelu_parts(nn(second[rows, :], wu[:, cut]) + bias_row[0:1, cut])
+                hidden[rows, cut] = value.astype(BF)
+                slope[rows, cut] = slant
+                return carry
+
+            lax.fori_loop(0, SEQ_LEN // 256, body, 0)
+            served(n)
             return carry
 
-        lax.fori_loop(0, SEQ_LEN // 256, body, 0)
-        for m in range(DPS):
-            serve_at(n == m, m)
-        return carry
-
-    lax.fori_loop(0, blocks, forward_block, 0)
-    token_finish(1)
-    keep(c_ref, c_out)
-    h = gp.shape[3]
-
-    def down_block(n, carry):
-        cut = span(n * width, width, width)
-        turned = hidden[:, cut].T
-        if blocks == DPS:
-            for half in range(2):
-                gp[n // 2, lax.rem(n, 2), half] = nn(turned[half * h : (half + 1) * h, :], c_ref[...]).astype(BF)
-        else:
-            gp[...] = nn(turned, c_ref[...]).astype(BF).reshape(2, 2, 2, h, D)
-        for m in range(DPS):
-            serve_at(n == m, DPS + m)
-        return carry
-
-    lax.fori_loop(0, blocks, down_block, 0)
-    keep(gp, gp_out)
-    home(DOWN).wait()
-    finished(DOWN)
-    sum_out[...] = jnp.zeros(sum_out.shape, F32)
-
-    def backward_block(n, carry):
-        cut = span(n * width, width, width)
-
-        def body(j, carry):
-            rows = span(j * 256, 256, 256)
-            grad = (nt(c_ref[rows, :], wp[cut, :]) * slope[rows, cut]).astype(BF)
-            ghp[rows, :] = grad
-            branch[rows, :] += nn(hidden[rows, cut], wp[cut, :])
-            comb[rows, :] += nt(grad, wu[:, cut])
-            sum_out[0:1, cut] += jnp.sum(grad.astype(F32), axis=0, keepdims=True)
+        lax.fori_loop(0, blocks, block, 0)
+
+    def down_grads(served):
+        token_finish(1)
+        keep(c_ref, c_out)
+        h = gp.shape[3]
+
+        def block(n, carry):
+            turned = hidden[:, span(n * width, width, width)].T
+            if blocks == DPS:
+                for half in range(2):
+                    gp[n // 2, lax.rem(n, 2), half] = nn(turned[half * h : (half + 1) * h, :], c_ref[...]).astype(BF)
+            else:
+                gp[...] = nn(turned, c_ref[...]).astype(BF).reshape(2, 2, 2, h, D)
+            served(n)
             return carry
 
-        for part_of in range(2):
-            lax.fori_loop(2 * part_of, 2 * part_of + 2, body, 0)
-            for m in range(DPS):
-                serve_at(n == m, 2 * DPS + 3 * m + part_of)
-
-        def up_body(r, carry):
-            value = nn(second_t[span(r * 256, 256, 256), :], ghp[...]).astype(BF)
-            gu[r, :, :, :, :, cut] = value.reshape(2, 2, 2, 32, width)
+        lax.fori_loop(0, blocks, block, 0)
+        keep(gp, gp_out)
+
+    def backward(served):
+        home(DOWN).wait()
+        finished(DOWN)
+        sum_out[...] = jnp.zeros(sum_out.shape, F32)
+
+        def block(n, carry):
+            cut = span(n * width, width, width)
+
+            def body(j, carry):
+                rows = span(j * 256, 256, 256)
+                grad = (nt(c_ref[rows, :], wp[cut, :]) * slope[rows, cut]).astype(BF)
+                ghp[rows, :] = grad
+                branch[rows, :] += nn(hidden[rows, cut], wp[cut, :])
+                comb[rows, :] += nt(grad, wu[:, cut])
+                sum_out[0:1, cut] += jnp.sum(grad.astype(F32), axis=0, keepdims=True)
+                return carry
+
+            for part_of in range(2):
+                lax.fori_loop(2 * part_of, 2 * part_of + 2, body, 0)
+                served(n, part_of, 3)
+
+            def up_body(r, carry):
+                value = nn(second_t[span(r * 256, 256, 256), :], ghp[...]).astype(BF)
+                gu[r, :, :, :, :, cut] = value.reshape(2, 2, 2, 32, width)
+                return carry
+
+            lax.fori_loop(0, ROWS, up_body, 0)
+            served(n, 2, 3)
             return carry
 
-        lax.fori_loop(0, ROWS, up_body, 0)
-        for m in range(DPS):
-            serve_at(n == m, 2 * DPS + 3 * m + 2)
-        return carry
-
-    lax.fori_loop(0, blocks, backward_block, 0)
+        lax.fori_loop(0, blocks, block, 0)
+
+    loops = {"N": (8, norm), "P": (blocks, forward), "D": (blocks, down_grads), "B": (3 * blocks, backward)}
+    plan = GATHER_PLAN
+    if blocks != DPS:
+        plan = [word for word in plan if word[0] not in loops]
+        for kind in "NPDB":
+            plan = plan + parts_of(kind, loops[kind][0])
+    run(plan, loops, act)
     for src, dst in ((gu, gu_out), (branch, branch_out), (comb, comb_out)):
         keep(src, dst)
     for w in (QKV, DENSE):
@@ -601,32 +611,15 @@
     )(tokens_in, cotangent, small, bias, wq, wu, wd, wp)
 
 
-BEFORE_HEADS = (
-    "f0", "f1", "J", "f2", "U",
-)
-AMONG_HEADS = (
-    (),
-    (),
-    (),
-    ("g0", "f3",),
-    (),
-    (),
-    (),
-    ("g1",),
-    ("f4",),
-    ("h0", "g2",),
-    (),
-    ("h1", "g3", "g4", "q0",),
-    (),
-    ("h2", "h3",),
-    (),
-    ("f5", "q1",),
-)
-AFTER_HEADS = (
-    "q2", "h4", "T", "q3", "r0", "q4", "r1", "g5", "f6", "u0", "X", "W", "g6", "r2", "f7", "u1", "f8", "h5", "G",
-    "g7", "h6", "Y", "g8", "f9", "u2", "r3", "h7", "f10", "q5", "h8", "v0", "q6", "g9", "v1", "f11", "v2", "q7",
-    "h9", "u3", "g10", "h10", "g11", "q8", "r4", "r5", "q9", "r6", "u4", "v3", "u5", "r7", "r8", "q10", "h11",
-    "q11", "u6", "u7", "u8", "r9", "u9", "r10", "v4", "u10", "r11", "u11",
+SCATTER_PLAN = (
+    "f0", "f1", "J0", "J1", "J2", "J3", "f2", "U", "H0", "H1", "H2", "H3", "H4", "H5", "g0", "f3", "H6", "H7",
+    "H8", "H9", "H10", "H11", "H12", "H13", "g1", "H14", "H15", "f4", "H16", "H17", "h0", "g2", "H18", "H19",
+    "H20", "H21", "h1", "g3", "g4", "q0", "H22", "H23", "H24", "H25", "h2", "h3", "H26", "H27", "H28", "H29", "f5",
+    "q1", "H30", "H31", "q2", "h4", "T", "q3", "r0", "q4", "r1", "g5", "f6", "u0", "X", "W0", "W1", "W2", "W3",
+    "g6", "r2", "f7", "u1", "f8", "h5", "G0", "G1", "G2", "G3", "g7", "h6", "Y", "g8", "f9", "u2", "r3", "h7",
+    "f10", "q5", "h8", "v0", "q6", "g9", "v1", "f11", "v2", "q7", "h9", "u3", "g10", "h10", "g11", "q8", "r4",
+    "r5", "q9", "r6", "u4", "v3", "u5", "r7", "r8", "q10", "h11", "q11", "u6", "u7", "u8", "r9", "u9", "r10", "v4",
+    "u10", "r11", "u11",
 )
 PIECES = 12
 
@@ -672,9 +665,9 @@
      comb_in) = refs[:15]
     (lo_out, gt_out, oq, ou, od, op, sm_out) = refs[15:22]
     (wq, wd, x_ref, c_ref, first, first_t, q_t, k_t, v_t, up_t, att_t, gm_t, grad_q, grad_k, grad_v) = refs[22:37]
-    (gq, gd, att, total_ref, branch_got, comb_got, gains, bias_row, out_bias, sm, sm_got, gain_sum) = refs[37:49]
-    mine_u, mine_p = refs[49:51], refs[51:53]
-    base = 53
+    (gq, gd, att, branch, comb, branch_got, comb_got, gains, bias_row, out_bias, sm, sm_got, gain_sum) = refs[37:50]
+    mine_u, mine_p = refs[50:52], refs[52:54]
+    base = 54
 
     def buffers(start):
         return [refs[start + 2 * i : start + 2 * i + 2] for i in range(n_p)]
@@ -696,7 +689,7 @@
         return pltpu.make_async_copy(src, dst, l_sem.at[n])
 
     loads = [load(first_in, first, 0), load(wq_in, wq, 1), load(wd_in, wd, 2), load(c_in, c_ref, 3), load(first_t_in, first_t, 4),
-             load(x_in, x_ref, 5), load(branch_in, total_ref, 6)]
+             load(branch_in, branch, 5), load(comb_in, comb, 6), load(x_in, x_ref, 7)]
     for one in loads:
         one.start()
     group = [(dp, lax.rem(row + step, ROWS), lax.rem(col + other, cols)) for step in range(ROWS) for other in range(cols)]
@@ -840,7 +833,7 @@
 
     def col_copy(kind, n):
         other = lax.rem(col + n, cols)
-        src = total_ref.at[part_rows(other), :]
+        src = (branch, comb)[kind].at[part_rows(other), :]
         dst = (branch_got, comb_got)[kind].at[n - 1]
         return remote(src, dst, d_send.at[kind, n - 1], d_recv.at[kind, n - 1], (dp, row, other))
 
@@ -879,7 +872,7 @@
         def body(i, carry):
             here = span(i * height, height, height)
             rows = span(col * part + i * height, height, height)
-            value = total_ref[rows, :]
+            value = (branch, comb)[kind][rows, :]
             for n in range(1, cols):
                 value = value + (branch_got, comb_got)[kind][n - 1, here, :]
             wide = x_ref[rows, :].astype(F32)
@@ -923,7 +916,7 @@
         for m in ((0,), (1,), (2, 3, 4), tuple(range(5, 4 + cols)), ())[n]:
             small_copy(m).start()
 
-    def project():
+    def project(served):
         read_gains(smalls, gains)
         lanes = lax.broadcasted_iota(jnp.int32, (1, 128), 1)
         for r in range(ROWS):
@@ -939,7 +932,7 @@
         sm[0, 6:7, 0:n_u] = sum_u[...]
         loads[0].wait()
         loads[1].wait()
-        project_stage(wq, first, bias_row, angles, q_t, k_t, v_t, heads)
+        project_stage(wq, first, bias_row, angles, q_t, k_t, v_t, heads, served)
 
     def upstream():
         loads[2].wait()
@@ -956,44 +949,46 @@
             return carry
 
         lax.fori_loop(0, heads // group_h, turn_body, 0)
-        loads[6].wait()
+        loads[5].wait()
 
         def out_body(j, carry):
             rows = span(j * 256, 256, 256)
-            total_ref[rows, :] += nn(att[rows, :], wd[...])
+            branch[rows, :] += nn(att[rows, :], wd[...])
             return carry
 
         lax.fori_loop(0, SEQ_LEN // 256, out_body, 0)
         for n in range(1, cols):
             col_copy(0, n).start()
 
-    def weight_grads():
-        all_heads = att_t[...].reshape(heads * HD, SEQ_LEN)
-        gd[...] = nn(all_heads, c_ref[...]).astype(BF).reshape(gd.shape)
-        loads[4].wait()
+    def weight_grads(n):
+        if n == 0:
+            all_heads = att_t[...].reshape(heads * HD, SEQ_LEN)
+            gd[...] = nn(all_heads, c_ref[...]).astype(BF).reshape(gd.shape)
+            return
+        if n == 1:
+            loads[4].wait()
         wide = min(512, n_q)
+        cut = pl.ds((n - 1) * wide, wide)
 
         def qkv_body(r, carry):
             rows = span(r * 256, 256, 256)
-            for n in range(n_q // wide):
-                cut = pl.ds(n * wide, wide)
-                gq[r, :, :, :, :, cut] = nt(first_t[rows, :], gm_t[cut, :]).astype(BF).reshape(2, 2, 2, 32, wide)
+            gq[r, :, :, :, :, cut] = nt(first_t[rows, :], gm_t[cut, :]).astype(BF).reshape(2, 2, 2, 32, wide)
             return carry
 
         lax.fori_loop(0, ROWS, qkv_body, 0)
 
-    load_comb = load(comb_in, total_ref, 6)
+    need_x = [loads[7]]
 
     def output_home():
-        loads[5].wait()
+        if len(need_x):
+            need_x.pop().wait()
         finish_rows(0)
         out_start(0)
-        for n in range(1, cols):
-            col_copy(0, n).wait_send()
-        load_comb.start()
-
-    def features():
-        load_comb.wait()
+
+    def features(served):
+        loads[6].wait()
+        if len(need_x):
+            need_x.pop().wait()
         for n in range(8):
             gain_sum[n : n + 1, :] = jnp.zeros((1, D), F32)
 
@@ -1001,13 +996,14 @@
             rows = span(j * 256, 256, 256)
             grad = gm_t[:, rows].T
             grad_first = nt(grad, wq[...])
-            grad_second = total_ref[rows, :]
+            grad_second = comb[rows, :]
             normed, ignored = norm_rows(x_ref[rows, :].astype(F32))
             for n, value in enumerate((normed * grad_first, grad_first, normed * grad_second, grad_second,
                                        c_ref[rows, :].astype(F32))):
                 gain_sum[n : n + 1, :] += jnp.sum(value, axis=0, keepdims=True)
             sm[0, 5:6, 0:n_q] += jnp.sum(grad.astype(F32), axis=0, keepdims=True)
-            total_ref[rows, :] = gains[0:1, :] * grad_first + gains[2:3, :] * grad_second
+            comb[rows, :] = gains[0:1, :] * grad_first + gains[2:3, :] * grad_second
+            served(j)
             return carry
 
         lax.fori_loop(0, SEQ_LEN // 256, body, 0)
@@ -1020,61 +1016,45 @@
         out_start(1)
 
     stages = {"f": begin, "g": stage_two, "h": stage_three, "q": stage_four, "r": stage_five, "u": stage_six}
-    others = {"J": project, "U": upstream, "T": attended, "W": weight_grads, "X": output_home, "G": features, "Y": gradient_home}
+    others = {"U": upstream, "T": attended, "X": output_home, "Y": gradient_home}
 
     def act(word):
         kind, rest = word[0], word[1:]
         if kind in others:
             others[kind]()
+        elif kind == "W":
+            weight_grads(int(rest))
         elif kind == "v":
             small_step(int(rest))
         else:
             stages[kind](int(rest))
 
-    plan = (BEFORE_HEADS, AMONG_HEADS, AFTER_HEADS)
+    def attention(served):
+        prefix = prefix_ref[0]
+
+        def head_body(h, carry):
+            attend_head(h, prefix, angles, q_t, k_t, v_t, up_t, att_t, gm_t, grad_q, grad_k, grad_v, served)
+            return carry
+
+        lax.fori_loop(0, heads, head_body, 0)
+
+    loops = {
+        "J": (heads // min(heads, 2), project), "H": (heads * (SEQ_LEN // 256), attention), "G": (SEQ_LEN // 256, features),
+    }
+    plan = SCATTER_PLAN
     if n_p != PIECES:
         late = [i for i in range(n_p) if pieces[i][0] in (QKV, DENSE)]
-        early = [i for i in range(n_p) if i not in late]
-        after = ["T", "W", "X", "G", "Y"] + ["f%d" % i for i in late] + [s + str(i) for s in "ghqru" for i in range(n_p)]
-        plan = (["f%d" % i for i in early] + ["J", "U"], ((),) * 16, after + ["v%d" % i for i in range(5)])
-    before_heads, among_heads, after_heads = plan
-
-    def serve_at(when, unit):
-        if among_heads[unit]:
-
-            @pl.when(when)
-            def _():
-                for word in among_heads[unit]:
-                    act(word)
-
-    for word in before_heads:
-        act(word)
-    prefix = prefix_ref[0]
-    units = len(among_heads) // 2
-
-    def head_body(h, carry):
-        for n in range(min(units, heads)):
-            serve_at(h == n, 2 * n)
-
-        def middle():
-            for n in range(min(units, heads)):
-                serve_at(h == n, 2 * n + 1)
-
-        attend_head(h, prefix, angles, q_t, k_t, v_t, up_t, att_t, gm_t, grad_q, grad_k, grad_v, middle)
-        return carry
-
-    lax.fori_loop(0, heads, head_body, 0)
-    for unit in range(2 * min(units, heads), 2 * units):
-        for word in among_heads[unit]:
-            act(word)
-    for word in after_heads:
-        act(word)
+        plan = ["f%d" % i for i in range(n_p) if i not in late] + parts_of("J", loops["J"][0]) + ["U"]
+        plan = plan + parts_of("H", loops["H"][0]) + ["T", "W0", "W1", "X"] + parts_of("G", loops["G"][0]) + ["Y"]
+        plan = plan + ["f%d" % i for i in late] + [s + str(i) for s in "ghqru" for i in range(n_p)] + parts_of("v", 5)
+    run(plan, loops, act)
     for i in range(n_p):
         drain(i)
     for kind in range(2):
         out_finish(kind)
     for n in range(1, cols):
-        col_copy(1, n).wait_send()
+        for kind in range(2):
+            col_copy(kind, n).wait_send()
     for n in range(4 + cols):
         small_copy(n).wait_send()
 
@@ -1100,7 +1080,7 @@
         buf((D, n_q), BF), buf(wd.shape, BF), buf(square, BF), buf(square, BF), buf(square, BF), buf(square, BF),
         turned, turned, turned, turned, turned, buf((n_q, SEQ_LEN), BF),
         buf((HD, SEQ_LEN), F32), buf((HD, SEQ_LEN), F32), buf((HD, SEQ_LEN), F32),
-        buf((ROWS, 2, 2, 2, 32, n_q), BF), buf((2, 2, 2, h_d // 2, D), BF), buf((SEQ_LEN, heads * HD), BF), buf(square, F32),
+        buf((ROWS, 2, 2, 2, 32, n_q), BF), buf((2, 2, 2, h_d // 2, D), BF), buf((SEQ_LEN, heads * HD), BF), buf(square, F32), buf(square, F32),
         buf((cols - 1, part, D), F32), buf((cols - 1, part, D), F32),
         buf((8, D), F32), buf((1, n_q), F32), buf((1, D), F32), buf((4, 8, line), F32), buf((4 + cols, 8, line), F32),
         buf((8, D), F32),
@@ -1116,7 +1096,7 @@
                 one = (size, 256 * count)
             scratch += [buf(one, BF)] * 2
     scratch += [
-        dma((7,)), dma((n_p, 2)), dma((n_p, 2)), dma((n_p, 2)), dma((n_p, 2)), dma((n_p, 2)), dma((n_p, 2)), dma((n_p, 2)),
+        dma((8,)), dma((n_p, 2)), dma((n_p, 2)), dma((n_p, 2)), dma((n_p, 2)), dma((n_p, 2)), dma((n_p, 2)), dma((n_p, 2)),
         dma((n_p, 2)), dma((n_p, 2)), dma((n_p, 2)), dma((n_p, 2)), dma((2, cols - 1)), dma((2, cols - 1)),
         dma((2, ROWS)), dma((2, tok_col // part)), dma((4 + cols,)), dma((4 + cols,)),
     ]
@@ -1133,6 +1113,48 @@
     )(prefix_len, smalls, angles, bias, sum_u, own_x, own_cot, wq, wd, first, first_t, gu, gp, branch, comb)
 
 
+def finish_kernel(*refs):
+    whole_in, sums, whole_out, q_b, u_b, d_b, p_b, gains, rooms, sem = (
+        refs[:6], refs[6], refs[7:13], *refs[13:17], refs[17:21], refs[21:27], refs[27]
+    )
+    arrive = [pltpu.make_async_copy(src, dst, sem.at[0, n]) for n, (src, dst) in enumerate(zip(whole_in, rooms))]
+    leave = [pltpu.make_async_copy(src, dst, sem.at[1, n]) for n, (src, dst) in enumerate(zip(rooms, whole_out))]
+    for copy in arrive:
+        copy.start()
+    dp, row = lax.axis_index("dp"), lax.axis_index("row")
+    for n, gain in enumerate(gains):
+        gain[...] = sums[n : n + 1, span(row * 256, 256, 256)].reshape(gain.shape)
+    for n, bias in ((5, q_b), (6, u_b)):
+        size = bias.shape[0]
+        bias[...] = sums[n : n + 1, span(dp * size, size, 128)].reshape(bias.shape)
+    me = row * DPS + dp
+    pair = sums[4:5, span((me // 2) * 128, 128, 128)]
+    pair = jnp.where(lax.rem(me, 2) == 0, pair, pltpu.roll(pair, 64, 1))
+    for bias in (d_b, p_b):
+        bias[...] = pair[:, 0:64].reshape(bias.shape)
+    for first, then in zip(arrive, leave):
+        first.wait()
+        then.start()
+    for copy in leave:
+        copy.wait()
+
+
+def finish(whole, sums, n_qb, n_ub):
+    any_spec = pl.BlockSpec(memory_space=pl.ANY)
+    vmem = pl.BlockSpec(memory_space=pltpu.VMEM)
+    shape = jax.ShapeDtypeStruct
+    sizes = [n_qb, n_ub, 64, 64] + [256] * 4
+    out = pl.pallas_call(
+        finish_kernel,
+        out_shape=[shape(a.shape, a.dtype) for a in whole] + [shape((size,), F32) for size in sizes],
+        in_specs=[any_spec] * 6 + [vmem],
+        out_specs=[any_spec] * 6 + [vmem] * 8,
+        scratch_shapes=[pltpu.VMEM(a.shape, a.dtype) for a in whole] + [pltpu.SemaphoreType.DMA((2, 6))],
+    )(*whole, sums)
+    lo, gt, gq, gu, gd, gp, q_b, u_b, d_b, p_b, *gains = out
+    return (lo, gt, gq, q_b, gu, u_b, gd, d_b, gp, p_b, *gains)
+
+
 def angles_table():
     half_rot = ROT // 2
     rates = np.exp(np.arange(half_rot, dtype=np.float32) * np.float32(-2.0 * math.log(10000.0) / ROT))
@@ -1144,7 +1166,6 @@
            up_weight, up_bias, dense_weight, dense_bias, down_weight, down_bias, cotangent):
     tok_col = tokens_in.shape[0]
     n_q, n_u = qkv_weight.shape[1], up_weight.shape[1]
-    h_d, h_p = dense_weight.shape[0], down_weight.shape[0]
 
     n_qb, n_ub = qkv_bias.shape[0], up_bias.shape[0]
     aligned = n_qb % 128 == 0 and n_ub % 128 == 0
@@ -1163,14 +1184,19 @@
         prefix_len, smalls, jnp.asarray(angles_table()), q_bias, sum_u, own_x, own_cot, wq, wd, first, first_t, gu, gp, branch,
         comb, cols, aligned, tok_col
     )
+    h_d, h_p = dense_weight.shape[0], down_weight.shape[0]
+    whole = (
+        layer_out, grad_tokens, out_q.reshape(64, n_q), out_u.reshape(64, n_u), out_d.reshape(h_d, 256), out_p.reshape(h_p, 256)
+    )
+    if aligned:
+        return finish(whole, sums, n_qb, n_ub)
     dp, row = lax.axis_index("dp"), lax.axis_index("row")
     gain_sums = lax.dynamic_slice(sums, (0, row * 256), (4, 256))
     out_b = lax.dynamic_slice(sums, (4, (row * DPS + dp) * 64), (1, 64))[0]
     q_b = lax.dynamic_slice(sums, (5, dp * n_qb), (1, n_qb))[0]
     u_b = lax.dynamic_slice(sums, (6, dp * n_ub), (1, n_ub))[0]
     return (
-        layer_out, grad_tokens, out_q.reshape(64, n_q), q_b, out_u.reshape(64, n_u), u_b,
-        out_d.reshape(h_d, 256), out_b, out_p.reshape(h_p, 256), out_b,
+        whole[0], whole[1], whole[2], q_b, whole[3], u_b, whole[4], out_b, whole[5], out_b,
         gain_sums[0], gain_sums[1], gain_sums[2], gain_sums[3],
     )
 

time: 293 us -> 284 us (0.969)
  local copies, waits for them, and re-layouts: 14.6 us -> 1.46 us
  Pallas kernels: 277 us -> 281 us
    unnamed x17 -> x0, local copies, waits for them, and re-layouts: 8.1 us -> none
    pallas_call x0 -> x1, Pallas kernels: none -> 4.6 us  [finish(): pl.pallas_call(finish_kernel, out_shape=[shape(a.shape, a.dtype) for a in...]
where the time goes in v5:
time: 284 us
  Pallas kernels  281 us (99%)
    pallas_call x1, Pallas kernels, scatter(): pl.pallas_call(functools.partial(scatter_kernel, cols, aligned, pieces),...  139 us
    pallas_call x1, Pallas kernels, gather(): pl.pallas_call(functools.partial(gather_kernel, cols, aligned), out_shape...  137 us

profile of v5, /device:TPU:0, one launch (start us, length us, event | category | flops | bytes accessed | tf_op | source)
XLA Modules:
  0.0 283.6 jit_solution(17472485511793109882)
XLA Ops:
  1.3 1.5 concatenate.3
  2.8 136.9 %shard_map.263 = (bf16[1024,1024]{1,0:T(8,128)(2,1)}, bf16[1024,1024]{1,0:T(8,128)(2,1)}, f32[16,16,128]{2,1,0:T(8,128)}, bf16[1024,1536]{1,0:T(8,128)(2,1)}, bf...) custom-call(bf16[2048,256]{1,0:T(8,128)(2,1)} %refs_0_.2, ...), custom_call_target="tpu_custom_call" | custom-call | tf_op jit(solution)/shard_map/pallas_call | solution.py:604
  139.6 139.2 %shard_map.264 = (bf16[2048,256]{1,0:T(8,128)(2,1)}, bf16[2048,256]{1,0:T(8,128)(2,1)}, f32[2,32,1536]{2,1,0:T(8,128)}, f32[2,32,2048]{2,1,0:T(8,128)}, f32[2,64...) custom-call(s32[1]{0:T(128)S(6)} %copy.30.refs_0_, f32[16,16,128]{2,1,0:T(8,128)} %get-tuple-element.47.refs_1_, ...), custom_call_target="tpu_custom_call" | custom-call | tf_op jit(solution)/shard_map/pallas_call | solution.py:1103
  278.8 4.6 %shard_map.265 = (bf16[2048,256]{1,0:T(8,128)(2,1)}, bf16[2048,256]{1,0:T(8,128)(2,1)}, f32[64,1536]{1,0:T(8,128)}, f32[64,2048]{1,0:T(8,128)}, f32[128,256]{1,0...) custom-call(bf16[2048,256]{1,0:T(8,128)(2,1)} %get-tuple-element.59., ...), custom_call_target="tpu_custom_call" | custom-call | tf_op jit(solution)/shard_map/pallas_call | solution.py:1147

commit v6 on v5

--- a/solution.py
+++ b/solution.py
@@ -64,12 +64,12 @@
 N_W = 4
 QKV, UP, DENSE, DOWN = range(N_W)
 GATHER_PLAN = (
-    "b1", "z10", "b0", "b3", "b2", "z20", "s10", "z11", "s11", "z12", "z30", "m", "s12", "z13", "s30", "t0", "z31",
-    "p10", "p11", "s31", "s13", "s00", "p31", "z32", "t1", "p12", "p13", "s32", "z33", "s20", "d0", "z00", "p30",
-    "z21", "s33", "N0", "N1", "N2", "N3", "N4", "N5", "N6", "N7", "p32", "P0", "d1", "P1", "P2", "P3", "z01",
-    "p33", "D0", "s01", "D1", "s21", "D2", "z02", "p00", "D3", "s02", "z22", "z23", "B0", "B1", "z03", "B2", "B3",
-    "s23", "B4", "B5", "p23", "s22", "p20", "p21", "B6", "B7", "p22", "p02", "s03", "B8", "p01", "B9", "B10",
-    "B11", "p03",
+    "b1", "z10", "b3", "s10", "s30", "z30", "b2", "z11", "p10", "z12", "b0", "z31", "p30", "m", "s12", "z20",
+    "z13", "s00", "t0", "s13", "s31", "z32", "s11", "t1", "s20", "d0", "z21", "s32", "p13", "p12", "N0", "p11",
+    "s21", "N1", "N2", "p20", "N3", "N4", "z33", "z00", "s33", "N5", "N6", "p31", "N7", "P0", "P1", "P2", "p32",
+    "p33", "d1", "P3", "p00", "z01", "s01", "D0", "D1", "z22", "D2", "s22", "z23", "s23", "D3", "B0", "z02", "B1",
+    "s02", "B2", "z03", "p21", "s03", "B3", "B4", "B5", "B6", "B7", "p03", "p02", "p01", "B8", "B9", "B10", "B11",
+    "p23", "p22",
 )
 
 
@@ -612,13 +612,13 @@
 
 
 SCATTER_PLAN = (
-    "f0", "f1", "J0", "J1", "J2", "J3", "f2", "U", "H0", "H1", "H2", "H3", "H4", "H5", "g0", "f3", "H6", "H7",
-    "H8", "H9", "H10", "H11", "H12", "H13", "g1", "H14", "H15", "f4", "H16", "H17", "h0", "g2", "H18", "H19",
-    "H20", "H21", "h1", "g3", "g4", "q0", "H22", "H23", "H24", "H25", "h2", "h3", "H26", "H27", "H28", "H29", "f5",
-    "q1", "H30", "H31", "q2", "h4", "T", "q3", "r0", "q4", "r1", "g5", "f6", "u0", "X", "W0", "W1", "W2", "W3",
-    "g6", "r2", "f7", "u1", "f8", "h5", "G0", "G1", "G2", "G3", "g7", "h6", "Y", "g8", "f9", "u2", "r3", "h7",
-    "f10", "q5", "h8", "v0", "q6", "g9", "v1", "f11", "v2", "q7", "h9", "u3", "g10", "h10", "g11", "q8", "r4",
-    "r5", "q9", "r6", "u4", "v3", "u5", "r7", "r8", "q10", "h11", "q11", "u6", "u7", "u8", "r9", "u9", "r10", "v4",
+    "f0", "f1", "J0", "J1", "J2", "f2", "J3", "U", "H0", "H1", "H2", "H3", "H4", "H5", "g0", "H6", "H7", "H8",
+    "H9", "H10", "g1", "f3", "H11", "H12", "H13", "H14", "H15", "h0", "H16", "H17", "g2", "h1", "H18", "H19", "f4",
+    "H20", "g3", "H21", "q0", "H22", "H23", "H24", "h2", "H25", "H26", "H27", "g4", "H28", "f5", "q1", "r0", "H29",
+    "h3", "H30", "H31", "h4", "q2", "T", "f6", "q3", "W0", "q4", "X", "f7", "G0", "G1", "G2", "g5", "W1", "G3",
+    "f8", "h5", "g6", "g7", "r1", "h6", "f9", "W2", "u0", "q5", "u1", "g8", "r2", "h7", "Y", "W3", "h8", "g9",
+    "q6", "f10", "r3", "u2", "f11", "v0", "h9", "r4", "g10", "q7", "u3", "q8", "v1", "h10", "r5", "g11", "v2",
+    "h11", "q9", "r6", "u4", "q10", "u5", "r7", "r8", "v3", "r9", "q11", "v4", "r10", "u6", "u7", "u8", "u9",
     "u10", "r11", "u11",
 )
 PIECES = 12

time: 284 us -> 276 us (0.972)
  Pallas kernels: 281 us -> 273 us
    pallas_call x1, Pallas kernels: 137 us -> 131 us  [gather(): pl.pallas_call(functools.partial(gather_kernel, cols, aligned), out_shape...]
where the time goes in v6:
time: 276 us
  Pallas kernels  273 us (99%)
    pallas_call x1, Pallas kernels, scatter(): pl.pallas_call(functools.partial(scatter_kernel, cols, aligned, pieces),...  138 us
    pallas_call x1, Pallas kernels, gather(): pl.pallas_call(functools.partial(gather_kernel, cols, aligned), out_shape...  131 us

profile of v6, /device:TPU:0, one launch (start us, length us, event | category | flops | bytes accessed | tf_op | source)
XLA Modules:
  0.0 276.0 jit_solution(16942446472475064443)
XLA Ops:
  1.3 1.5 concatenate.3
  2.8 130.8 %shard_map.263 = (bf16[1024,1024]{1,0:T(8,128)(2,1)}, bf16[1024,1024]{1,0:T(8,128)(2,1)}, f32[16,16,128]{2,1,0:T(8,128)}, bf16[1024,1536]{1,0:T(8,128)(2,1)}, bf...) custom-call(bf16[2048,256]{1,0:T(8,128)(2,1)} %refs_0_.2, ...), custom_call_target="tpu_custom_call" | custom-call | tf_op jit(solution)/shard_map/pallas_call | solution.py:604
  133.6 137.7 %shard_map.264 = (bf16[2048,256]{1,0:T(8,128)(2,1)}, bf16[2048,256]{1,0:T(8,128)(2,1)}, f32[2,32,1536]{2,1,0:T(8,128)}, f32[2,32,2048]{2,1,0:T(8,128)}, f32[2,64...) custom-call(s32[1]{0:T(128)S(6)} %copy.30.refs_0_, f32[16,16,128]{2,1,0:T(8,128)} %get-tuple-element.47.refs_1_, ...), custom_call_target="tpu_custom_call" | custom-call | tf_op jit(solution)/shard_map/pallas_call | solution.py:1103
  271.2 4.6 %shard_map.265 = (bf16[2048,256]{1,0:T(8,128)(2,1)}, bf16[2048,256]{1,0:T(8,128)(2,1)}, f32[64,1536]{1,0:T(8,128)}, f32[64,2048]{1,0:T(8,128)}, f32[128,256]{1,0...) custom-call(bf16[2048,256]{1,0:T(8,128)(2,1)} %get-tuple-element.59., ...), custom_call_target="tpu_custom_call" | custom-call | tf_op jit(solution)/shard_map/pallas_call | solution.py:1147

commit v7 on v6

--- a/solution.py
+++ b/solution.py
@@ -64,12 +64,12 @@
 N_W = 4
 QKV, UP, DENSE, DOWN = range(N_W)
 GATHER_PLAN = (
-    "b1", "z10", "b3", "s10", "s30", "z30", "b2", "z11", "p10", "z12", "b0", "z31", "p30", "m", "s12", "z20",
-    "z13", "s00", "t0", "s13", "s31", "z32", "s11", "t1", "s20", "d0", "z21", "s32", "p13", "p12", "N0", "p11",
-    "s21", "N1", "N2", "p20", "N3", "N4", "z33", "z00", "s33", "N5", "N6", "p31", "N7", "P0", "P1", "P2", "p32",
-    "p33", "d1", "P3", "p00", "z01", "s01", "D0", "D1", "z22", "D2", "s22", "z23", "s23", "D3", "B0", "z02", "B1",
-    "s02", "B2", "z03", "p21", "s03", "B3", "B4", "B5", "B6", "B7", "p03", "p02", "p01", "B8", "B9", "B10", "B11",
-    "p23", "p22",
+    "b1", "z10", "b3", "s30", "b2", "z30", "s10", "z11", "z12", "s11", "m", "z31", "z20", "s12", "p11", "z13",
+    "p30", "s13", "t0", "s20", "z32", "p10", "b0", "p13", "t1", "s32", "d0", "s31", "N0", "p12", "N1", "N2", "N3",
+    "N4", "s00", "z33", "s33", "N5", "N6", "z00", "N7", "p32", "P0", "P1", "z21", "p31", "P2", "P3", "d1", "p33",
+    "s21", "z01", "s01", "D0", "D1", "D2", "D3", "z22", "s22", "z02", "B0", "B1", "s02", "p21", "B2", "B3", "B4",
+    "z23", "p02", "z03", "B5", "p00", "p20", "s03", "B6", "B7", "s23", "p22", "B8", "p03", "B9", "B10", "B11",
+    "p23", "p01",
 )
 
 
@@ -213,7 +213,17 @@
             up_t[h, :, toks] = grad[HD * h : HD * (h + 1)]
 
 
-def attend_head(h, prefix, angles, q_t, k_t, v_t, up_t, att_t, gm_t, grad_q, grad_k, grad_v, served):
+def hide_stage(prefix, hidden_keys):
+    for i in range(SEQ_LEN // 256):
+        low = 256 * i
+        seen = max(512, low + 256)
+        place, size = (0, 512) if i == 0 else (256 * (i + 1), 256)
+        keys = lax.broadcasted_iota(jnp.int32, (size, 256), 0) + seen - size
+        queries = lax.broadcasted_iota(jnp.int32, (size, 256), 1) + low
+        hidden_keys[place : place + size, :] = jnp.where((keys <= queries) | (keys < prefix), 0.0, NEGATIVE)
+
+
+def attend_head(h, hidden_keys, angles, q_t, k_t, v_t, up_t, att_t, gm_t, grad_q, grad_k, grad_v, served):
     keys_plain, values_plain = k_t[h].T, v_t[h].T
     done = 0
     for i in range(SEQ_LEN // 256):
@@ -222,11 +232,9 @@
         spot = pl.ds(low, 256)
         q, up = q_t[h, :, spot], up_t[h, :, spot]
         scores = nn(keys_plain[0:seen], q)
-        plain = min(low, seen)
-        keys = lax.broadcasted_iota(jnp.int32, (seen - plain, 256), 0) + plain
-        queries = lax.broadcasted_iota(jnp.int32, (seen - plain, 256), 1) + low
-        masked = jnp.where((keys <= queries) | (keys < prefix), scores[plain:], NEGATIVE)
-        scores = jnp.concatenate([scores[:plain], masked], axis=0) if plain else masked
+        place, size = (0, 512) if i == 0 else (256 * (i + 1), 256)
+        masked = scores[seen - size :] + hidden_keys[place : place + size, :]
+        scores = jnp.concatenate([scores[: seen - size], masked], axis=0) if seen > size else masked
         exponent = jnp.exp(scores - jnp.max(scores, axis=0, keepdims=True))
         probs = exponent * (1.0 / jnp.sum(exponent, axis=0, keepdims=True))
         weights = probs.astype(BF)
@@ -665,9 +673,9 @@
      comb_in) = refs[:15]
     (lo_out, gt_out, oq, ou, od, op, sm_out) = refs[15:22]
     (wq, wd, x_ref, c_ref, first, first_t, q_t, k_t, v_t, up_t, att_t, gm_t, grad_q, grad_k, grad_v) = refs[22:37]
-    (gq, gd, att, branch, comb, branch_got, comb_got, gains, bias_row, out_bias, sm, sm_got, gain_sum) = refs[37:50]
-    mine_u, mine_p = refs[50:52], refs[52:54]
-    base = 54
+    (gq, gd, att, branch, comb, branch_got, comb_got, gains, bias_row, out_bias, sm, sm_got, gain_sum, hidden_keys) = refs[37:51]
+    mine_u, mine_p = refs[51:53], refs[53:55]
+    base = 55
 
     def buffers(start):
         return [refs[start + 2 * i : start + 2 * i + 2] for i in range(n_p)]
@@ -682,6 +690,7 @@
     middle, end = side == 1, side == 0
     n_q, n_u = wq_in.shape[1], sum_u.shape[1]
     heads = q_t.shape[0]
+    folded = small_room(n_q, n_u)[0]
     tok_col = lo_out.shape[0]
     part = SEQ_LEN // cols
 
@@ -909,10 +918,10 @@
                 sm[n] = value
             else:
                 sm_out[...] = value
-                value = value[0:4]
+                value = value[0:4, 0:D]
                 for m in waits:
-                    value = value + sm_got[m, 0:4, :]
-                sm_out[0:4, :] = value
+                    value = value + sm_got[m, 0:4, 0:D]
+                sm_out[0:4, 0:D] = value
         for m in ((0,), (1,), (2, 3, 4), tuple(range(5, 4 + cols)), ())[n]:
             small_copy(m).start()
 
@@ -929,7 +938,7 @@
         else:
             bias_row[...] = bias_in[...]
         sm[0] = jnp.zeros(sm.shape[1:], F32)
-        sm[0, 6:7, 0:n_u] = sum_u[...]
+        put_up(sm.at[0], sum_u[...], folded)
         loads[0].wait()
         loads[1].wait()
         project_stage(wq, first, bias_row, angles, q_t, k_t, v_t, heads, served)
@@ -1001,7 +1010,7 @@
             for n, value in enumerate((normed * grad_first, grad_first, normed * grad_second, grad_second,
                                        c_ref[rows, :].astype(F32))):
                 gain_sum[n : n + 1, :] += jnp.sum(value, axis=0, keepdims=True)
-            sm[0, 5:6, 0:n_q] += jnp.sum(grad.astype(F32), axis=0, keepdims=True)
+            add_qkv(sm.at[0], jnp.sum(grad.astype(F32), axis=0, keepdims=True), folded)
             comb[rows, :] = gains[0:1, :] * grad_first + gains[2:3, :] * grad_second
             served(j)
             return carry
@@ -1030,10 +1039,10 @@
             stages[kind](int(rest))
 
     def attention(served):
-        prefix = prefix_ref[0]
+        hide_stage(prefix_ref[0], hidden_keys)
 
         def head_body(h, carry):
-            attend_head(h, prefix, angles, q_t, k_t, v_t, up_t, att_t, gm_t, grad_q, grad_k, grad_v, served)
+            attend_head(h, hidden_keys, angles, q_t, k_t, v_t, up_t, att_t, gm_t, grad_q, grad_k, grad_v, served)
             return carry
 
         lax.fori_loop(0, heads, head_body, 0)
@@ -1073,7 +1082,7 @@
     pieces = pieces_of(n_q, n_u, h_d, h_p)
     n_p = len(pieces)
     part = SEQ_LEN // cols
-    line = max(n_q, n_u, D)
+    line = small_room(n_q, n_u)[1]
     square = (SEQ_LEN, D)
     turned = buf((heads, HD, SEQ_LEN), BF)
     scratch = [
@@ -1083,7 +1092,7 @@
         buf((ROWS, 2, 2, 2, 32, n_q), BF), buf((2, 2, 2, h_d // 2, D), BF), buf((SEQ_LEN, heads * HD), BF), buf(square, F32), buf(square, F32),
         buf((cols - 1, part, D), F32), buf((cols - 1, part, D), F32),
         buf((8, D), F32), buf((1, n_q), F32), buf((1, D), F32), buf((4, 8, line), F32), buf((4 + cols, 8, line), F32),
-        buf((8, D), F32),
+        buf((8, D), F32), buf((1280, 256), F32),
     ]
     scratch += [buf((ROWS, 2, 32, n_u), BF)] * 2 + [buf((2, h_p // 2, D), BF)] * 2
     for lead, count in (((ROWS, 2), None), ((ROWS,), None), ((3,), 3), ((2,), 2)):
@@ -1113,10 +1122,33 @@
     )(prefix_len, smalls, angles, bias, sum_u, own_x, own_cot, wq, wd, first, first_t, gu, gp, branch, comb)
 
 
+def small_room(n_q, n_u):
+    folded = n_q == D + 512 and n_u == 2 * D
+    return folded, (D + 128 if folded else max(n_q, n_u, D))
+
+
+def put_up(rows, value, folded):
+    if not folded:
+        rows[6:7, 0 : value.shape[1]] = value
+        return
+    rows[6:7, 0:D] = value[:, 0:D]
+    rows[7:8, 0:D] = value[:, D:]
+
+
+def add_qkv(rows, value, folded):
+    if not folded:
+        rows[5:6, 0 : value.shape[1]] += value
+        return
+    rows[5:6, 0:D] += value[:, 0:D]
+    for n in range(4):
+        rows[n : n + 1, D : D + 128] += value[:, D + 128 * n : D + 128 * (n + 1)]
+
+
 def finish_kernel(*refs):
     whole_in, sums, whole_out, q_b, u_b, d_b, p_b, gains, rooms, sem = (
         refs[:6], refs[6], refs[7:13], *refs[13:17], refs[17:21], refs[21:27], refs[27]
     )
+    q_row, u_row = refs[28], refs[29]
     arrive = [pltpu.make_async_copy(src, dst, sem.at[0, n]) for n, (src, dst) in enumerate(zip(whole_in, rooms))]
     leave = [pltpu.make_async_copy(src, dst, sem.at[1, n]) for n, (src, dst) in enumerate(zip(rooms, whole_out))]
     for copy in arrive:
@@ -1124,9 +1156,18 @@
     dp, row = lax.axis_index("dp"), lax.axis_index("row")
     for n, gain in enumerate(gains):
         gain[...] = sums[n : n + 1, span(row * 256, 256, 256)].reshape(gain.shape)
-    for n, bias in ((5, q_b), (6, u_b)):
+    if sums.shape[1] == D + 128:
+        q_row[:, 0:D] = sums[5:6, 0:D]
+        for n in range(4):
+            q_row[:, D + 128 * n : D + 128 * (n + 1)] = sums[n : n + 1, D : D + 128]
+        u_row[:, 0:D] = sums[6:7, 0:D]
+        u_row[:, D:] = sums[7:8, 0:D]
+    else:
+        q_row[...] = sums[5:6, 0 : q_row.shape[1]]
+        u_row[...] = sums[6:7, 0 : u_row.shape[1]]
+    for row_of, bias in ((q_row, q_b), (u_row, u_b)):
         size = bias.shape[0]
-        bias[...] = sums[n : n + 1, span(dp * size, size, 128)].reshape(bias.shape)
+        bias[...] = row_of[0:1, span(dp * size, size, 128)].reshape(bias.shape)
     me = row * DPS + dp
     pair = sums[4:5, span((me // 2) * 128, 128, 128)]
     pair = jnp.where(lax.rem(me, 2) == 0, pair, pltpu.roll(pair, 64, 1))
@@ -1149,7 +1190,9 @@
         out_shape=[shape(a.shape, a.dtype) for a in whole] + [shape((size,), F32) for size in sizes],
         in_specs=[any_spec] * 6 + [vmem],
         out_specs=[any_spec] * 6 + [vmem] * 8,
-        scratch_shapes=[pltpu.VMEM(a.shape, a.dtype) for a in whole] + [pltpu.SemaphoreType.DMA((2, 6))],
+        scratch_shapes=[pltpu.VMEM(a.shape, a.dtype) for a in whole] + [
+            pltpu.SemaphoreType.DMA((2, 6)), pltpu.VMEM((1, n_qb * DPS), F32), pltpu.VMEM((1, n_ub * DPS), F32),
+        ],
     )(*whole, sums)
     lo, gt, gq, gu, gd, gp, q_b, u_b, d_b, p_b, *gains = out
     return (lo, gt, gq, q_b, gu, u_b, gd, d_b, gp, p_b, *gains)

time: 276 us -> 274 us (level)
    pallas_call x1, Pallas kernels: 138 us -> 134 us  [scatter(): pl.pallas_call(functools.partial(scatter_kernel, cols, aligned, pieces),...]
where the time goes in v7:
time: 274 us
  Pallas kernels  271 us (99%)
    pallas_call x1, Pallas kernels, scatter(): pl.pallas_call(functools.partial(scatter_kernel, cols, aligned, pieces),...  134 us
    pallas_call x1, Pallas kernels, gather(): pl.pallas_call(functools.partial(gather_kernel, cols, aligned), out_shape...  132 us

profile of v7, /device:TPU:0, one launch (start us, length us, event | category | flops | bytes accessed | tf_op | source)
XLA Modules:
  0.0 273.5 jit_solution(472022528008767790)
XLA Ops:
  1.3 1.5 concatenate.3
  2.8 131.8 %shard_map.263 = (bf16[1024,1024]{1,0:T(8,128)(2,1)}, bf16[1024,1024]{1,0:T(8,128)(2,1)}, f32[16,16,128]{2,1,0:T(8,128)}, bf16[1024,1536]{1,0:T(8,128)(2,1)}, bf...) custom-call(bf16[2048,256]{1,0:T(8,128)(2,1)} %refs_0_.2, ...), custom_call_target="tpu_custom_call" | custom-call | tf_op jit(solution)/shard_map/pallas_call | solution.py:612
  134.5 134.3 %shard_map.264 = (bf16[2048,256]{1,0:T(8,128)(2,1)}, bf16[2048,256]{1,0:T(8,128)(2,1)}, f32[2,32,1536]{2,1,0:T(8,128)}, f32[2,32,2048]{2,1,0:T(8,128)}, f32[2,64...) custom-call(s32[1]{0:T(128)S(6)} %copy.30.refs_0_, f32[16,16,128]{2,1,0:T(8,128)} %get-tuple-element.47.refs_1_, ...), custom_call_target="tpu_custom_call" | custom-call | tf_op jit(solution)/shard_map/pallas_call | solution.py:1112
  268.8 4.5 %shard_map.265 = (bf16[2048,256]{1,0:T(8,128)(2,1)}, bf16[2048,256]{1,0:T(8,128)(2,1)}, f32[64,1536]{1,0:T(8,128)}, f32[64,2048]{1,0:T(8,128)}, f32[128,256]{1,0...) custom-call(bf16[2048,256]{1,0:T(8,128)(2,1)} %get-tuple-element.59., ...), custom_call_target="tpu_custom_call" | custom-call | tf_op jit(solution)/shard_map/pallas_call | solution.py:1188

commit v8 on v7

--- a/solution.py
+++ b/solution.py
@@ -648,7 +648,7 @@
         dst[where] = (dst[where].astype(F32) + src[where].astype(F32)).astype(BF)
         return carry
 
-    lax.fori_loop(0, total, body, 0)
+    lax.fori_loop(0, total, body, 0, unroll=min(4, total))
 
 
 def pieces_of(n_q, n_u, h_d, h_p):

time: 274 us -> 273 us (level)
  no operation moved by 1% of the time
where the time goes in v8:
time: 273 us
  Pallas kernels  270 us (99%)
    pallas_call x1, Pallas kernels, scatter(): pl.pallas_call(functools.partial(scatter_kernel, cols, aligned, pieces),...  133 us
    pallas_call x1, Pallas kernels, gather(): pl.pallas_call(functools.partial(gather_kernel, cols, aligned), out_shape...  132 us

profile of v8, /device:TPU:0, one launch (start us, length us, event | category | flops | bytes accessed | tf_op | source)
XLA Modules:
  0.0 272.6 jit_solution(16500562156538879695)
XLA Ops:
  1.3 1.5 concatenate.3
  2.8 131.8 %shard_map.263 = (bf16[1024,1024]{1,0:T(8,128)(2,1)}, bf16[1024,1024]{1,0:T(8,128)(2,1)}, f32[16,16,128]{2,1,0:T(8,128)}, bf16[1024,1536]{1,0:T(8,128)(2,1)}, bf...) custom-call(bf16[2048,256]{1,0:T(8,128)(2,1)} %refs_0_.2, ...), custom_call_target="tpu_custom_call" | custom-call | tf_op jit(solution)/shard_map/pallas_call | solution.py:612
  134.5 133.4 %shard_map.264 = (bf16[2048,256]{1,0:T(8,128)(2,1)}, bf16[2048,256]{1,0:T(8,128)(2,1)}, f32[2,32,1536]{2,1,0:T(8,128)}, f32[2,32,2048]{2,1,0:T(8,128)}, f32[2,64...) custom-call(s32[1]{0:T(128)S(6)} %copy.30.refs_0_, f32[16,16,128]{2,1,0:T(8,128)} %get-tuple-element.47.refs_1_, ...), custom_call_target="tpu_custom_call" | custom-call | tf_op jit(solution)/shard_map/pallas_call | solution.py:1112
  267.9 4.5 %shard_map.265 = (bf16[2048,256]{1,0:T(8,128)(2,1)}, bf16[2048,256]{1,0:T(8,128)(2,1)}, f32[64,1536]{1,0:T(8,128)}, f32[64,2048]{1,0:T(8,128)}, f32[128,256]{1,0...) custom-call(bf16[2048,256]{1,0:T(8,128)(2,1)} %get-tuple-element.59., ...), custom_call_target="tpu_custom_call" | custom-call | tf_op jit(solution)/shard_map/pallas_call | solution.py:1188
